TPU v7x, 32 devices: a whole 2x2x4 slice. The times are simulated.
32 devices in a mesh: slab: 16 (over z, x, core), view: 2 (over y).
Axes of the slice: x: 2, y: 2, z: 4, core: 2. Of those that a mesh axis runs over, the one named last changes fastest.
Arguments:
- activity: float32 [512, 32, 1024], P('slab'), may hold values from 0.5 to 2
- sensitivity: float32 [512, 32, 1024], P('slab'), may hold values from 1 to 8
- psf_width: float32 [512], P('slab'), may hold values from 0.05 to 0.3
- measured: bfloat16 [2, 1024, 32, 128], P('view', 'slab'), may hold values from 0.25 to 4
- block_slab: int32 [2, 1024, 1], P('view', 'slab'), may hold values from 0 to 15; in each aligned block of 64 rows (0 to 63, 64 to 127, ..., all dimensions but the last counted through in order) at most 8 rows name the same one
- block_line: int32 [2, 1024], P('view', 'slab'), may hold values from 0 to 31
- block_angle: int32 [2, 1024], P('view', 'slab'), may hold values from 0 to 7
- subset_views: int32 [2, 8], P('view'), may hold values from 0 to 335
Outputs:
- updated: float32 [512, 32, 1024], P('slab')
Inputs may be any that keep to these rules, and one draw needn't show every extreme that they name: `block_slab`: among the 64 blocks of one device (aligned blocks of 64 rows) no slab is named more than 8 times, a bound that some block reaches.
All inputs are finite; a program needn't handle non-finite values.
Results may differ from a plain program's by a relative error of at most 0.0014.
Values may be sent and summed in bfloat16 or wider, within the bound.
No kernel may reach another device: no remote copies, remote signals or barrier semaphores. Data moves between devices by JAX's collectives and lax.ppermute only.
A program may use at most 64 MiB of HBM per device.

v0:
```python
import math

import jax
import jax.numpy as jnp
from jax import lax
from jax.sharding import PartitionSpec as P

VIEWS_ALL = 336


BACKGROUND = 0.05


def with_halo(value, sides, width):
    for axis, dim in sides:
        size, length = (lax.axis_size(axis), value.shape[dim])
        up = [(i, (i + 1) % size) for i in range(size - 1)]
        down = [(j, i) for i, j in up]
        last = lax.slice_in_dim(value, length - width, length, axis=dim)
        leading = lax.slice_in_dim(value, 0, width, axis=dim)
        before = lax.ppermute(last, axis, up)
        after = lax.ppermute(leading, axis, down)
        value = jnp.concatenate([before, value, after], axis=dim)
    return value


def kernels(angles, bins, length):
    view_angle = math.pi * angles.astype(jnp.float32) / VIEWS_ALL
    step_width = length / bins
    deviation = 0.25 * step_width
    spacing = step_width * (0.75 + 0.25 * jnp.cos(2.0 * view_angle))
    offset = 1.5 * step_width * jnp.sin(view_angle)
    centres = (jnp.arange(bins, dtype=jnp.float32) + 0.5 - bins / 2)[None, :] * spacing[
        :, None
    ] + offset[:, None]
    voxel_pos = jnp.arange(length, dtype=jnp.float32) + 0.5 - length / 2
    distance = voxel_pos[None, None, :] - centres[:, :, None]
    values = jnp.exp(-distance * distance / (2.0 * deviation * deviation)) / (
        deviation * math.sqrt(2.0 * math.pi)
    )
    return values.astype(jnp.bfloat16)


def on_device(
    activity, sensitivity, psf_width, measured, block_slab, block_line, block_angle, subset_views
):
    weight = psf_width[:, None, None]
    padded = with_halo(activity, (("slab", 0),), 1)
    blurred = ((1.0 - 2.0 * weight) * activity + weight * (padded[:-2] + padded[2:])).astype(
        jnp.bfloat16
    )
    planes, lines_here, length = activity.shape
    bins = measured.shape[3]
    tof_kernel = kernels(subset_views[0], bins, length)
    angle_count = tof_kernel.shape[0]
    projected = jnp.einsum("zlv,atv->alzt", blurred, tof_kernel, preferred_element_type=jnp.float32)
    projected = projected.reshape(angle_count * lines_here, planes, bins)
    slab_count = lax.axis_size("slab")
    block_total = measured.shape[1]
    capacity = 2 * block_total // slab_count
    targets = block_slab[0, :, 0]
    onehot = (targets[:, None] == jnp.arange(slab_count, dtype=jnp.int32)[None, :]).astype(
        jnp.int32
    )
    slot_pos = jnp.sum((jnp.cumsum(onehot, axis=0) - onehot) * onehot, axis=1)
    send_rows = (
        jnp.zeros((slab_count, capacity, planes, bins), jnp.bfloat16)
        .at[targets, slot_pos]
        .set(measured[0])
    )
    send_index = (
        jnp.zeros((slab_count, capacity), jnp.int32)
        .at[targets, slot_pos]
        .set(block_angle[0] * lines_here + block_line[0])
    )
    rows = lax.all_to_all(send_rows, "slab", split_axis=0, concat_axis=0, tiled=True)
    index = lax.all_to_all(send_index, "slab", split_axis=0, concat_axis=0, tiled=True)
    estimate = projected[index]
    ratios, index = (rows.astype(jnp.float32) / (estimate + BACKGROUND), index)
    sums = jnp.zeros((angle_count * lines_here, planes, bins), jnp.float32)
    sums = sums.at[index.reshape(-1)].add(ratios.reshape(-1, planes, bins))
    rounded = sums.astype(jnp.bfloat16).reshape(angle_count, lines_here, planes, bins)
    back = jnp.einsum("alzt,atv->zlv", rounded, tof_kernel, preferred_element_type=jnp.float32)
    total = lax.psum(back, "view")
    edges = with_halo(weight * total, (("slab", 0),), 1)
    smoothed = (1.0 - 2.0 * weight) * total + edges[:-2] + edges[2:]
    return activity * smoothed / sensitivity


def solution(mesh):
    in_specs = (
        P("slab", None, None),
        P("slab", None, None),
        P("slab"),
        P("view", "slab", None, None),
        P("view", "slab", None),
        P("view", "slab"),
        P("view", "slab"),
        P("view", None),
    )
    out_specs = P("slab", None, None)
    return jax.shard_map(
        on_device, mesh=mesh, in_specs=in_specs, out_specs=out_specs, check_vma=False
    )
```

profile of v0, /device:TPU:0, one launch (start us, length us, event | category | flops | bytes accessed | tf_op | source)
XLA Modules:
  0.0 243.0 jit_solution(12498067578959987370)
XLA Ops:
  6.5 0.7 fusion.23
  7.3 0.1 reduce_window_sum.11
  7.4 0.8 select_reduce_fusion
  8.2 0.7 fusion.26
  8.9 0.7 add_bitcast_fusion
  9.5 3.5 %scatter_fusion = s32[16,8]{0,1:T(8,128)S(1)} fusion(s32[16,8]{0,1:T(8,128)S(1)} %broadcast.188, s32[64]{0:T(128)S(1)} %fusion.26, s32[64]{0:T(128)S(1)} %add_bitcast_fusion), kind=kCustom, calls=%fused_computation.1 | custom fusion | bytes 1280 | tf_op jit(solution)/shard_map/scatter | solution.py:74
  13.0 0.7 copy.33
  13.7 7.4 %all-to-all-start = ((s32[16,1,8]{2,1,0:T(1,128)}), s32[16,1,8]{2,1,0:T(1,128)S(1)}, u32[]{:S(2)}, u32[]{:S(2)}) async-start(s32[16,1,8]{2,1,0:T(1,128)} %copy.33), calls=%async_computation | async-start | bytes 16384 | tf_op jit(solution)/shard_map/all_to_all | solution.py:77
  21.1 1.0 fusion.32
  22.1 0.1 copy.37
  22.2 1.3 collective-permute-start.1
  23.5 0.1 copy.35
  23.7 3.0 %collective-permute-start = (f32[1,32,1024]{2,0,1:T(1,128)S(1)}, f32[1,32,1024]{2,0,1:T(1,128)S(1)}, u32[]{:S(2)}, u32[]{:S(2)}) collective-permute-start(f32[1,32,1024]{2,0,1:T(1,128)S(1)} %copy.35), channel_id=1, source_target_pairs={{0,2},{2,4},{4,6},{6,8},{8,10},{10,12},{12,14},{14,16},{16,18},{18... | collective-permute-start | bytes 393224 | tf_op jit(solution)/shard_map/ppermute | solution.py:21
  26.7 0.7 multiply_bitcast_fusion
  27.4 0.1 multiply_add_fusion
  27.5 0.7 multiply_subtract_fusion
  28.2 1.2 broadcast_in_dim.5
  29.4 8.0 %scatter_fusion.1 = bf16[16,8,32,128]{3,2,1,0:T(8,128)(2,1)} fusion(bf16[16,8,32,128]{3,2,1,0:T(8,128)(2,1)} %broadcast_in_dim.5, s32[64]{0:T(128)S(1)} %fusion.26, bf16[64,32,128]{2,1,0:T(8,128)(2,1)} %bitcast.57), kind=kCustom, calls=%fused_computation.2 | custom fusion | bytes 1573376 | tf_op jit(solution)/shard_map/scatter | solution.py:69
  37.4 0.0 all-to-all-done
  37.4 7.0 %all-to-all-start.1 = ((bf16[16,8,32,128]{3,2,1,0:T(8,128)(2,1)}), bf16[16,8,32,128]{3,2,1,0:T(8,128)(2,1)S(1)}, u32[]{:S(2)}, u32[]{:S(2)}) async-start(bf16[16,8,32,128]{3,2,1,0:T(8,128)(2,1)} %scatter_fusion.1), calls=%async_computation.1 | async-start | bytes 2097152 | tf_op jit(solution)/shard_map/all_to_all | solution.py:76
  44.4 0.0 all-reduce.2.cloned.1.call-start
  44.4 0.0 copy-start.2
  44.4 6.6 %copy.44 = f32[32,32,1024]{2,0,1:T(8,128)} copy(f32[32,32,1024]{2,1,0:T(8,128)} %param.8) | data formatting | bytes 8388608 | tf_op args[0]
  51.1 0.6 broadcast.255
  51.7 0.7 reduce.3
  52.4 0.1 reshape.197
  52.5 0.1 copy.41
  52.5 0.1 copy.42
  52.6 0.1 reshape.207
  52.7 0.0 collective-permute-done.1
  52.7 0.0 collective-permute-done
  52.8 0.0 copy-done.2
  52.8 6.8 %fusion.11 = bf16[32,32,1024]{2,0,1:T(8,128)(2,1)S(1)} fusion(f32[1,32,1024]{2,0,1:T(1,128)S(1)} %collective-permute-done.1, f32[32,32,1024]{2,0,1:T(8,128)} %copy.44, f32[1,32,1024]{2,0,1:T(1,128)S(1)} %collective-permute-done, f32[32]{0:T(128)S(1)} %copy-done.2, f32[32]{0:T(128)S(1)} %multiply_subtract_fusion), kind=kLoop, calls=%fused_computation.19 | loop fusion | flops 7340032 | bytes 6553856 | tf_op jit(solution)/shard_map/convert_element_type | solution.py:49
  59.6 3.3 %convolution_bitcast_fusion.1 = f32[8,32,32,128]{3,1,2,0:T(8,128)S(1)} fusion(bf16[32,32,1024]{2,0,1:T(8,128)(2,1)S(1)} %fusion.11, f32[8,128]{1,0:T(8,128)S(1)} %multiply_add_fusion, f32[1024]{0:T(1024)S(1)} %iota_add_fusion), kind=kOutput, calls=%fused_computation.22 | convolution fusion | flops 2153775104 | bytes 6299648 | tf_op jit(solution)/shard_map/zlv,atv->alzt/dot_general | solution.py:56
  62.9 4.4 %copy.40 = f32[8,32,32,128]{3,2,1,0:T(8,128)} copy(f32[8,32,32,128]{3,1,2,0:T(8,128)S(1)} %convolution_bitcast_fusion.1) | data formatting | bytes 8388608 | tf_op jit(solution)/shard_map/zlv,atv->alzt/transpose | solution.py:56
  67.3 2.9 %gather_fusion = f32[128,32,128]{2,1,0:T(8,128)S(1)} fusion(f32[256,32,128]{2,1,0:T(8,128)} %bitcast.53, s32[1024]{0:T(1024)S(1)} %pad_clamp_fusion), kind=kCustom, calls=%fused_computation | custom fusion | bytes 4194816 | tf_op jit(solution)/shard_map/gather | solution.py:78
  70.1 1.6 broadcast_add_fusion
  71.7 0.0 all-to-all-done.1
  71.7 2.0 convert_divide_fusion
  73.7 2.5 %broadcast_in_dim.4 = f32[256,32,128]{2,1,0:T(8,128)} broadcast(f32[]{:T(128)} %constant.17.clone.1), dimensions={} | broadcast | bytes 4194308 | tf_op jit(solution)/shard_map/broadcast_in_dim | solution.py:80
  76.3 18.7 %scatter_fusion.2 = f32[256,32,128]{2,1,0:T(8,128)} fusion(f32[256,32,128]{2,1,0:T(8,128)} %broadcast_in_dim.4, s32[128]{0:T(128)S(1)} %fusion.25, f32[128,32,128]{2,1,0:T(8,128)S(1)} %bitcast.54), kind=kCustom, calls=%fused_computation.3 | custom fusion | flops 524288 | bytes 6291968 | tf_op jit(solution)/shard_map/scatter-add | solution.py:81
  94.9 2.7 %convert_element_type.31 = bf16[256,32,128]{2,1,0:T(8,128)(2,1)S(1)} convert(f32[256,32,128]{2,1,0:T(8,128)} %scatter_fusion.2) | non-fusion elementwise | flops 1048576 | bytes 6291456 | tf_op jit(solution)/shard_map/convert_element_type | solution.py:82
  97.6 4.6 %convolution_bitcast_fusion = f32[32,32,1024]{2,0,1:T(8,128)} fusion(bf16[8,32,32,128]{3,2,1,0:T(8,128)(2,1)S(1)} %bitcast.56, f32[8,128]{1,0:T(8,128)S(1)} %multiply_add_fusion, f32[1024]{0:T(1024)S(1)} %iota_add_fusion), kind=kOutput, calls=%fused_computation.21 | convolution fusion | flops 2153775104 | bytes 6299648 | tf_op jit(solution)/shard_map/alzt,atv->zlv/dot_general | solution.py:83
  102.2 0.0 all-reduce.2.cloned.1.call-update
  102.2 110.4 %all-reduce.2.cloned.1.call-done = f32[32,32,1024]{2,0,1:T(8,128)} async-done(((f32[32,32,1024]{2,0,1:T(8,128)}), f32[32,32,1024]{2,0,1:T(8,128)}) %all-reduce.2.cloned.1.call-update) | async-done | bytes 4194320 | tf_op jit(solution)/shard_map/psum | solution.py:84
  212.7 0.0 copy-start
  212.7 0.0 copy-start.1
  212.7 3.1 %broadcast_multiply_fusion = f32[32,32,1024]{2,0,1:T(8,128)S(1)} fusion(f32[32,32,1024]{2,0,1:T(8,128)} %all-reduce.2.cloned.1.call-done, f32[32]{0:T(128)S(1)} %copy-done.2), kind=kLoop, calls=%fused_computation.26 | loop fusion | flops 1048576 | bytes 8388736 | tf_op jit(solution)/shard_map/mul | solution.py:85
  215.7 0.2 fusion.31
  216.0 1.9 collective-permute-start.2
  217.9 1.3 collective-permute-start.3
  219.2 0.0 collective-permute-done.2
  219.2 3.2 %collective-permute-done.3 = f32[1,32,1024]{2,0,1:T(1,128)S(1)} collective-permute-done((f32[1,32,1024]{2,0,1:T(1,128)S(1)}, f32[1,32,1024]{2,0,1:T(1,128)S(1)}, u32[]{:S(2)}, u32[]{:S(2)}) %collective-permute-start.3) | collective-permute-done | bytes 131104 | tf_op jit(solution)/shard_map/ppermute | solution.py:22
  222.3 0.0 copy-done
  222.4 0.0 copy-done.1
  222.4 9.4 %fusion.6 = f32[32,32,1024]{2,0,1:T(8,128)S(1)} fusion(f32[1,32,1024]{2,0,1:T(1,128)S(1)} %collective-permute-done.3, f32[32,32,1024]{2,0,1:T(8,128)S(1)} %broadcast_multiply_fusion, f32[1,32,1024]{2,0,1:T(1,128)S(1)} %collective-permute-done.2, f32[32,32,1024]{2,1,0:T(8,128)} %param.9, f32[32,32,1024]{2,0,1:T(8,128)S(1)} %copy-done.1, ...), kind=kLoop, calls=%fused_computation.12 | loop fusion | flops 7340032 | bytes 21233792 | tf_op jit(solution)/shard_map/div | solution.py:87
  231.7 4.4 %copy.46 = f32[32,32,1024]{2,1,0:T(8,128)} copy(f32[32,32,1024]{2,0,1:T(8,128)S(1)} %fusion.6) | data formatting | bytes 8388608 | tf_op jit(solution)/shard_map/div | solution.py:87
  (6 shorter events, 0.0 us)
Async XLA Ops:
  13.7 23.6 %all-to-all-start = ((s32[16,1,8]{2,1,0:T(1,128)}), s32[16,1,8]{2,1,0:T(1,128)S(1)}, u32[]{:S(2)}, u32[]{:S(2)}) async-start(s32[16,1,8]{2,1,0:T(1,128)} %copy.33), calls=%async_computation | async-start | bytes 16384 | tf_op jit(solution)/shard_map/all_to_all | solution.py:77
  22.2 30.5 %collective-permute-start.1 = (f32[1,32,1024]{2,0,1:T(1,128)S(1)}, f32[1,32,1024]{2,0,1:T(1,128)S(1)}, u32[]{:S(2)}, u32[]{:S(2)}) collective-permute-start(f32[1,32,1024]{2,0,1:T(1,128)S(1)} %copy.37), channel_id=1, source_target_pairs={{2,0},{4,2},{6,4},{8,6},{10,8},{12,10},{14,12},{16,14},{18,16},{20... | collective-permute-start | bytes 393224 | tf_op jit(solution)/shard_map/ppermute | solution.py:22
  23.7 29.1 %collective-permute-start = (f32[1,32,1024]{2,0,1:T(1,128)S(1)}, f32[1,32,1024]{2,0,1:T(1,128)S(1)}, u32[]{:S(2)}, u32[]{:S(2)}) collective-permute-start(f32[1,32,1024]{2,0,1:T(1,128)S(1)} %copy.35), channel_id=1, source_target_pairs={{0,2},{2,4},{4,6},{6,8},{8,10},{10,12},{12,14},{14,16},{16,18},{18... | collective-permute-start | bytes 393224 | tf_op jit(solution)/shard_map/ppermute | solution.py:21
  37.4 34.3 %all-to-all-start.1 = ((bf16[16,8,32,128]{3,2,1,0:T(8,128)(2,1)}), bf16[16,8,32,128]{3,2,1,0:T(8,128)(2,1)S(1)}, u32[]{:S(2)}, u32[]{:S(2)}) async-start(bf16[16,8,32,128]{3,2,1,0:T(8,128)(2,1)} %scatter_fusion.1), calls=%async_computation.1 | async-start | bytes 2097152 | tf_op jit(solution)/shard_map/all_to_all | solution.py:76
  44.4 168.3 %all-reduce.2.cloned.1.call-start = ((), (), s32[]{:S(2)}) async-start(), calls=%async_computation.2 | async-start | bytes 8388608 | tf_op jit(solution)/shard_map/psum | solution.py:84
  44.4 8.3 %copy-start.2 = (f32[32]{0:T(128)S(1)}, f32[32]{0:T(128)}, u32[]{:S(2)}) copy-start(f32[32]{0:T(128)} %param.10) | copy-start | bytes 388
  212.7 9.7 %copy-start = (f32[32,32,1024]{2,1,0:T(8,128)S(1)}, f32[32,32,1024]{2,1,0:T(8,128)}, u32[]{:S(2)}) copy-start(f32[32,32,1024]{2,1,0:T(8,128)} %param.8) | copy-start | bytes 12582916
  212.7 9.7 %copy-start.1 = (f32[32,32,1024]{2,0,1:T(8,128)S(1)}, f32[32,32,1024]{2,0,1:T(8,128)}, u32[]{:S(2)}) copy-start(f32[32,32,1024]{2,0,1:T(8,128)} %all-reduce.2.cloned.1.call-done) | copy-start | bytes 12582916
  216.0 3.2 %collective-permute-start.2 = (f32[1,32,1024]{2,0,1:T(1,128)S(1)}, f32[1,32,1024]{2,0,1:T(1,128)S(1)}, u32[]{:S(2)}, u32[]{:S(2)}) collective-permute-start(f32[1,32,1024]{2,0,1:T(1,128)S(1)} %get-tuple-element.5), channel_id=1, source_target_pairs={{0,2},{2,4},{4,6},{6,8},{8,10},{10,12},{12,14},{14,16},{16,18},{18... | collective-permute-start | bytes 393224 | tf_op jit(solution)/shard_map/ppermute | solution.py:21
  217.9 4.5 %collective-permute-start.3 = (f32[1,32,1024]{2,0,1:T(1,128)S(1)}, f32[1,32,1024]{2,0,1:T(1,128)S(1)}, u32[]{:S(2)}, u32[]{:S(2)}) collective-permute-start(f32[1,32,1024]{2,0,1:T(1,128)S(1)} %get-tuple-element.6), channel_id=1, source_target_pairs={{2,0},{4,2},{6,4},{8,6},{10,8},{12,10},{14,12},{16,14},{18,16},{20... | collective-permute-start | bytes 393224 | tf_op jit(solution)/shard_map/ppermute | solution.py:22
Sparse Core Ops, SparseCore 0:
  102.4 110.2 all-reduce.1
where the time goes:
time: 247 us; the launch traced here: 243 us
  waiting for transfers between devices  114 us (46%)
  other arithmetic  49.3 us (20%)
  local copies, waits for them, and re-layouts  36.6 us (15%)
  starting transfers between devices  21.9 us (9%)
  between operations  13.6 us (6%)
  matrix products  7.88 us (3%)
    psum x1, waiting for transfers between devices, on_device(): total = lax.psum(back, 'view')  110 us
    scatter-add x1, other arithmetic, on_device(): sums = sums.at[index.reshape(-1)].add(ratios.reshape(-1, planes, bins))  18.7 us
    div x1, other arithmetic, on_device(): return activity * smoothed / sensitivity  9.36 us
    scatter x1, local copies, waits for them, and re-layouts, on_device(): send_rows = jnp.zeros((slab_count, capacity, planes, bins), jnp.bfloat16)...  8 us
    all_to_all x1, starting transfers between devices, on_device(): lax.all_to_all(send_index, 'slab', split_axis=0, concat_axis=0, tiled=True)  7.36 us
    all_to_all x1, starting transfers between devices, on_device(): lax.all_to_all(send_rows, 'slab', split_axis=0, concat_axis=0, tiled=True)  6.99 us
    convert_element_type x1, other arithmetic, on_device(): ((1.0 - 2.0 * weight) * activity + weight * (padded[:-2] + padded[2:])).a...  6.8 us
    unnamed x7, local copies, waits for them, and re-layouts  6.65 us
  transfers between devices with their start and end apart: 7, of which 2 were waited for; matrix products, arithmetic and copies ran while one was open for 16% of the time, Pallas kernels for 0%

commit v1 on v0

v1 whole, which is shorter than its diff:
```python
import functools
import math

import jax
import jax.numpy as jnp
from jax import lax
from jax.experimental import pallas as pl
from jax.experimental.pallas import tpu as pltpu
from jax.sharding import PartitionSpec as P

VIEWS_ALL = 336
BACKGROUND = 0.05
SLOTS = 8
EDGE = 2 * SLOTS
META = 16
HALF = 64
F32 = jnp.float32
BF16 = jnp.bfloat16
SMEM = pltpu.SMEM
VMEM = pltpu.VMEM
MIB = 1024 * 1024


def iota(shape, dim):
    return lax.broadcasted_iota(jnp.int32, shape, dim)


def matmul(a, b, contract=(1, 0)):
    dims = (((contract[0],), (contract[1],)), ((), ()))
    return lax.dot_general(a, b, dims, preferred_element_type=F32)


def params(limit):
    return pltpu.CompilerParams(vmem_limit_bytes=limit * MIB)


def bucket_kernel(
    slabs, capacity, lines, slab_s, slab_v, line_v, angle_v, measured, out, count, extra, sems
):
    blocks, planes, bins = measured.shape
    body = capacity * planes
    for s in range(slabs):
        count[s] = 0

    def send(m, carry):
        s = slab_s[0, m]
        place = count[s]
        count[s] = place + 1
        start = pl.multiple_of(place * planes, planes)
        pltpu.make_async_copy(
            measured.at[m], out.at[s, pl.ds(start, planes), :], sems.at[0]
        ).start()
        return carry

    lax.fori_loop(0, blocks, send, 0)

    slab = slab_v[...]
    code = (angle_v[...] * lines + line_v[...] + 1).astype(F32)
    names = (iota((slabs, blocks), 0) == slab).astype(F32)
    earlier = (iota((blocks, blocks), 0) < iota((blocks, blocks), 1)).astype(BF16)
    ranks = matmul(names.astype(BF16), earlier)
    slot = jnp.sum(names * ranks, axis=0, keepdims=True).astype(jnp.int32)

    row = iota((slabs * EDGE, blocks), 0)
    place = row % EDGE
    before = place < SLOTS
    wanted = jnp.where(before, row // EDGE - 1, row // EDGE + 1)
    match = (slab == wanted) & (slot == place % SLOTS)
    chosen = match.astype(F32).astype(BF16)
    chosen_last = (match & before).astype(F32).astype(BF16)
    chosen_first = (match & ~before).astype(F32).astype(BF16)
    flat = measured[...].reshape(blocks * planes, bins)
    column = iota((blocks, blocks * planes), 1)
    base = iota((blocks, blocks * planes), 0) * planes
    first_rows = matmul((column == base).astype(F32).astype(BF16), flat).astype(BF16)
    last_rows = matmul((column == base + planes - 1).astype(F32).astype(BF16), flat).astype(BF16)
    edges = matmul(chosen_last, last_rows) + matmul(chosen_first, first_rows)
    extra[:, 0:EDGE, :] = edges.astype(BF16).reshape(slabs, EDGE, bins)

    lane = iota((bins, blocks), 0)
    low = jnp.where(lane < HALF, code, 0.0).astype(BF16)
    edge_codes = matmul(chosen, low, (1, 1)).reshape(slabs, EDGE, bins)
    own_slot = (slot + HALF == lane).astype(F32).astype(BF16)
    own_codes = matmul((names * code).astype(BF16), own_slot, (1, 1))
    extra[:, EDGE:, :] = (edge_codes + own_codes.reshape(slabs, 1, bins)).astype(BF16)

    tail = pltpu.make_async_copy(extra, out.at[:, pl.ds(body, EDGE + META), :], sems.at[1])
    tail.start()
    pltpu.make_async_copy(measured, measured, sems.at[0]).wait()
    tail.wait()


def bucket(measured, slab, line, angle, slabs, capacity, lines):
    blocks, planes, bins = measured.shape
    rows = capacity * planes + EDGE + META
    vmem = pl.BlockSpec(memory_space=VMEM)
    return pl.pallas_call(
        functools.partial(bucket_kernel, slabs, capacity, lines),
        out_shape=jax.ShapeDtypeStruct((slabs, rows, bins), BF16),
        in_specs=[pl.BlockSpec(memory_space=SMEM)] + [vmem] * 4,
        out_specs=pl.BlockSpec(memory_space=pl.ANY),
        scratch_shapes=[
            SMEM((slabs,), jnp.int32),
            VMEM((slabs, EDGE + META, bins), BF16),
            pltpu.SemaphoreType.DMA((2,)),
        ],
        compiler_params=params(16),
        name="bucket",
    )(slab, slab, line, angle, measured)


def front_kernel(groups, lines, width, spacing, offset, activity, low, high, k_out, r_out, blurred):
    rows, length = activity.shape
    planes = rows // lines
    angles = spacing.shape[1]
    bins = k_out.shape[1] // angles

    def put(at, w, here, down, up):
        value = (1.0 - 2.0 * w) * here + w * (down + up)
        blurred[pl.ds(at, lines), :] = value.astype(BF16)

    def plane(z):
        return activity[pl.ds(z * lines, lines), :]

    near_low, near_high = low[lines : 2 * lines, :], high[0:lines, :]
    wide_low = low[2 * lines : 2 * lines + 1, :]
    wide_high = high[2 * lines : 2 * lines + 1, :]
    put(0, wide_low, near_low, low[0:lines, :], plane(0))
    put(lines, width[0], plane(0), near_low, plane(1))
    put(planes * lines, width[planes - 1], plane(planes - 1), plane(planes - 2), near_high)
    put((planes + 1) * lines, wide_high, near_high, plane(planes - 1), high[lines : 2 * lines, :])

    def inner(z, carry):
        start = pl.multiple_of(z * lines, lines)
        here = activity[pl.ds(start, lines), :]
        down = activity[pl.ds(pl.multiple_of(start - lines, lines), lines), :]
        up = activity[pl.ds(pl.multiple_of(start + lines, lines), lines), :]
        put(pl.multiple_of(start + lines, lines), width[z], here, down, up)
        return carry

    lax.fori_loop(1, planes - 1, inner, 0)

    step_width = length / bins
    deviation = 0.25 * step_width
    scale = deviation * math.sqrt(2.0 * math.pi)
    some = 16
    chunk = r_out.shape[1] // 4
    for g in range(groups):

        def fill(i, carry, g=g):
            start = pl.multiple_of(i * some, some)
            a = i // (bins // some)
            first = (i % (bins // some)) * some
            t = (iota((some, length), 0) + first).astype(F32) + 0.5 - bins / 2
            voxel = iota((some, length), 1).astype(F32) + 0.5 - length / 2
            distance = voxel - (t * spacing[g, a] + offset[g, a])
            value = jnp.exp(-distance * distance / (2.0 * deviation * deviation)) / scale
            k_out[g, pl.ds(start, some), :] = value.astype(BF16)
            return carry

        lax.fori_loop(0, angles * bins // some, fill, 0)

        def project(i, carry, g=g):
            start = pl.multiple_of(i * chunk, 16)
            estimate = matmul(blurred[pl.ds(start, chunk), :], k_out[g], (1, 1))
            r_out[g, pl.ds(start, chunk), :] = 1.0 / (estimate + BACKGROUND)
            return carry

        lax.fori_loop(0, 4, project, 0)


def front(width, spacing, offset, activity, low, high, lines, bins):
    rows, length = activity.shape
    groups, angles = spacing.shape
    extended = rows + 2 * lines
    smem, vmem = pl.BlockSpec(memory_space=SMEM), pl.BlockSpec(memory_space=VMEM)
    flops = groups * 2 * extended * length * angles * bins
    return pl.pallas_call(
        functools.partial(front_kernel, groups, lines),
        out_shape=(
            jax.ShapeDtypeStruct((groups, angles * bins, length), BF16),
            jax.ShapeDtypeStruct((groups, extended, angles * bins), F32),
        ),
        in_specs=[smem, smem, smem, vmem, vmem, vmem],
        out_specs=(vmem, vmem),
        scratch_shapes=[VMEM((extended, length), BF16)],
        compiler_params=params(48),
        cost_estimate=pl.CostEstimate(
            flops=flops, bytes_accessed=rows * length * 12, transcendentals=groups * MIB
        ),
        name="front",
    )(width, spacing, offset, activity, low, high)


def tail_kernel(
    capacity, lines, *refs
):
    (width, low, high, received, k_in, r_in, activity_in, sensitivity_in, out) = refs[:9]
    (sums, total, k_buf, r_buf, activity, sensitivity, updated, codes_v, codes, sems) = refs[9:]
    groups, slabs, rows_sent, bins = received.shape
    rows, length = activity.shape
    planes = rows // lines
    extended = rows + 2 * lines
    angles = k_in.shape[1] // bins
    body = capacity * planes
    shift = lines.bit_length() - 1

    def fetch(g):
        slot = g % 2
        return (
            pltpu.make_async_copy(k_in.at[g], k_buf.at[slot], sems.at[slot]),
            pltpu.make_async_copy(r_in.at[g], r_buf.at[slot], sems.at[2 + slot]),
        )

    for copy in fetch(0):
        copy.start()
    for g in range(groups):
        for s in range(slabs):
            tile = received[g, s, body + EDGE : body + EDGE + META, :].astype(F32)
            codes_v[g * slabs + s : g * slabs + s + 1, :] = tile[0:1, :].astype(jnp.int32)
    list_codes = pltpu.make_async_copy(codes_v, codes, sems.at[4])
    list_codes.start()
    get_activity = pltpu.make_async_copy(activity_in, activity, sems.at[5])
    get_activity.start()
    get_sensitivity = pltpu.make_async_copy(sensitivity_in, sensitivity, sems.at[6])
    get_sensitivity.start()

    chunk = extended // 4
    for g in range(groups):
        if g + 1 < groups:
            for copy in fetch(g + 1):
                copy.start()

        def clear(i, carry):
            start = pl.multiple_of(lines + i * lines, lines)
            for a in range(angles):
                sums[a, pl.ds(start, lines), :] = jnp.zeros((lines, bins), F32)
            return carry

        lax.fori_loop(0, planes, clear, 0)

        side = slabs * SLOTS
        edge_rows = received[g, :, body : body + EDGE, :].astype(F32)
        edge_codes = received[g, :, body + EDGE : body + EDGE + META, :].astype(F32)
        lane = iota((side, bins), 1)
        for part, at in ((0, 0), (1, extended - lines)):
            data = edge_rows[:, part * SLOTS : (part + 1) * SLOTS, :].reshape(side, bins)
            code = edge_codes[:, part * SLOTS : (part + 1) * SLOTS, :].reshape(side, bins)
            code = jnp.where(lane < HALF, code, pltpu.roll(code, HALF, 1)).astype(jnp.int32)
            index = code - 1
            named = (index & (lines - 1) == lane) & (code > 0)
            named = jnp.transpose(named.astype(F32))[0:lines, :].astype(BF16)
            for a in range(angles):
                of_angle = (index >> shift == a) & (code > 0)
                spread = jnp.where(of_angle, data, 0.0).astype(BF16)
                sums[a, at : at + lines, :] = matmul(named, spread)

        if g == 0:
            list_codes.wait()

        def scatter(s, carry, g=g):
            for p in range(capacity):
                code = codes[g * slabs + s, HALF + p]

                @pl.when(code > 0)
                def _():
                    index = code - 1
                    a = index >> shift
                    place = pl.ds(lines + (index & (lines - 1)), planes, stride=lines)
                    block = received[g, s, p * planes : (p + 1) * planes, :].astype(F32)
                    sums[a, place, :] = sums[a, place, :] + block

            return carry

        lax.fori_loop(0, slabs, scatter, 0)

        for copy in fetch(g):
            copy.wait()

        def project(i, carry, g=g):
            start = pl.multiple_of(i * chunk, 16)
            here = pl.ds(start, chunk)
            parts = []
            for a in range(angles):
                inverse = r_buf[g % 2, here, a * bins : (a + 1) * bins]
                parts.append((sums[a, here, :] * inverse).astype(BF16))
            back = matmul(jnp.concatenate(parts, axis=1), k_buf[g % 2])
            total[here, :] = back if g == 0 else total[here, :] + back
            return carry

        lax.fori_loop(0, 4, project, 0)

    get_activity.wait()
    get_sensitivity.wait()
    wide_low, wide_high = low[0:1, :], high[0:1, :]

    def smooth(z, w_down, w_up):
        start = z * lines
        w = width[z]
        down = total[pl.ds(start, lines), :]
        here = total[pl.ds(start + lines, lines), :]
        up = total[pl.ds(start + 2 * lines, lines), :]
        smoothed = (1.0 - 2.0 * w) * here + w_down * down + w_up * up
        at = pl.ds(start, lines)
        updated[at, :] = activity[at, :] * smoothed / sensitivity[at, :]

    pieces = 4
    count = planes // pieces
    writes = []
    for piece in range(pieces):
        first, last = piece * count, (piece + 1) * count
        if piece == 0:
            smooth(0, wide_low, width[1])
            first = 1
        if piece == pieces - 1:
            last = planes - 1

        def inner(z, carry):
            smooth(z, width[z - 1], width[z + 1])
            return carry

        lax.fori_loop(first, last, inner, 0)
        if piece == pieces - 1:
            smooth(planes - 1, width[planes - 2], wide_high)
        at = pl.ds(piece * count * lines, count * lines)
        write = pltpu.make_async_copy(updated.at[at, :], out.at[at, :], sems.at[7 + piece])
        write.start()
        writes.append(write)
    for write in writes:
        write.wait()


def tail(width, low, high, received, k_all, r_all, activity, sensitivity, capacity, lines):
    groups, slabs, _, bins = received.shape
    rows, length = activity.shape
    extended = rows + 2 * lines
    wide = k_all.shape[1]
    angles = wide // bins
    smem, vmem = pl.BlockSpec(memory_space=SMEM), pl.BlockSpec(memory_space=VMEM)
    anywhere = pl.BlockSpec(memory_space=pl.ANY)
    edge = pl.BlockSpec((8, length), lambda i: (2 * lines // 8, 0))
    whole = pl.BlockSpec(received.shape, lambda i: (0, 0, 0, 0))
    return pl.pallas_call(
        functools.partial(tail_kernel, capacity, lines),
        out_shape=jax.ShapeDtypeStruct((rows, length), F32),
        grid=(1,),
        in_specs=[smem, edge, edge, whole] + [anywhere] * 4,
        out_specs=anywhere,
        scratch_shapes=[
            VMEM((angles, extended, bins), F32),
            VMEM((extended, length), F32),
            VMEM((2, wide, length), BF16),
            VMEM((2, extended, wide), F32),
            VMEM((rows, length), F32),
            VMEM((rows, length), F32),
            VMEM((rows, length), F32),
            VMEM((groups * slabs, bins), jnp.int32),
            SMEM((groups * slabs, bins), jnp.int32),
            pltpu.SemaphoreType.DMA((11,)),
        ],
        compiler_params=params(56),
        cost_estimate=pl.CostEstimate(
            flops=groups * 2 * extended * length * wide,
            bytes_accessed=rows * length * 12,
            transcendentals=0,
        ),
        name="tail",
    )(width, low, high, received, k_all, r_all, activity, sensitivity)


def other_groups(value):
    size = lax.axis_size("view")
    if size == 2:
        other = lax.ppermute(value, "view", [(0, 1), (1, 0)])
        return jnp.stack([value, other])
    return lax.all_gather(value, "view")


def on_device(
    activity, sensitivity, psf_width, measured, block_slab, block_line, block_angle, subset_views
):
    planes, lines, length = activity.shape
    _, blocks, _, bins = measured.shape
    slabs = lax.axis_size("slab")
    capacity = 2 * blocks // slabs
    assert capacity <= SLOTS and subset_views.shape[1] * lines <= 256

    flat = activity.reshape(planes * lines, length)
    ups = [(i, i + 1) for i in range(slabs - 1)]
    downs = [(j, i) for i, j in ups]
    wide_first = jnp.broadcast_to(psf_width[0:1, None], (8, length))
    wide_last = jnp.broadcast_to(psf_width[planes - 1 :, None], (8, length))
    low = lax.ppermute(jnp.concatenate([flat[-2 * lines :], wide_last]), "slab", ups)
    high = lax.ppermute(jnp.concatenate([flat[: 2 * lines], wide_first]), "slab", downs)

    views = other_groups(subset_views[0])
    angle = math.pi * views.astype(F32) / VIEWS_ALL
    step_width = length / bins
    spacing = step_width * (0.75 + 0.25 * jnp.cos(2.0 * angle))
    offset = 1.5 * step_width * jnp.sin(angle)

    send = bucket(
        measured[0], block_slab.reshape(1, blocks), block_line, block_angle, slabs, capacity, lines
    )
    own = lax.all_to_all(send, "slab", split_axis=0, concat_axis=0, tiled=True)
    received = other_groups(own)

    k_all, r_all = front(psf_width, spacing, offset, flat, low, high, lines, bins)
    result = tail(
        psf_width,
        low,
        high,
        received,
        k_all,
        r_all,
        flat,
        sensitivity.reshape(planes * lines, length),
        capacity,
        lines,
    )
    return result.reshape(planes, lines, length)


def solution(mesh):
    in_specs = (
        P("slab", None, None),
        P("slab", None, None),
        P("slab"),
        P("view", "slab", None, None),
        P("view", "slab", None),
        P("view", "slab"),
        P("view", "slab"),
        P("view", None),
    )
    out_specs = P("slab", None, None)
    return jax.shard_map(
        on_device, mesh=mesh, in_specs=in_specs, out_specs=out_specs, check_vma=False
    )
```

time: 247 us -> 108 us (0.44); the launches traced: 243 us -> 107 us
  waiting for transfers between devices: 114 us -> 18.8 us
  other arithmetic: 49.3 us -> 1.78 us
  blocking collectives: 0 us -> 36.6 us
  Pallas kernels: 0 us -> 36.2 us
  local copies, waits for them, and re-layouts: 36.6 us -> 7.04 us
  starting transfers between devices: 21.9 us -> 6.43 us
  between operations: 13.6 us -> 0.12 us
  matrix products: 7.88 us -> 0 us
    psum x1 -> x0, waiting for transfers between devices: 110 us -> none  [on_device(): total = lax.psum(back, 'view')]
    all_to_all x0 -> x1, blocking collectives: none -> 36.6 us  [on_device(): own = lax.all_to_all(send, 'slab', split_axis=0, concat_axis=0, tiled=True)]
    pallas_call x0 -> x3, Pallas kernels: none -> 36.2 us  [the longest x1 17.7 us: front(): pl.pallas_call(functools.partial(front_kernel, groups, lines), out_shape=...]
    scatter-add x1 -> x0, other arithmetic: 18.7 us -> none  [on_device(): sums = sums.at[index.reshape(-1)].add(ratios.reshape(-1, planes, bins))]
    ppermute x4, waiting for transfers between devices: 3.19 us -> 18.8 us  [the longest x2 18.8 us: other_groups(): other = lax.ppermute(value, 'view', [(0, 1), (1, 0)])]
    all_to_all x2 -> x0, starting transfers between devices: 14.4 us -> none  [the longest x1 7.36 us: on_device(): lax.all_to_all(send_index, 'slab', split_axis=0, concat_axis=0, tiled=True)]
    scatter x2 -> x0, local copies, waits for them, and re-layouts: 11.5 us -> none  [the longest x1 8 us: on_device(): send_rows = jnp.zeros((slab_count, capacity, planes, bins), jnp.bfloat16)...]
    div x2 -> x0, other arithmetic: 11.4 us -> none  [the longest x1 9.36 us: on_device(): return activity * smoothed / sensitivity]
  transfers between devices with their start and end apart: 7 -> 4, of which waited for: 2 -> 1; matrix products, arithmetic and copies ran while one was open for 16% -> 3% of each run, Pallas kernels for 0% -> 17%
where the time goes in v1:
time: 108 us; the launch traced here: 107 us
  blocking collectives  36.6 us (34%)
  Pallas kernels  36.2 us (34%)
  waiting for transfers between devices  18.8 us (17%)
  local copies, waits for them, and re-layouts  7.04 us (7%)
  starting transfers between devices  6.43 us (6%)
  other arithmetic  1.78 us (2%)
    all_to_all x1, blocking collectives, on_device(): own = lax.all_to_all(send, 'slab', split_axis=0, concat_axis=0, tiled=True)  36.6 us
    ppermute x2, waiting for transfers between devices, other_groups(): other = lax.ppermute(value, 'view', [(0, 1), (1, 0)])  18.8 us
    pallas_call x1, Pallas kernels, front(): pl.pallas_call(functools.partial(front_kernel, groups, lines), out_shape=...  17.7 us
    pallas_call x1, Pallas kernels, tail(): pl.pallas_call(functools.partial(tail_kernel, capacity, lines), out_shape...  15.9 us
    unnamed x18, local copies, waits for them, and re-layouts  4.05 us
    ppermute x1, starting transfers between devices, on_device(): lax.ppermute(jnp.concatenate([flat[-2 * lines:], wide_last]), 'slab', ups)  3.05 us
    pallas_call x1, Pallas kernels, bucket(): pl.pallas_call(functools.partial(bucket_kernel, slabs, capacity, lines),...  2.57 us
  transfers between devices with their start and end apart: 4, of which 1 were waited for; matrix products, arithmetic and copies ran while one was open for 3% of the time, Pallas kernels for 17%

profile of v1, /device:TPU:0, one launch (start us, length us, event | category | flops | bytes accessed | tf_op | source)
XLA Modules:
  0.0 107.0 jit_solution(10224394520025325981)
XLA Ops:
  0.0 0.0 copy-start.4
  0.0 0.0 copy-start.1
  0.0 1.1 copy-done.1
  1.1 0.0 copy-start.5
  1.1 0.7 copy-done.5
  1.7 0.0 copy-start.6
  1.7 0.7 copy-done.6
  2.4 0.0 copy-start.7
  2.4 0.7 copy-done.7
  3.0 2.6 %bucket.1 = bf16[16,288,128]{2,1,0:T(8,128)(2,1)S(1)} custom-call(s32[1,64]{1,0:T(1,128)S(1)} %bitcast.14, s32[1,64]{1,0:T(1,128)S(1)} %bitcast.15, s32[1,64]{1,0:T(1,128)S(1)} %copy-done.6, s32[1,64]{1,0:T(1,128)S(1)} %copy-done.7, bf16[64,32,128]{2,1,0:T(8,128)(2,1)S(1)} %bitcast.13), custom_call_target="tpu_custom_call" | custom-call | tf_op jit(solution)/shard_map/bucket/pallas_call | solution.py:97
  5.6 0.0 copy-start.8
  5.6 36.6 %all_to_all.5 = bf16[16,288,128]{2,1,0:T(8,128)(2,1)S(1)} all-to-all(bf16[16,288,128]{2,1,0:T(8,128)(2,1)S(1)} %bucket.1), channel_id=1, replica_groups=mesh['slab'=16,'view'=2] {'slab'}, dimensions={0} | all-to-all | bytes 2359296 | tf_op jit(solution)/shard_map/all_to_all | solution.py:405
  42.3 1.5 %collective-permute-start.2 = (bf16[16,288,128]{2,1,0:T(8,128)(2,1)S(1)}, bf16[16,288,128]{2,1,0:T(8,128)(2,1)S(1)}, u32[]{:S(2)}, u32[]{:S(2)}) collective-permute-start(bf16[16,288,128]{2,1,0:T(8,128)(2,1)S(1)} %all_to_all.5), channel_id=1, source_target_pairs={{0,1},{1,0},{2,3},{3,2},{4,5},{5,4},{6,7},{7,6},{8,9},{9,8},{10,11... | collective-permute-start | bytes 3538952 | tf_op jit(solution)/shard_map/ppermute | solution.py:374
  43.8 0.0 copy-done.4
  43.8 0.6 fusion.1
  44.4 1.1 fusion
  45.5 0.7 concatenate.7
  46.1 1.3 %collective-permute-start.1 = (f32[72,1024]{1,0:T(8,128)S(1)}, f32[72,1024]{1,0:T(8,128)S(1)}, u32[]{:S(2)}, u32[]{:S(2)}) collective-permute-start(f32[72,1024]{1,0:T(8,128)S(1)} %concatenate.7), channel_id=1, source_target_pairs={{2,0},{4,2},{6,4},{8,6},{10,8},{12,10},{14,12},{16,14},{18,16},{20... | collective-permute-start | bytes 884744 | tf_op jit(solution)/shard_map/ppermute | solution.py:394
  47.4 0.7 concatenate.6
  48.1 3.0 %collective-permute-start = (f32[72,1024]{1,0:T(8,128)S(1)}, f32[72,1024]{1,0:T(8,128)S(1)}, u32[]{:S(2)}, u32[]{:S(2)}) collective-permute-start(f32[72,1024]{1,0:T(8,128)S(1)} %concatenate.6), channel_id=1, source_target_pairs={{0,2},{2,4},{4,6},{6,8},{8,10},{10,12},{12,14},{14,16},{16,18},{18... | collective-permute-start | bytes 884744 | tf_op jit(solution)/shard_map/ppermute | solution.py:393
  51.1 0.0 copy-done.8
  51.2 0.6 collective-permute-start.3
  51.7 18.8 %collective-permute-done.3 = s32[8]{0:T(128)S(1)} collective-permute-done((s32[8]{0:T(128)S(1)}, s32[8]{0:T(128)S(1)}, u32[]{:S(2)}, u32[]{:S(2)}) %collective-permute-start.3) | collective-permute-done | bytes 64 | tf_op jit(solution)/shard_map/ppermute | solution.py:374
  70.5 0.1 sine_multiply_fusion
  70.6 0.0 collective-permute-done.1.high.refs_2_
  70.6 0.0 copy-start.2
  70.6 0.0 collective-permute-done.low.refs_1_
  70.6 0.0 copy-start.3
  70.6 17.7 %front.1 = (bf16[2,1024,1024]{2,1,0:T(8,128)(2,1)S(1)}, f32[2,1088,1024]{2,1,0:T(8,128)}) custom-call(f32[32]{0:T(128)S(1)} %copy-done.4, f32[2,8]{1,0:T(2,128)S(1)} %get-tuple-element.12.spacing, f32[2,8]{1,0:T(2,128)S(1)} %get-tuple-element.11.offset, f32[1024,1024]{1,0:T(8,128)} %bitcast.16, f32[72,1024]{1,0:T(8,128)S(1)} %collective-permute-done.low.refs_1_, ...), custom_call_target="tpu_custom_call" | custom-call | flops 4563402752 | bytes 12582912 | tf_op jit(solution)/shard_map/front/pallas_call | solution.py:178
  88.3 0.0 copy-done.2
  88.3 0.0 copy-done.3
  88.3 0.0 copy-start
  88.3 0.0 collective-permute-done.2
  88.4 1.7 %pad_maximum_fusion.refs_3_ = bf16[2,16,288,128]{3,2,1,0:T(8,128)(2,1)} fusion(bf16[1,16,288,128]{3,2,1,0:T(8,128)(2,1)S(1)} %bitcast.20, bf16[1,16,288,128]{3,2,1,0:T(8,128)(2,1)S(1)} %bitcast.18), kind=kLoop, calls=%fused_computation | loop fusion | flops 1179648 | bytes 4718592 | tf_op jit(solution)/shard_map/stack | solution.py:375
  90.1 1.0 copy-done
  91.1 15.9 %tail.1 = f32[1024,1024]{1,0:T(8,128)} custom-call(f32[32]{0:T(128)} %refs_0_.1, f32[72,1024]{1,0:T(8,128)} %copy-done.3, f32[72,1024]{1,0:T(8,128)} %copy-done.2, bf16[2,16,288,128]{3,2,1,0:T(8,128)(2,1)} %pad_maximum_fusion.refs_3_, bf16[2,1024,1024]{2,1,0:T(8,128)(2,1)} %copy-done, f32[2,1088,1024]{2,1,0:T(8,128)} %get-tuple-element.8.refs_5_, ...), custom_call_target="tpu_custom_call" | custom-call | flops 4563402752 | bytes 12582912 | tf_op jit(solution)/shard_map/tail/pallas_call | solution.py:343
Async XLA Ops:
  0.0 43.8 %copy-start.4 = (f32[32]{0:T(128)S(1)}, f32[32]{0:T(128)}, u32[]{:S(2)}) copy-start(f32[32]{0:T(128)} %refs_0_.1) | copy-start | bytes 388
  0.0 1.1 copy-start.1
  1.1 0.7 copy-start.5
  1.7 0.7 copy-start.6
  2.4 0.7 copy-start.7
  5.6 45.5 %copy-start.8 = (s32[1,8]{1,0:T(1,128)S(1)}, s32[1,8]{1,0:T(1,128)}, u32[]{:S(2)}) copy-start(s32[1,8]{1,0:T(1,128)} %param.15) | copy-start | bytes 100
  42.3 46.1 %collective-permute-start.2 = (bf16[16,288,128]{2,1,0:T(8,128)(2,1)S(1)}, bf16[16,288,128]{2,1,0:T(8,128)(2,1)S(1)}, u32[]{:S(2)}, u32[]{:S(2)}) collective-permute-start(bf16[16,288,128]{2,1,0:T(8,128)(2,1)S(1)} %all_to_all.5), channel_id=1, source_target_pairs={{0,1},{1,0},{2,3},{3,2},{4,5},{5,4},{6,7},{7,6},{8,9},{9,8},{10,11... | collective-permute-start | bytes 3538952 | tf_op jit(solution)/shard_map/ppermute | solution.py:374
  46.1 24.4 %collective-permute-start.1 = (f32[72,1024]{1,0:T(8,128)S(1)}, f32[72,1024]{1,0:T(8,128)S(1)}, u32[]{:S(2)}, u32[]{:S(2)}) collective-permute-start(f32[72,1024]{1,0:T(8,128)S(1)} %concatenate.7), channel_id=1, source_target_pairs={{2,0},{4,2},{6,4},{8,6},{10,8},{12,10},{14,12},{16,14},{18,16},{20... | collective-permute-start | bytes 884744 | tf_op jit(solution)/shard_map/ppermute | solution.py:394
  48.1 22.5 %collective-permute-start = (f32[72,1024]{1,0:T(8,128)S(1)}, f32[72,1024]{1,0:T(8,128)S(1)}, u32[]{:S(2)}, u32[]{:S(2)}) collective-permute-start(f32[72,1024]{1,0:T(8,128)S(1)} %concatenate.6), channel_id=1, source_target_pairs={{0,2},{2,4},{4,6},{6,8},{8,10},{10,12},{12,14},{14,16},{16,18},{18... | collective-permute-start | bytes 884744 | tf_op jit(solution)/shard_map/ppermute | solution.py:393
  51.2 19.4 %collective-permute-start.3 = (s32[8]{0:T(128)S(1)}, s32[8]{0:T(128)S(1)}, u32[]{:S(2)}, u32[]{:S(2)}) collective-permute-start(s32[8]{0:T(128)S(1)} %bitcast.23), channel_id=1, source_target_pairs={{0,1},{1,0},{2,3},{3,2},{4,5},{5,4},{6,7},{7,6},{8,9},{9,8},{10,11... | collective-permute-start | bytes 104 | tf_op jit(solution)/shard_map/ppermute | solution.py:374
  70.6 17.8 %copy-start.2 = (f32[72,1024]{1,0:T(8,128)}, f32[72,1024]{1,0:T(8,128)S(1)}, u32[]{:S(2)}) copy-start(f32[72,1024]{1,0:T(8,128)S(1)} %collective-permute-done.1.high.refs_2_) | copy-start | bytes 884740
  70.6 17.7 %copy-start.3 = (f32[72,1024]{1,0:T(8,128)}, f32[72,1024]{1,0:T(8,128)S(1)}, u32[]{:S(2)}) copy-start(f32[72,1024]{1,0:T(8,128)S(1)} %collective-permute-done.low.refs_1_) | copy-start | bytes 884740
  88.3 2.8 %copy-start = (bf16[2,1024,1024]{2,1,0:T(8,128)(2,1)}, bf16[2,1024,1024]{2,1,0:T(8,128)(2,1)S(1)}, u32[]{:S(2)}) copy-start(bf16[2,1024,1024]{2,1,0:T(8,128)(2,1)S(1)} %get-tuple-element.7.refs_4_) | copy-start | bytes 12582916

commit v2 on v0

v2 whole, which is shorter than its diff:
```python
import functools
import math

import jax
import jax.numpy as jnp
from jax import lax
from jax.experimental import pallas as pl
from jax.experimental.pallas import tpu as pltpu
from jax.sharding import PartitionSpec as P

VIEWS_ALL = 336
BACKGROUND = 0.05
SLOTS = 8
PAIR = 2 * SLOTS
META = 16
WIDE = 64
F32 = jnp.float32
BF16 = jnp.bfloat16
I32 = jnp.int32
SMEM = pltpu.SMEM
VMEM = pltpu.VMEM
MIB = 1024 * 1024
LIMIT_FRONT = 12
LIMIT_BACK = 14
LIMIT_UPDATE = 16


def iota(shape, dim):
    return lax.broadcasted_iota(I32, shape, dim)


def matmul(a, b, contract=(1, 0)):
    dims = (((contract[0],), (contract[1],)), ((), ()))
    return lax.dot_general(a, b, dims, preferred_element_type=F32)


def params(limit):
    return pltpu.CompilerParams(vmem_limit_bytes=limit * MIB)


def cost(flops, moved):
    return pl.CostEstimate(flops=flops, bytes_accessed=moved, transcendentals=0)


SPEC_SMEM = pl.BlockSpec(memory_space=SMEM)
SPEC_VMEM = pl.BlockSpec(memory_space=VMEM)
SPEC_ANY = pl.BlockSpec(memory_space=pl.ANY)
SPEC_HBM = pl.BlockSpec(memory_space=pltpu.HBM)


def one_hot(mask):
    return mask.astype(F32).astype(BF16)


def bucket_kernel(chips, relative, planes, lines, *refs):
    raws, tables = refs[0:2], refs[2:4]
    out, wide, flat = refs[4:]
    rows, bins = raws[0].shape
    blocks = rows // planes
    both = 2 * blocks
    me = lax.axis_index("slab")

    for i, raw in enumerate(raws):
        wide[i] = raw[...].astype(F32)

    def turn(z, carry):
        column = pl.ds(pl.multiple_of(z * bins, bins), bins)
        for i in range(2):
            part = wide[i, pl.ds(z, blocks, stride=planes), :]
            flat[i * blocks : (i + 1) * blocks, column] = part.astype(BF16)
        return carry

    lax.fori_loop(0, planes, turn, 0, unroll=4)

    def lanes(row):
        return tables[0][row : row + 1, :] + pltpu.roll(tables[1][row : row + 1, :], blocks, 1)

    slab, code = lanes(0), (lanes(2) * lines + lanes(1) + 1).astype(F32)
    shape = (both, both)
    earlier = (iota(shape, 0) < iota(shape, 1)) & (iota(shape, 0) // blocks == iota(shape, 1) // blocks)
    names = (iota((WIDE, both), 0) == slab).astype(F32)
    ranks = matmul(names.astype(BF16), one_hot(earlier))
    slot = jnp.sum(names * ranks, axis=0, keepdims=True).astype(I32)
    slot = slot + iota((1, both), 1) // blocks * SLOTS

    def target(chip):
        return (2 * chip) ^ me if relative else 2 * chip + (me & 1)

    row = iota((chips * PAIR, both), 0)
    aim = target(row // PAIR)
    here = slot == row % PAIR
    chosen = one_hot((slab == aim) & here)

    some = 2

    def deal(i, carry):
        column = pl.ds(pl.multiple_of(i * some * bins, some * bins), some * bins)
        dealt = matmul(chosen, flat[:, column]).astype(BF16)
        for j in range(some):
            at = pl.ds(pl.multiple_of((i * some + j) * PAIR, PAIR), PAIR)
            for chip in range(chips):
                part = dealt[chip * PAIR : (chip + 1) * PAIR, j * bins : (j + 1) * bins]
                out[chip, at, :] = part
        return carry

    lax.fori_loop(0, planes // some, deal, 0, unroll=4)

    body = planes * PAIR
    aim_row = target(iota((chips, both), 0))
    lane = iota((bins, both), 0)
    codes = jnp.zeros((chips, bins), F32)
    for kind, (shift, z) in enumerate(((0, None), (-1, planes - 1), (1, 0))):
        picked = ((slab == aim_row + shift).astype(F32) * code).astype(BF16)
        codes = codes + matmul(picked, one_hot(slot + kind * PAIR == lane), (1, 1))
        if kind:
            edge = one_hot((slab == aim + shift) & here)
            dealt = matmul(edge, flat[:, z * bins : (z + 1) * bins]).astype(BF16)
            at = body + (kind - 1) * PAIR
            for chip in range(chips):
                out[chip, at : at + PAIR, :] = dealt[chip * PAIR : (chip + 1) * PAIR, :]
    codes = codes.astype(BF16)
    for chip in range(chips):
        spread = jnp.broadcast_to(codes[chip : chip + 1, :].astype(F32), (META, bins))
        out[chip, body + 2 * PAIR :, :] = spread.astype(BF16)


def bucket(raws, tables, chips, relative, planes, lines):
    rows, bins = raws[0].shape
    sent = (planes + 2) * PAIR + META
    return pl.pallas_call(
        functools.partial(bucket_kernel, chips, relative, planes, lines),
        out_shape=jax.ShapeDtypeStruct((chips, sent, bins), BF16),
        in_specs=[SPEC_VMEM] * 4,
        out_specs=SPEC_VMEM,
        scratch_shapes=[VMEM((2, rows, bins), F32), VMEM((2 * rows // planes, planes * bins), BF16)],
        compiler_params=params(24),
        cost_estimate=cost(10**8, 4 * MIB),
        name="bucket",
    )(*raws, *tables)


def halo_kernel(width, first, final, low_out, high_out):
    edge, length = first.shape
    low_out[0:edge, :] = final[...]
    low_out[edge : edge + 8, :] = jnp.full((8, length), width[width.shape[0] - 1], F32)
    high_out[0:edge, :] = first[...]
    high_out[edge : edge + 8, :] = jnp.full((8, length), width[0], F32)


def halo(width, activity, lines):
    rows, length = activity.shape
    edge = 2 * lines
    shape = jax.ShapeDtypeStruct((edge + 8, length), F32)
    out = pl.BlockSpec((edge + 8, length), lambda i: (0, 0))
    return pl.pallas_call(
        halo_kernel,
        out_shape=(shape, shape),
        grid=(1,),
        in_specs=[
            SPEC_SMEM,
            pl.BlockSpec((edge, length), lambda i: (0, 0)),
            pl.BlockSpec((edge, length), lambda i: (rows // edge - 1, 0)),
        ],
        out_specs=(out, out),
        compiler_params=params(8),
        cost_estimate=cost(0, MIB),
        name="halo",
    )(width, activity, activity)


def blur(lines, width, activity, low, high, blurred):
    planes = activity.shape[0] // lines

    def put(at, w, here, down, up):
        value = (1.0 - 2.0 * w) * here + w * (down + up)
        blurred[pl.ds(at, lines), :] = value.astype(BF16)

    def plane(z):
        return activity[z * lines : (z + 1) * lines, :]

    near_low, near_high = low[lines : 2 * lines, :], high[0:lines, :]
    wide_low = low[2 * lines : 2 * lines + 1, :]
    wide_high = high[2 * lines : 2 * lines + 1, :]
    put(0, wide_low, near_low, low[0:lines, :], plane(0))
    put(lines, width[0], plane(0), near_low, plane(1))
    put(planes * lines, width[planes - 1], plane(planes - 1), plane(planes - 2), near_high)
    put((planes + 1) * lines, wide_high, near_high, plane(planes - 1), high[lines : 2 * lines, :])

    def inner(z, carry):
        start = pl.multiple_of(z * lines, lines)
        here = activity[pl.ds(start, lines), :]
        down = activity[pl.ds(pl.multiple_of(start - lines, lines), lines), :]
        up = activity[pl.ds(pl.multiple_of(start + lines, lines), lines), :]
        put(pl.multiple_of(start + lines, lines), width[z], here, down, up)
        return carry

    lax.fori_loop(1, planes - 1, inner, 0)


def front_kernel(lines, *refs):
    if lines is not None:
        spacing, offset, width, activity, low, high, blurred, k_out, r_out = refs
        blur(lines, width, activity, low, high, blurred)
    else:
        spacing, offset, blurred, k_out, r_out = refs
    extended, length = blurred.shape
    angles = spacing.shape[0]
    bins = k_out.shape[0] // angles
    step_width = length / bins
    deviation = 0.25 * step_width
    scale = 1.0 / (deviation * math.sqrt(2.0 * math.pi))
    sharp = -math.log2(math.e) / (2.0 * deviation * deviation)
    some = 32
    pair = 2
    voxel = iota((1, length), 1).astype(F32) + 0.5 - length / 2
    bin_at = iota((some, 1), 0).astype(F32) + 0.5 - bins / 2

    def group(q, carry):
        begin = pl.multiple_of(q * pair * bins, pair * bins)
        for i in range(pair * bins // some):
            a = q * pair + i * some // bins
            centre = (bin_at + float(i * some % bins)) * spacing[a] + offset[a]
            distance = voxel - centre
            value = jnp.exp2(distance * distance * sharp) * scale
            k_out[pl.ds(begin + i * some, some), :] = value.astype(BF16)
        columns = pl.ds(begin, pair * bins)
        estimate = matmul(blurred[...], k_out[columns, :], (1, 1))
        r_out[:, columns] = 1.0 / (estimate + BACKGROUND)
        return carry

    lax.fori_loop(0, angles // pair, group, 0)


def front(spacing, offset, blurred, bins, planes_in=None):
    (angles,) = spacing.shape
    wide = angles * bins
    lines = None
    if planes_in is None:
        extended, length = blurred.shape
        operands, specs = [blurred], [SPEC_VMEM]
    else:
        *operands, lines = planes_in
        rows, length = operands[1].shape
        extended = rows + 2 * lines
        specs = [SPEC_SMEM] + [SPEC_VMEM] * 3
    shapes = [
        jax.ShapeDtypeStruct((wide, length), BF16),
        jax.ShapeDtypeStruct((extended, wide), F32),
    ]
    if planes_in is not None:
        shapes.insert(0, jax.ShapeDtypeStruct((extended, length), BF16))
    return pl.pallas_call(
        functools.partial(front_kernel, lines),
        out_shape=shapes,
        in_specs=[SPEC_SMEM, SPEC_SMEM] + specs,
        out_specs=[SPEC_VMEM] * len(shapes),
        compiler_params=params(LIMIT_FRONT),
        cost_estimate=cost(2 * extended * length * wide, 12 * MIB),
        name="front",
    )(spacing, offset, *operands)


def back_kernel(counts, has_prior, last, lines, *refs):
    refs = list(refs)

    def take(number):
        taken = refs[:number]
        del refs[:number]
        return taken

    received = take(len(counts))
    k_buf, r_buf = take(2)
    (prior,) = take(1) if has_prior else (None,)
    if last:
        width, low, high, activity, sensitivity = take(5)
    (out,) = take(1)
    (rounded,) = take(1)
    if last:
        total, updated, sems = take(3)
    sources = [(ref, s) for ref, count in zip(received, counts) for s in range(count)]
    bins = received[0].shape[-1]
    extended, wide = r_buf.shape
    length = k_buf.shape[1]
    angles = wide // bins
    planes = extended // lines - 2
    body = planes * PAIR
    group = bins // PAIR

    rows = [
        ref[s, body + 2 * PAIR : body + 2 * PAIR + META, :].astype(F32)[0:8, :] for ref, s in sources
    ]
    lane = iota((8, bins), 1)
    named = []
    for kind in range(3):
        parts = []
        for first in range(0, len(rows), group):
            codes = jnp.zeros((8, bins), F32)
            for i in range(first, min(first + group, len(rows))):
                own = jnp.where(lane // PAIR == kind, rows[i], 0.0)
                codes = codes + pltpu.roll(own, (i - first - kind) % group * PAIR, 1)
            parts.append(codes[0:1, :])
        codes = jnp.concatenate(parts, axis=1).astype(I32)
        named.append(one_hot(codes - 1 == iota((angles * lines, codes.shape[1]), 0)))

    def sums(kind, at, start):
        held = [ref[s, pl.ds(at, PAIR), :] for ref, s in sources]
        spare = -len(held) % group * PAIR
        if spare:
            held.append(jnp.zeros((spare, bins), BF16))
        sums = matmul(named[kind], jnp.concatenate(held))
        for a in range(angles):
            place = (pl.ds(start, lines), pl.ds(a * bins, bins))
            rounded[place] = (sums[a * lines : (a + 1) * lines, :] * r_buf[place]).astype(BF16)

    sums(1, body, 0)
    sums(2, body + PAIR, extended - lines)

    def inner(z, carry):
        sums(0, pl.multiple_of(z * PAIR, PAIR), pl.multiple_of((z + 1) * lines, lines))
        return carry

    lax.fori_loop(0, planes, inner, 0, unroll=4)

    block = 256
    steps = length // block

    def project(columns):
        value = matmul(rounded[...], k_buf[:, columns])
        return prior[:, columns] + value if has_prior else value

    if not last:

        def step(i, carry):
            columns = pl.ds(pl.multiple_of(i * block, block), block)
            out[:, columns] = project(columns)
            return carry

        lax.fori_loop(0, steps, step, 0)
        return

    def write(i):
        columns = pl.ds(i * block, block)
        return pltpu.make_async_copy(updated.at[i % 2], out.at[:, columns], sems.at[i % 2])

    for i in range(steps):
        columns = pl.ds(i * block, block)
        total[...] = project(columns)
        if i >= 2:
            write(i - 2).wait()

        def smooth(z, w_down, w_up, i=i, columns=columns):
            start = z * lines
            w = width[z]
            down = total[pl.ds(start, lines), :]
            here = total[pl.ds(start + lines, lines), :]
            up = total[pl.ds(start + 2 * lines, lines), :]
            smoothed = (1.0 - 2.0 * w) * here + w_down * down + w_up * up
            at = pl.ds(start, lines)
            value = activity[at, columns] * smoothed / sensitivity[at, columns]
            updated[i % 2, at, :] = value

        def inside(z, carry, smooth=smooth):
            smooth(z, width[z - 1], width[z + 1])
            return carry

        smooth(0, low[2 * lines : 2 * lines + 1, 0:block], width[1])
        lax.fori_loop(1, planes - 1, inside, 0, unroll=10)
        smooth(planes - 1, width[planes - 2], high[2 * lines : 2 * lines + 1, 0:block])
        write(i).start()
    for i in range(max(0, steps - 2), steps):
        write(i).wait()


def back(pieces, k, r, prior, final, lines):
    extended, wide = r.shape
    _, length = k.shape
    operands = [*pieces, k, r]
    specs = [SPEC_VMEM] * len(operands)
    if prior is not None:
        operands.append(prior)
        specs.append(SPEC_VMEM)
    scratch = [VMEM((extended, wide), BF16)]
    shape = (extended, length)
    if final is not None:
        rows = extended - 2 * lines
        operands += final
        specs += [SPEC_SMEM] + [SPEC_VMEM] * 4
        scratch += [
            VMEM((extended, 256), F32),
            VMEM((2, rows, 256), F32),
            pltpu.SemaphoreType.DMA((2,)),
        ]
        shape = (rows, length)
    return pl.pallas_call(
        functools.partial(
            back_kernel,
            [piece.shape[0] for piece in pieces],
            prior is not None,
            final is not None,
            lines,
        ),
        out_shape=jax.ShapeDtypeStruct(shape, F32),
        in_specs=specs,
        out_specs=SPEC_VMEM if final is None else SPEC_HBM,
        scratch_shapes=scratch,
        compiler_params=params(LIMIT_BACK if final is None else LIMIT_UPDATE),
        cost_estimate=cost(2 * extended * length * wide, 12 * MIB),
        name="back" if final is None else "update",
    )(*operands)


def swap(value):
    return lax.ppermute(value, "view", [(0, 1), (1, 0)])


def flip(value, mask):
    size = lax.axis_size("slab")
    return lax.ppermute(value, "slab", [(i, i ^ mask) for i in range(size)])


def on_device(
    activity, sensitivity, psf_width, measured, block_slab, block_line, block_angle, subset_views
):
    planes, lines, length = activity.shape
    _, blocks, _, bins = measured.shape
    slabs, view_count = lax.axis_size("slab"), lax.axis_size("view")
    assert 2 * blocks <= SLOTS * slabs and 2 * blocks == bins and slabs <= WIDE
    assert subset_views.shape[1] * lines <= 256

    flat = activity.reshape(planes * lines, length)
    raw = measured.reshape(blocks * planes, bins)
    parts = [block_slab.reshape(1, blocks), block_line, block_angle]
    parts = [jnp.pad(part, ((i, 7 - i), (0, bins - blocks))) for i, part in enumerate(parts)]
    table = functools.reduce(jnp.add, parts)
    raws, tables = [raw, flip(raw, 1)], [table, flip(table, 1)]
    ups = [(i, i + 1) for i in range(slabs - 1)]
    downs = [(j, i) for i, j in ups]
    low_mine, high_mine = halo(psf_width, flat, lines)
    low = lax.ppermute(low_mine, "slab", ups)
    high = lax.ppermute(high_mine, "slab", downs)
    chips = slabs // 2
    if slabs == 16 and view_count == 2:
        send = bucket(raws, tables, chips, True, planes, lines)
        far = [flip(send[j : j + 1], 2 * j) for j in range(4, 8)]
        near = [send[0:1]] + [flip(send[j : j + 1], 2 * j) for j in range(1, 4)]
        over = [swap(jnp.concatenate(part)) for part in (near, far[:2], far[2:])]
        pieces = [near + far, over]
        views = [subset_views[0], swap(subset_views[0])]
    else:
        send = bucket(raws, tables, chips, False, planes, lines)
        cores = [[2 * chip + core for chip in range(chips)] for core in range(2)]
        own = lax.all_to_all(
            send, "slab", split_axis=0, concat_axis=0, axis_index_groups=cores, tiled=True
        )
        everyone = lax.all_gather(own, "view")
        pieces = [[everyone[g]] for g in range(view_count)]
        gathered = lax.all_gather(subset_views[0], "view")
        views = [gathered[g] for g in range(view_count)]

    step_width = length / bins
    fronts = []
    for view in views:
        angle = math.pi * view.astype(F32) / VIEWS_ALL
        spacing = step_width * (0.75 + 0.25 * jnp.cos(2.0 * angle))
        offset = 1.5 * step_width * jnp.sin(angle)
        if not fronts:
            planes_in = (psf_width, flat, low, high, lines)
            blurred, *made = front(spacing, offset, None, bins, planes_in)
        else:
            made = front(spacing, offset, blurred, bins)
        fronts.append(made)

    result = None
    for g in range(view_count):
        final = None
        if g == view_count - 1:
            final = [psf_width, low, high, flat, sensitivity.reshape(planes * lines, length)]
        result = back(pieces[g], *fronts[g], result, final, lines)
    return result.reshape(planes, lines, length)


def solution(mesh):
    in_specs = (
        P("slab", None, None),
        P("slab", None, None),
        P("slab"),
        P("view", "slab", None, None),
        P("view", "slab", None),
        P("view", "slab"),
        P("view", "slab"),
        P("view", None),
    )
    out_specs = P("slab", None, None)
    return jax.shard_map(
        on_device, mesh=mesh, in_specs=in_specs, out_specs=out_specs, check_vma=False
    )
```

time: 247 us -> 73.1 us (0.30); the launches traced: 243 us -> 72.9 us
  waiting for transfers between devices: 114 us -> 14.9 us
  other arithmetic: 49.3 us -> 0.94 us
  local copies, waits for them, and re-layouts: 36.6 us -> 2.95 us
  Pallas kernels: 0 us -> 29.4 us
  between operations: 13.6 us -> 0.16 us
  matrix products: 7.88 us -> 0 us
  starting transfers between devices: 21.9 us -> 24.6 us
    psum x1 -> x0, waiting for transfers between devices: 110 us -> none  [on_device(): total = lax.psum(back, 'view')]
    pallas_call x0 -> x6, Pallas kernels: none -> 29.4 us  [the longest x2 15.5 us: back(): pl.pallas_call(functools.partial(back_kernel, [piece.shape[0] for piece i...]
    scatter-add x1 -> x0, other arithmetic: 18.7 us -> none  [on_device(): sums = sums.at[index.reshape(-1)].add(ratios.reshape(-1, planes, bins))]
    ppermute x4 -> x15, starting transfers between devices: 7.5 us -> 24.6 us  [the longest x9 15.4 us: flip(): return lax.ppermute(value, 'slab', [(i, i ^ mask) for i in range(size)])]
    all_to_all x2 -> x0, starting transfers between devices: 14.4 us -> none  [the longest x1 7.36 us: on_device(): lax.all_to_all(send_index, 'slab', split_axis=0, concat_axis=0, tiled=True)]
    ppermute x4 -> x15, waiting for transfers between devices: 3.19 us -> 14.9 us  [the longest x9 10.1 us: flip(): return lax.ppermute(value, 'slab', [(i, i ^ mask) for i in range(size)])]
    scatter x2 -> x0, local copies, waits for them, and re-layouts: 11.5 us -> none  [the longest x1 8 us: on_device(): send_rows = jnp.zeros((slab_count, capacity, planes, bins), jnp.bfloat16)...]
    div x2 -> x0, other arithmetic: 11.4 us -> none  [the longest x1 9.36 us: on_device(): return activity * smoothed / sensitivity]
  transfers between devices with their start and end apart: 7 -> 15, of which waited for: 2 -> 5; matrix products, arithmetic and copies ran while one was open for 16% -> 1% of each run, Pallas kernels for 0% -> 26%
where the time goes in v2:
time: 73.1 us; the launch traced here: 72.9 us
  Pallas kernels  29.4 us (40%)
  starting transfers between devices  24.6 us (34%)
  waiting for transfers between devices  14.9 us (20%)
  local copies, waits for them, and re-layouts  2.95 us (4%)
  other arithmetic  0.94 us (1%)
    pallas_call x2, Pallas kernels, back(): pl.pallas_call(functools.partial(back_kernel, [piece.shape[0] for piece i...  15.5 us
    ppermute x9, starting transfers between devices, flip(): return lax.ppermute(value, 'slab', [(i, i ^ mask) for i in range(size)])  15.4 us
    ppermute x9, waiting for transfers between devices, flip(): return lax.ppermute(value, 'slab', [(i, i ^ mask) for i in range(size)])  10.1 us
    pallas_call x2, Pallas kernels, front(): pl.pallas_call(functools.partial(front_kernel, lines), out_shape=shapes,...  10 us
    ppermute x4, starting transfers between devices, swap(): return lax.ppermute(value, 'view', [(0, 1), (1, 0)])  5.69 us
    ppermute x4, waiting for transfers between devices, swap(): return lax.ppermute(value, 'view', [(0, 1), (1, 0)])  4.85 us
    pallas_call x1, Pallas kernels, bucket(): pl.pallas_call(functools.partial(bucket_kernel, chips, relative, planes,...  3.27 us
    unnamed x14, local copies, waits for them, and re-layouts  2.87 us
  transfers between devices with their start and end apart: 15, of which 5 were waited for; matrix products, arithmetic and copies ran while one was open for 1% of the time, Pallas kernels for 26%

profile of v2, /device:TPU:0, one launch (start us, length us, event | category | flops | bytes accessed | tf_op | source)
XLA Modules:
  0.0 72.9 jit_solution(18226900836553189611)
XLA Ops:
  0.0 3.0 %collective-permute-start.12 = (s32[8]{0:T(128)}, s32[8]{0:T(128)S(1)}, u32[]{:S(2)}, u32[]{:S(2)}) collective-permute-start(s32[8]{0:T(128)} %bitcast.16), channel_id=1, source_target_pairs={{0,1},{1,0},{2,3},{3,2},{4,5},{5,4},{6,7},{7,6},{8,9},{9,8},{10,11... | collective-permute-start | bytes 104 | tf_op jit(solution)/shard_map/ppermute | solution.py:413
  3.0 0.0 collective-permute-start
  3.0 0.7 pad_add_fusion.refs_2_
  3.7 0.6 collective-permute-start.1
  4.2 0.0 copy-start
  4.2 2.2 %copy-done = f32[32,32,1024]{2,1,0:T(8,128)S(1)} copy-done((f32[32,32,1024]{2,1,0:T(8,128)S(1)}, f32[32,32,1024]{2,1,0:T(8,128)}, u32[]{:S(2)}) %copy-start) | copy-done | bytes 4194328
  6.4 0.0 copy-start.4
  6.4 0.7 copy-done.4
  7.1 0.0 copy-start.6
  7.1 0.0 copy-start.3
  7.1 0.6 halo.1
  7.7 0.0 copy-start.1
  7.7 0.0 copy-start.5
  7.7 2.2 %collective-permute-start.13 = (f32[72,1024]{1,0:T(8,128)S(1)}, f32[72,1024]{1,0:T(8,128)S(1)}, u32[]{:S(2)}, u32[]{:S(2)}) collective-permute-start(f32[72,1024]{1,0:T(8,128)S(1)} %get-tuple-element.12), channel_id=1, source_target_pairs={{0,2},{2,4},{4,6},{6,8},{8,10},{10,12},{12,14},{14,16},{16,18},{18... | collective-permute-start | bytes 884744 | tf_op jit(solution)/shard_map/ppermute | solution.py:439
  9.9 1.3 %collective-permute-start.14 = (f32[72,1024]{1,0:T(8,128)S(1)}, f32[72,1024]{1,0:T(8,128)S(1)}, u32[]{:S(2)}, u32[]{:S(2)}) collective-permute-start(f32[72,1024]{1,0:T(8,128)S(1)} %get-tuple-element.13), channel_id=1, source_target_pairs={{2,0},{4,2},{6,4},{8,6},{10,8},{12,10},{14,12},{16,14},{18,16},{20... | collective-permute-start | bytes 884744 | tf_op jit(solution)/shard_map/ppermute | solution.py:440
  11.2 0.0 copy-done.6
  11.2 0.1 sine_multiply_fusion
  11.3 0.0 collective-permute-done.12
  11.3 0.1 sine_multiply_fusion.1
  11.3 0.0 collective-permute-done.1.refs_3_
  11.3 0.0 collective-permute-done.refs_1_
  11.3 0.0 copy-done.3
  11.4 3.3 %bucket.1 = bf16[8,560,128]{2,1,0:T(8,128)(2,1)S(1)} custom-call(bf16[2048,128]{1,0:T(8,128)(2,1)S(1)} %bitcast.14, bf16[2048,128]{1,0:T(8,128)(2,1)S(1)} %collective-permute-done.refs_1_, s32[8,128]{1,0:T(8,128)S(1)} %pad_add_fusion.refs_2_, s32[8,128]{1,0:T(8,128)S(1)} %collective-permute-done.1.refs_3_), custom_call_target="tpu_custom_call" | custom-call | flops 100000000 | bytes 4194304 | tf_op jit(solution)/shard_map/bucket/pallas_call | solution.py:130
  14.6 0.1 fusion
  14.7 6.9 %collective-permute-start.9 = (bf16[1,560,128]{2,1,0:T(8,128)(2,1)S(1)}, bf16[1,560,128]{2,1,0:T(8,128)(2,1)S(1)}, u32[]{:S(2)}, u32[]{:S(2)}) collective-permute-start(bf16[1,560,128]{2,1,0:T(8,128)(2,1)S(1)} %get-tuple-element.19), channel_id=1, source_target_pairs={{0,24},{2,26},{4,28},{6,30},{8,16},{10,18},{12,20},{14,22},{16,8},... | collective-permute-start | bytes 430088 | tf_op jit(solution)/shard_map/ppermute | solution.py:418
  21.6 0.3 collective-permute-start.10
  21.9 0.7 collective-permute-start.4
  22.5 0.0 collective-permute-done.13.refs_4_.refs_7_
  22.5 2.1 %collective-permute-start.3 = (bf16[1,560,128]{2,1,0:T(8,128)(2,1)S(1)}, bf16[1,560,128]{2,1,0:T(8,128)(2,1)S(1)}, u32[]{:S(2)}, u32[]{:S(2)}) collective-permute-start(bf16[1,560,128]{2,1,0:T(8,128)(2,1)S(1)} %get-tuple-element.24), channel_id=1, source_target_pairs={{0,8},{2,10},{4,12},{6,14},{8,0},{10,2},{12,4},{14,6},{16,24},{18,... | collective-permute-start | bytes 430088 | tf_op jit(solution)/shard_map/ppermute | solution.py:418
  24.6 0.0 collective-permute-done.14.refs_5_.refs_8_
  24.6 0.7 %collective-permute-start.2 = (bf16[1,560,128]{2,1,0:T(8,128)(2,1)S(1)}, bf16[1,560,128]{2,1,0:T(8,128)(2,1)S(1)}, u32[]{:S(2)}, u32[]{:S(2)}) collective-permute-start(bf16[1,560,128]{2,1,0:T(8,128)(2,1)S(1)} %get-tuple-element.25), channel_id=1, source_target_pairs={{0,4},{2,6},{4,0},{6,2},{8,12},{10,14},{12,8},{14,10},{16,20},{18,... | collective-permute-start | bytes 430088 | tf_op jit(solution)/shard_map/ppermute | solution.py:418
  25.4 0.0 copy-done.1
  25.4 0.0 copy-done.5
  25.4 5.5 %front.2 = (bf16[1088,1024]{1,0:T(8,128)(2,1)S(1)}, bf16[1024,1024]{1,0:T(8,128)(2,1)S(1)}, f32[1088,1024]{1,0:T(8,128)S(1)}) custom-call(f32[8]{0:T(128)S(1)} %get-tuple-element.28.refs_0_, f32[8]{0:T(128)S(1)} %get-tuple-element.27.refs_1_, f32[32]{0:T(128)S(1)} %copy-done.5, f32[1024,1024]{1,0:T(8,128)S(1)} %bitcast.10, ...), custom_call_target="tpu_custom_call" | custom-call | flops 2281701376 | bytes 12582912 | tf_op jit(solution)/shard_map/front/pallas_call | solution.py:252
  30.8 1.0 %collective-permute-done.4.refs_3_ = bf16[1,560,128]{2,1,0:T(8,128)(2,1)S(1)} collective-permute-done((bf16[1,560,128]{2,1,0:T(8,128)(2,1)S(1)}, bf16[1,560,128]{2,1,0:T(8,128)(2,1)S(1)}, u32[]{:S(2)}, u32[]{:S(2)}) %collective-permute-start.4) | collective-permute-done | bytes 143392 | tf_op jit(solution)/shard_map/ppermute | solution.py:418
  31.8 3.2 %collective-permute-start.7 = (bf16[1,560,128]{2,1,0:T(8,128)(2,1)S(1)}, bf16[1,560,128]{2,1,0:T(8,128)(2,1)S(1)}, u32[]{:S(2)}, u32[]{:S(2)}) collective-permute-start(bf16[1,560,128]{2,1,0:T(8,128)(2,1)S(1)} %get-tuple-element.21), channel_id=1, source_target_pairs={{0,20},{2,22},{4,16},{6,18},{8,28},{10,30},{12,24},{14,26},{16,4},... | collective-permute-start | bytes 430088 | tf_op jit(solution)/shard_map/ppermute | solution.py:418
  35.1 0.0 collective-permute-done.3.refs_2_
  35.1 1.0 %collective-permute-start.6 = (bf16[1,560,128]{2,1,0:T(8,128)(2,1)S(1)}, bf16[1,560,128]{2,1,0:T(8,128)(2,1)S(1)}, u32[]{:S(2)}, u32[]{:S(2)}) collective-permute-start(bf16[1,560,128]{2,1,0:T(8,128)(2,1)S(1)} %get-tuple-element.22), channel_id=1, source_target_pairs={{0,16},{2,18},{4,20},{6,22},{8,24},{10,26},{12,28},{14,30},{16,0},... | collective-permute-start | bytes 430088 | tf_op jit(solution)/shard_map/ppermute | solution.py:418
  36.1 0.0 collective-permute-done.2.refs_1_
  36.1 0.1 pad_maximum_fusion
  36.1 0.6 collective-permute-start.5
  36.7 0.0 collective-permute-done.9.refs_6_
  36.7 0.0 collective-permute-done.10.refs_7_
  36.7 1.6 %collective-permute-start.11 = (bf16[2,560,128]{2,1,0:T(8,128)(2,1)S(1)}, bf16[2,560,128]{2,1,0:T(8,128)(2,1)S(1)}, u32[]{:S(2)}, u32[]{:S(2)}) collective-permute-start(bf16[2,560,128]{2,1,0:T(8,128)(2,1)S(1)} %pad_maximum_fusion.2), channel_id=1, source_target_pairs={{0,1},{1,0},{2,3},{3,2},{4,5},{5,4},{6,7},{7,6},{8,9},{9,8},{10,11... | collective-permute-start | bytes 860168 | tf_op jit(solution)/shard_map/ppermute | solution.py:413
  38.3 6.8 %collective-permute-done.7.refs_5_ = bf16[1,560,128]{2,1,0:T(8,128)(2,1)S(1)} collective-permute-done((bf16[1,560,128]{2,1,0:T(8,128)(2,1)S(1)}, bf16[1,560,128]{2,1,0:T(8,128)(2,1)S(1)}, u32[]{:S(2)}, u32[]{:S(2)}) %collective-permute-start.7) | collective-permute-done | bytes 143392 | tf_op jit(solution)/shard_map/ppermute | solution.py:418
  45.2 2.2 %collective-permute-done.6.refs_4_ = bf16[1,560,128]{2,1,0:T(8,128)(2,1)S(1)} collective-permute-done((bf16[1,560,128]{2,1,0:T(8,128)(2,1)S(1)}, bf16[1,560,128]{2,1,0:T(8,128)(2,1)S(1)}, u32[]{:S(2)}, u32[]{:S(2)}) %collective-permute-start.6) | collective-permute-done | bytes 143392 | tf_op jit(solution)/shard_map/ppermute | solution.py:418
  47.4 0.6 collective-permute-start.8
  48.0 4.5 %front.3 = (bf16[1024,1024]{1,0:T(8,128)(2,1)S(1)}, f32[1088,1024]{1,0:T(8,128)S(1)}) custom-call(f32[8]{0:T(128)S(1)} %get-tuple-element.30.refs_0_, f32[8]{0:T(128)S(1)} %get-tuple-element.29.refs_1_, bf16[1088,1024]{1,0:T(8,128)(2,1)S(1)} %get-tuple-element.14.refs_2_), custom_call_target="tpu_custom_call" | custom-call | flops 2281701376 | bytes 12582912 | tf_op jit(solution)/shard_map/front/pallas_call | solution.py:252
  52.5 0.0 copy-start.2
  52.5 5.1 %back.1.refs_5_ = f32[1088,1024]{1,0:T(8,128)S(1)} custom-call(bf16[1,560,128]{2,1,0:T(8,128)(2,1)S(1)} %get-tuple-element.26.refs_0_, bf16[1,560,128]{2,1,0:T(8,128)(2,1)S(1)} %collective-permute-done.2.refs_1_, bf16[1,560,128]{2,1,0:T(8,128)(2,1)S(1)} %collective-permute-done.3.refs_2_, bf16[1,560,128]{2,1,0:T(8,128)(2,1)S(1)} %collective-permute-done.4.refs_3_, ...), custom_call_target="tpu_custom_call" | custom-call | flops 2281701376 | bytes 12582912 | tf_op jit(solution)/shard_map/back/pallas_call | solution.py:394
  57.6 0.6 collective-permute-done.11.refs_2_
  58.3 4.2 %collective-permute-done.8.refs_1_ = bf16[2,560,128]{2,1,0:T(8,128)(2,1)S(1)} collective-permute-done((bf16[2,560,128]{2,1,0:T(8,128)(2,1)S(1)}, bf16[2,560,128]{2,1,0:T(8,128)(2,1)S(1)}, u32[]{:S(2)}, u32[]{:S(2)}) %collective-permute-start.8) | collective-permute-done | bytes 286752 | tf_op jit(solution)/shard_map/ppermute | solution.py:413
  62.5 0.0 collective-permute-done.5.refs_0_
  62.5 0.0 copy-done.2
  62.5 10.4 %update.1 = f32[1024,1024]{1,0:T(8,128)} custom-call(bf16[4,560,128]{2,1,0:T(8,128)(2,1)S(1)} %collective-permute-done.5.refs_0_, bf16[2,560,128]{2,1,0:T(8,128)(2,1)S(1)} %collective-permute-done.8.refs_1_, bf16[2,560,128]{2,1,0:T(8,128)(2,1)S(1)} %collective-permute-done.11.refs_2_, bf16[1024,1024]{1,0:T(8,128)(2,1)S(1)} %get-tuple-element.15.refs_3_, ...), custom_call_target="tpu_custom_call" | custom-call | flops 2281701376 | bytes 12582912 | tf_op jit(solution)/shard_map/update/pallas_call | solution.py:394
  (2 shorter events, 0.1 us)
Async XLA Ops:
  0.0 11.3 %collective-permute-start.12 = (s32[8]{0:T(128)}, s32[8]{0:T(128)S(1)}, u32[]{:S(2)}, u32[]{:S(2)}) collective-permute-start(s32[8]{0:T(128)} %bitcast.16), channel_id=1, source_target_pairs={{0,1},{1,0},{2,3},{3,2},{4,5},{5,4},{6,7},{7,6},{8,9},{9,8},{10,11... | collective-permute-start | bytes 104 | tf_op jit(solution)/shard_map/ppermute | solution.py:413
  3.0 8.4 %collective-permute-start = (bf16[2048,128]{1,0:T(8,128)(2,1)}, bf16[2048,128]{1,0:T(8,128)(2,1)S(1)}, u32[]{:S(2)}, u32[]{:S(2)}) collective-permute-start(bf16[2048,128]{1,0:T(8,128)(2,1)} %bitcast.13), channel_id=1, source_target_pairs={{0,2},{2,0},{4,6},{6,4},{8,10},{10,8},{12,14},{14,12},{16,18},{18,... | collective-permute-start | bytes 1572872 | tf_op jit(solution)/shard_map/ppermute | solution.py:418
  3.7 7.7 %collective-permute-start.1 = (s32[8,128]{1,0:T(8,128)S(1)}, s32[8,128]{1,0:T(8,128)S(1)}, u32[]{:S(2)}, u32[]{:S(2)}) collective-permute-start(s32[8,128]{1,0:T(8,128)S(1)} %pad_add_fusion.refs_2_), channel_id=1, source_target_pairs={{0,2},{2,0},{4,6},{6,4},{8,10},{10,8},{12,14},{14,12},{16,18},{18,... | collective-permute-start | bytes 12296 | tf_op jit(solution)/shard_map/ppermute | solution.py:418
  4.2 2.2 %copy-start = (f32[32,32,1024]{2,1,0:T(8,128)S(1)}, f32[32,32,1024]{2,1,0:T(8,128)}, u32[]{:S(2)}) copy-start(f32[32,32,1024]{2,1,0:T(8,128)} %param.8) | copy-start | bytes 12582916
  6.4 0.7 copy-start.4
  7.1 4.1 %copy-start.6 = (s32[1,8]{1,0:T(1,128)S(1)}, s32[1,8]{1,0:T(1,128)}, u32[]{:S(2)}) copy-start(s32[1,8]{1,0:T(1,128)} %param.15) | copy-start | bytes 100
  7.1 4.3 %copy-start.3 = (bf16[1,64,32,128]{3,2,1,0:T(8,128)(2,1)S(1)}, bf16[1,64,32,128]{3,2,1,0:T(8,128)(2,1)}, u32[]{:S(2)}) copy-start(bf16[1,64,32,128]{3,2,1,0:T(8,128)(2,1)} %param.11) | copy-start | bytes 1572868
  7.7 17.7 %copy-start.1 = (f32[32,32,1024]{2,1,0:T(8,128)S(1)}, f32[32,32,1024]{2,1,0:T(8,128)}, u32[]{:S(2)}) copy-start(f32[32,32,1024]{2,1,0:T(8,128)} %param.8) | copy-start | bytes 12582916
  7.7 17.7 %copy-start.5 = (f32[32]{0:T(128)S(1)}, f32[32]{0:T(128)}, u32[]{:S(2)}) copy-start(f32[32]{0:T(128)} %refs_6_.1) | copy-start | bytes 388
  7.7 14.8 %collective-permute-start.13 = (f32[72,1024]{1,0:T(8,128)S(1)}, f32[72,1024]{1,0:T(8,128)S(1)}, u32[]{:S(2)}, u32[]{:S(2)}) collective-permute-start(f32[72,1024]{1,0:T(8,128)S(1)} %get-tuple-element.12), channel_id=1, source_target_pairs={{0,2},{2,4},{4,6},{6,8},{8,10},{10,12},{12,14},{14,16},{16,18},{18... | collective-permute-start | bytes 884744 | tf_op jit(solution)/shard_map/ppermute | solution.py:439
  9.9 14.7 %collective-permute-start.14 = (f32[72,1024]{1,0:T(8,128)S(1)}, f32[72,1024]{1,0:T(8,128)S(1)}, u32[]{:S(2)}, u32[]{:S(2)}) collective-permute-start(f32[72,1024]{1,0:T(8,128)S(1)} %get-tuple-element.13), channel_id=1, source_target_pairs={{2,0},{4,2},{6,4},{8,6},{10,8},{12,10},{14,12},{16,14},{18,16},{20... | collective-permute-start | bytes 884744 | tf_op jit(solution)/shard_map/ppermute | solution.py:440
  14.7 22.0 %collective-permute-start.9 = (bf16[1,560,128]{2,1,0:T(8,128)(2,1)S(1)}, bf16[1,560,128]{2,1,0:T(8,128)(2,1)S(1)}, u32[]{:S(2)}, u32[]{:S(2)}) collective-permute-start(bf16[1,560,128]{2,1,0:T(8,128)(2,1)S(1)} %get-tuple-element.19), channel_id=1, source_target_pairs={{0,24},{2,26},{4,28},{6,30},{8,16},{10,18},{12,20},{14,22},{16,8},... | collective-permute-start | bytes 430088 | tf_op jit(solution)/shard_map/ppermute | solution.py:418
  21.6 15.1 %collective-permute-start.10 = (bf16[1,560,128]{2,1,0:T(8,128)(2,1)S(1)}, bf16[1,560,128]{2,1,0:T(8,128)(2,1)S(1)}, u32[]{:S(2)}, u32[]{:S(2)}) collective-permute-start(bf16[1,560,128]{2,1,0:T(8,128)(2,1)S(1)} %get-tuple-element.20), channel_id=1, source_target_pairs={{0,28},{2,30},{4,24},{6,26},{8,20},{10,22},{12,16},{14,18},{16,12}... | collective-permute-start | bytes 430088 | tf_op jit(solution)/shard_map/ppermute | solution.py:418
  21.9 10.0 %collective-permute-start.4 = (bf16[1,560,128]{2,1,0:T(8,128)(2,1)S(1)}, bf16[1,560,128]{2,1,0:T(8,128)(2,1)S(1)}, u32[]{:S(2)}, u32[]{:S(2)}) collective-permute-start(bf16[1,560,128]{2,1,0:T(8,128)(2,1)S(1)} %get-tuple-element.23), channel_id=1, source_target_pairs={{0,12},{2,14},{4,8},{6,10},{8,4},{10,6},{12,0},{14,2},{16,28},{18,... | collective-permute-start | bytes 430088 | tf_op jit(solution)/shard_map/ppermute | solution.py:418
  22.5 12.5 %collective-permute-start.3 = (bf16[1,560,128]{2,1,0:T(8,128)(2,1)S(1)}, bf16[1,560,128]{2,1,0:T(8,128)(2,1)S(1)}, u32[]{:S(2)}, u32[]{:S(2)}) collective-permute-start(bf16[1,560,128]{2,1,0:T(8,128)(2,1)S(1)} %get-tuple-element.24), channel_id=1, source_target_pairs={{0,8},{2,10},{4,12},{6,14},{8,0},{10,2},{12,4},{14,6},{16,24},{18,... | collective-permute-start | bytes 430088 | tf_op jit(solution)/shard_map/ppermute | solution.py:418
  24.6 11.4 %collective-permute-start.2 = (bf16[1,560,128]{2,1,0:T(8,128)(2,1)S(1)}, bf16[1,560,128]{2,1,0:T(8,128)(2,1)S(1)}, u32[]{:S(2)}, u32[]{:S(2)}) collective-permute-start(bf16[1,560,128]{2,1,0:T(8,128)(2,1)S(1)} %get-tuple-element.25), channel_id=1, source_target_pairs={{0,4},{2,6},{4,0},{6,2},{8,12},{10,14},{12,8},{14,10},{16,20},{18,... | collective-permute-start | bytes 430088 | tf_op jit(solution)/shard_map/ppermute | solution.py:418
  31.8 13.3 %collective-permute-start.7 = (bf16[1,560,128]{2,1,0:T(8,128)(2,1)S(1)}, bf16[1,560,128]{2,1,0:T(8,128)(2,1)S(1)}, u32[]{:S(2)}, u32[]{:S(2)}) collective-permute-start(bf16[1,560,128]{2,1,0:T(8,128)(2,1)S(1)} %get-tuple-element.21), channel_id=1, source_target_pairs={{0,20},{2,22},{4,16},{6,18},{8,28},{10,30},{12,24},{14,26},{16,4},... | collective-permute-start | bytes 430088 | tf_op jit(solution)/shard_map/ppermute | solution.py:418
  35.1 12.3 %collective-permute-start.6 = (bf16[1,560,128]{2,1,0:T(8,128)(2,1)S(1)}, bf16[1,560,128]{2,1,0:T(8,128)(2,1)S(1)}, u32[]{:S(2)}, u32[]{:S(2)}) collective-permute-start(bf16[1,560,128]{2,1,0:T(8,128)(2,1)S(1)} %get-tuple-element.22), channel_id=1, source_target_pairs={{0,16},{2,18},{4,20},{6,22},{8,24},{10,26},{12,28},{14,30},{16,0},... | collective-permute-start | bytes 430088 | tf_op jit(solution)/shard_map/ppermute | solution.py:418
  36.1 26.3 %collective-permute-start.5 = (bf16[4,560,128]{2,1,0:T(8,128)(2,1)S(1)}, bf16[4,560,128]{2,1,0:T(8,128)(2,1)S(1)}, u32[]{:S(2)}, u32[]{:S(2)}) collective-permute-start(bf16[4,560,128]{2,1,0:T(8,128)(2,1)S(1)} %pad_maximum_fusion), channel_id=1, source_target_pairs={{0,1},{1,0},{2,3},{3,2},{4,5},{5,4},{6,7},{7,6},{8,9},{9,8},{10,11... | collective-permute-start | bytes 1720328 | tf_op jit(solution)/shard_map/ppermute | solution.py:413
  36.7 21.5 %collective-permute-start.11 = (bf16[2,560,128]{2,1,0:T(8,128)(2,1)S(1)}, bf16[2,560,128]{2,1,0:T(8,128)(2,1)S(1)}, u32[]{:S(2)}, u32[]{:S(2)}) collective-permute-start(bf16[2,560,128]{2,1,0:T(8,128)(2,1)S(1)} %pad_maximum_fusion.2), channel_id=1, source_target_pairs={{0,1},{1,0},{2,3},{3,2},{4,5},{5,4},{6,7},{7,6},{8,9},{9,8},{10,11... | collective-permute-start | bytes 860168 | tf_op jit(solution)/shard_map/ppermute | solution.py:413
  47.4 15.1 %collective-permute-start.8 = (bf16[2,560,128]{2,1,0:T(8,128)(2,1)S(1)}, bf16[2,560,128]{2,1,0:T(8,128)(2,1)S(1)}, u32[]{:S(2)}, u32[]{:S(2)}) collective-permute-start(bf16[2,560,128]{2,1,0:T(8,128)(2,1)S(1)} %pad_maximum_fusion.1), channel_id=1, source_target_pairs={{0,1},{1,0},{2,3},{3,2},{4,5},{5,4},{6,7},{7,6},{8,9},{9,8},{10,11... | collective-permute-start | bytes 860168 | tf_op jit(solution)/shard_map/ppermute | solution.py:413
  52.5 10.0 %copy-start.2 = (f32[32,32,1024]{2,1,0:T(8,128)S(1)}, f32[32,32,1024]{2,1,0:T(8,128)}, u32[]{:S(2)}) copy-start(f32[32,32,1024]{2,1,0:T(8,128)} %param.9) | copy-start | bytes 12582916

commit v3 on v2

--- a/solution.py
+++ b/solution.py
@@ -20,9 +20,10 @@
 SMEM = pltpu.SMEM
 VMEM = pltpu.VMEM
 MIB = 1024 * 1024
+BLOCK = 512
 LIMIT_FRONT = 12
 LIMIT_BACK = 14
-LIMIT_UPDATE = 16
+LIMIT_UPDATE = 20
 
 
 def iota(shape, dim):
@@ -139,71 +140,140 @@
     )(*raws, *tables)
 
 
-def halo_kernel(width, first, final, low_out, high_out):
-    edge, length = first.shape
-    low_out[0:edge, :] = final[...]
-    low_out[edge : edge + 8, :] = jnp.full((8, length), width[width.shape[0] - 1], F32)
-    high_out[0:edge, :] = first[...]
-    high_out[edge : edge + 8, :] = jnp.full((8, length), width[0], F32)
-
-
-def halo(width, activity, lines):
-    rows, length = activity.shape
-    edge = 2 * lines
-    shape = jax.ShapeDtypeStruct((edge + 8, length), F32)
-    out = pl.BlockSpec((edge + 8, length), lambda i: (0, 0))
-    return pl.pallas_call(
-        halo_kernel,
-        out_shape=(shape, shape),
-        grid=(1,),
-        in_specs=[
-            SPEC_SMEM,
-            pl.BlockSpec((edge, length), lambda i: (0, 0)),
-            pl.BlockSpec((edge, length), lambda i: (rows // edge - 1, 0)),
-        ],
-        out_specs=(out, out),
+def relay_kernel(count, unread, *refs):
+    arrived, out = refs[:count], refs[count + unread]
+    for i, ref in enumerate(arrived):
+        out[i] = ref[0]
+
+
+def relay(arrived, passed, after):
+    count = len(arrived)
+    like = [jax.ShapeDtypeStruct(value.shape, value.dtype) for value in passed]
+    joined, *rest = pl.pallas_call(
+        functools.partial(relay_kernel, count, len(passed) + len(after)),
+        out_shape=[jax.ShapeDtypeStruct((count, *arrived[0].shape[1:]), BF16), *like],
+        in_specs=[SPEC_VMEM] * count + [SPEC_ANY] * (len(passed) + len(after)),
+        out_specs=[SPEC_VMEM] + [SPEC_ANY] * len(passed),
+        input_output_aliases={count + i: 1 + i for i in range(len(passed))},
         compiler_params=params(8),
         cost_estimate=cost(0, MIB),
-        name="halo",
-    )(width, activity, activity)
-
-
-def blur(lines, width, activity, low, high, blurred):
-    planes = activity.shape[0] // lines
-
-    def put(at, w, here, down, up):
-        value = (1.0 - 2.0 * w) * here + w * (down + up)
-        blurred[pl.ds(at, lines), :] = value.astype(BF16)
-
-    def plane(z):
-        return activity[z * lines : (z + 1) * lines, :]
-
-    near_low, near_high = low[lines : 2 * lines, :], high[0:lines, :]
-    wide_low = low[2 * lines : 2 * lines + 1, :]
-    wide_high = high[2 * lines : 2 * lines + 1, :]
-    put(0, wide_low, near_low, low[0:lines, :], plane(0))
-    put(lines, width[0], plane(0), near_low, plane(1))
-    put(planes * lines, width[planes - 1], plane(planes - 1), plane(planes - 2), near_high)
-    put((planes + 1) * lines, wide_high, near_high, plane(planes - 1), high[lines : 2 * lines, :])
+        name="relay",
+    )(*arrived, *passed, *after)
+    return joined, rest
+
+
+def behind_kernel(*refs):
+    del refs
+
+
+def behind(passed, after):
+    return pl.pallas_call(
+        behind_kernel,
+        out_shape=[jax.ShapeDtypeStruct(value.shape, value.dtype) for value in passed],
+        in_specs=[SPEC_ANY] * (len(passed) + 1),
+        out_specs=[SPEC_ANY] * len(passed),
+        input_output_aliases={i: i for i in range(len(passed))},
+        compiler_params=params(8),
+        cost_estimate=cost(0, 0),
+        name="behind",
+    )(*passed, after)
+
+
+def mix(w, here, down, up):
+    return ((1.0 - 2.0 * w) * here + w * (down + up)).astype(BF16)
+
+
+def blur_kernel(lines, width, activity, _, blurred, low_out, high_out):
+    rows, length = activity.shape
+    planes = rows // lines
+    edge = 2 * lines
+    low_out[0:edge, :] = activity[rows - edge :, :]
+    low_out[edge : edge + 8, :] = jnp.full((8, length), width[planes - 1], F32)
+    high_out[0:edge, :] = activity[0:edge, :]
+    high_out[edge : edge + 8, :] = jnp.full((8, length), width[0], F32)
 
     def inner(z, carry):
         start = pl.multiple_of(z * lines, lines)
         here = activity[pl.ds(start, lines), :]
         down = activity[pl.ds(pl.multiple_of(start - lines, lines), lines), :]
         up = activity[pl.ds(pl.multiple_of(start + lines, lines), lines), :]
-        put(pl.multiple_of(start + lines, lines), width[z], here, down, up)
+        at = pl.ds(pl.multiple_of(start - lines, lines), lines)
+        blurred[at, :] = mix(width[z], here, down, up)
         return carry
 
     lax.fori_loop(1, planes - 1, inner, 0)
 
 
-def front_kernel(lines, *refs):
-    if lines is not None:
-        spacing, offset, width, activity, low, high, blurred, k_out, r_out = refs
-        blur(lines, width, activity, low, high, blurred)
-    else:
-        spacing, offset, blurred, k_out, r_out = refs
-    extended, length = blurred.shape
+def blur(width, activity, after, lines):
+    rows, length = activity.shape
+    shape = jax.ShapeDtypeStruct((2 * lines + 8, length), F32)
+    return pl.pallas_call(
+        functools.partial(blur_kernel, lines),
+        out_shape=(jax.ShapeDtypeStruct((rows - 2 * lines, length), BF16), shape, shape),
+        in_specs=[SPEC_SMEM, SPEC_VMEM, SPEC_ANY],
+        out_specs=(SPEC_VMEM, SPEC_VMEM, SPEC_VMEM),
+        compiler_params=params(12),
+        cost_estimate=cost(0, 4 * MIB),
+        name="blur",
+    )(width, activity, after)
+
+
+def edge_kernel(lines, groups, after, width, low, high, activity, sensitivity, *refs):
+    kernels, refs = refs[:groups], refs[groups + after :]
+    edges, gain, blurred = refs[:groups], refs[groups], refs[groups + 1]
+    rows, length = activity.shape
+    planes = rows // lines
+    bins = 256
+
+    def plane(z):
+        return activity[z * lines : (z + 1) * lines, :]
+
+    near_low, near_high = low[lines : 2 * lines, :], high[0:lines, :]
+    wide_low = low[2 * lines : 2 * lines + 1, :]
+    wide_high = high[2 * lines : 2 * lines + 1, :]
+    final, before = plane(planes - 1), plane(planes - 2)
+    blurred[0:lines, :] = mix(wide_low, near_low, low[0:lines, :], plane(0))
+    blurred[lines : 2 * lines, :] = mix(width[0], plane(0), near_low, plane(1))
+    blurred[2 * lines : 3 * lines, :] = mix(width[planes - 1], final, before, near_high)
+    blurred[3 * lines : 4 * lines, :] = mix(wide_high, near_high, final, high[lines : 2 * lines, :])
+    for kernel, edge in zip(kernels, edges):
+
+        def project(i, carry, kernel=kernel, edge=edge):
+            columns = pl.ds(pl.multiple_of(i * bins, bins), bins)
+            estimate = matmul(blurred[...], kernel[columns, :], (1, 1))
+            edge[:, columns] = 1.0 / (estimate + BACKGROUND)
+            return carry
+
+        lax.fori_loop(0, kernel.shape[0] // bins, project, 0)
+
+    def divide(i, carry):
+        at = pl.ds(pl.multiple_of(i * lines, lines), lines)
+        gain[at, :] = activity[at, :] / sensitivity[at, :]
+        return carry
+
+    lax.fori_loop(0, planes, divide, 0)
+
+
+def edge(width, low, high, activity, sensitivity, kernels, after, lines):
+    rows, length = activity.shape
+    groups = len(kernels)
+    shape = jax.ShapeDtypeStruct((4 * lines, kernels[0].shape[0]), F32)
+    *edges, gain = pl.pallas_call(
+        functools.partial(edge_kernel, lines, groups, len(after)),
+        out_shape=[shape] * groups + [jax.ShapeDtypeStruct((rows, length), F32)],
+        in_specs=[SPEC_SMEM] + [SPEC_VMEM] * (4 + groups) + [SPEC_ANY] * len(after),
+        out_specs=[SPEC_VMEM] * (groups + 1),
+        scratch_shapes=[VMEM((4 * lines, length), BF16)],
+        compiler_params=params(LIMIT_BACK),
+        cost_estimate=cost(groups * 2 * 4 * lines * length * 1024, 12 * MIB),
+        name="edge",
+    )(width, low, high, activity, sensitivity, *kernels, *after)
+    return edges, gain
+
+
+def front_kernel(after, spacing, offset, blurred, *refs):
+    k_out, r_out = refs[after:]
+    length = blurred.shape[1]
     angles = spacing.shape[0]
     bins = k_out.shape[0] // angles
     step_width = length / bins
@@ -211,7 +281,7 @@
     scale = 1.0 / (deviation * math.sqrt(2.0 * math.pi))
     sharp = -math.log2(math.e) / (2.0 * deviation * deviation)
     some = 32
-    pair = 2
+    pair = 4
     voxel = iota((1, length), 1).astype(F32) + 0.5 - length / 2
     bin_at = iota((some, 1), 0).astype(F32) + 0.5 - bins / 2
 
@@ -231,33 +301,22 @@
     lax.fori_loop(0, angles // pair, group, 0)
 
 
-def front(spacing, offset, blurred, bins, planes_in=None):
+def front(spacing, offset, blurred, bins, after=()):
     (angles,) = spacing.shape
     wide = angles * bins
-    lines = None
-    if planes_in is None:
-        extended, length = blurred.shape
-        operands, specs = [blurred], [SPEC_VMEM]
-    else:
-        *operands, lines = planes_in
-        rows, length = operands[1].shape
-        extended = rows + 2 * lines
-        specs = [SPEC_SMEM] + [SPEC_VMEM] * 3
-    shapes = [
-        jax.ShapeDtypeStruct((wide, length), BF16),
-        jax.ShapeDtypeStruct((extended, wide), F32),
-    ]
-    if planes_in is not None:
-        shapes.insert(0, jax.ShapeDtypeStruct((extended, length), BF16))
+    rows, length = blurred.shape
     return pl.pallas_call(
-        functools.partial(front_kernel, lines),
-        out_shape=shapes,
-        in_specs=[SPEC_SMEM, SPEC_SMEM] + specs,
-        out_specs=[SPEC_VMEM] * len(shapes),
+        functools.partial(front_kernel, len(after)),
+        out_shape=(
+            jax.ShapeDtypeStruct((wide, length), BF16),
+            jax.ShapeDtypeStruct((rows, wide), F32),
+        ),
+        in_specs=[SPEC_SMEM, SPEC_SMEM, SPEC_VMEM] + [SPEC_ANY] * len(after),
+        out_specs=(SPEC_VMEM, SPEC_VMEM),
         compiler_params=params(LIMIT_FRONT),
-        cost_estimate=cost(2 * extended * length * wide, 12 * MIB),
+        cost_estimate=cost(2 * rows * length * wide, 8 * MIB),
         name="front",
-    )(spacing, offset, *operands)
+    )(spacing, offset, blurred, *after)
 
 
 def back_kernel(counts, has_prior, last, lines, *refs):
@@ -269,17 +328,17 @@
         return taken
 
     received = take(len(counts))
-    k_buf, r_buf = take(2)
+    k_buf, r_buf, edge_buf = take(3)
     (prior,) = take(1) if has_prior else (None,)
     if last:
-        width, low, high, activity, sensitivity = take(5)
+        width, low, high, gain = take(4)
     (out,) = take(1)
     (rounded,) = take(1)
     if last:
         total, updated, sems = take(3)
     sources = [(ref, s) for ref, count in zip(received, counts) for s in range(count)]
     bins = received[0].shape[-1]
-    extended, wide = r_buf.shape
+    extended, wide = rounded.shape
     length = k_buf.shape[1]
     angles = wide // bins
     planes = extended // lines - 2
@@ -302,26 +361,31 @@
         codes = jnp.concatenate(parts, axis=1).astype(I32)
         named.append(one_hot(codes - 1 == iota((angles * lines, codes.shape[1]), 0)))
 
-    def sums(kind, at, start):
+    def sums(kind, at, start, inverse, first):
         held = [ref[s, pl.ds(at, PAIR), :] for ref, s in sources]
         spare = -len(held) % group * PAIR
         if spare:
             held.append(jnp.zeros((spare, bins), BF16))
         sums = matmul(named[kind], jnp.concatenate(held))
         for a in range(angles):
-            place = (pl.ds(start, lines), pl.ds(a * bins, bins))
-            rounded[place] = (sums[a * lines : (a + 1) * lines, :] * r_buf[place]).astype(BF16)
-
-    sums(1, body, 0)
-    sums(2, body + PAIR, extended - lines)
+            columns = pl.ds(a * bins, bins)
+            ratio = sums[a * lines : (a + 1) * lines, :] * inverse[pl.ds(first, lines), columns]
+            rounded[pl.ds(start, lines), columns] = ratio.astype(BF16)
+
+    sums(1, body, 0, edge_buf, 0)
+    sums(0, 0, lines, edge_buf, lines)
+    sums(0, body - PAIR, extended - 2 * lines, edge_buf, 2 * lines)
+    sums(2, body + PAIR, extended - lines, edge_buf, 3 * lines)
 
     def inner(z, carry):
-        sums(0, pl.multiple_of(z * PAIR, PAIR), pl.multiple_of((z + 1) * lines, lines))
+        start = pl.multiple_of(z * lines, lines)
+        first = pl.multiple_of(start - lines, lines)
+        sums(0, pl.multiple_of(z * PAIR, PAIR), start + lines, r_buf, first)
         return carry
 
-    lax.fori_loop(0, planes, inner, 0, unroll=4)
-
-    block = 256
+    lax.fori_loop(1, planes - 1, inner, 0, unroll=5)
+
+    block = total.shape[2] if last else 512
     steps = length // block
 
     def project(columns):
@@ -342,39 +406,36 @@
         columns = pl.ds(i * block, block)
         return pltpu.make_async_copy(updated.at[i % 2], out.at[:, columns], sems.at[i % 2])
 
-    for i in range(steps):
-        columns = pl.ds(i * block, block)
-        total[...] = project(columns)
-        if i >= 2:
-            write(i - 2).wait()
-
-        def smooth(z, w_down, w_up, i=i, columns=columns):
+    def smooth(i):
+        held, columns = total.at[i % 2], pl.ds(i * block, block)
+        for z in range(planes):
+            edge_low = low[2 * lines : 2 * lines + 1, 0:block] if z == 0 else width[z - 1]
+            edge_high = high[2 * lines : 2 * lines + 1, 0:block] if z == planes - 1 else width[z + 1]
             start = z * lines
-            w = width[z]
-            down = total[pl.ds(start, lines), :]
-            here = total[pl.ds(start + lines, lines), :]
-            up = total[pl.ds(start + 2 * lines, lines), :]
-            smoothed = (1.0 - 2.0 * w) * here + w_down * down + w_up * up
+            down = held[start : start + lines, :]
+            here = held[start + lines : start + 2 * lines, :]
+            up = held[start + 2 * lines : start + 3 * lines, :]
+            value = (1.0 - 2.0 * width[z]) * here + edge_low * down + edge_high * up
             at = pl.ds(start, lines)
-            value = activity[at, columns] * smoothed / sensitivity[at, columns]
-            updated[i % 2, at, :] = value
-
-        def inside(z, carry, smooth=smooth):
-            smooth(z, width[z - 1], width[z + 1])
-            return carry
-
-        smooth(0, low[2 * lines : 2 * lines + 1, 0:block], width[1])
-        lax.fori_loop(1, planes - 1, inside, 0, unroll=10)
-        smooth(planes - 1, width[planes - 2], high[2 * lines : 2 * lines + 1, 0:block])
-        write(i).start()
+            updated[i % 2, at, :] = value * gain[at, columns]
+
+    for i in range(steps + 1):
+        if i >= 3:
+            write(i - 3).wait()
+        if i < steps:
+            total[i % 2] = project(pl.ds(i * block, block))
+        if i:
+            smooth(i - 1)
+            write(i - 1).start()
     for i in range(max(0, steps - 2), steps):
         write(i).wait()
 
 
-def back(pieces, k, r, prior, final, lines):
-    extended, wide = r.shape
+def back(pieces, k, r, edges, prior, final, lines):
+    rows, wide = r.shape
+    extended = rows + 4 * lines
     _, length = k.shape
-    operands = [*pieces, k, r]
+    operands = [*pieces, k, r, edges]
     specs = [SPEC_VMEM] * len(operands)
     if prior is not None:
         operands.append(prior)
@@ -384,10 +445,10 @@
     if final is not None:
         rows = extended - 2 * lines
         operands += final
-        specs += [SPEC_SMEM] + [SPEC_VMEM] * 4
+        specs += [SPEC_SMEM] + [SPEC_VMEM] * 3
         scratch += [
-            VMEM((extended, 256), F32),
-            VMEM((2, rows, 256), F32),
+            VMEM((2, extended, BLOCK), F32),
+            VMEM((2, rows, BLOCK), F32),
             pltpu.SemaphoreType.DMA((2,)),
         ]
         shape = (rows, length)
@@ -435,19 +496,32 @@
     raws, tables = [raw, flip(raw, 1)], [table, flip(table, 1)]
     ups = [(i, i + 1) for i in range(slabs - 1)]
     downs = [(j, i) for i, j in ups]
-    low_mine, high_mine = halo(psf_width, flat, lines)
-    low = lax.ppermute(low_mine, "slab", ups)
-    high = lax.ppermute(high_mine, "slab", downs)
     chips = slabs // 2
+    step_width = length / bins
+
+    def forward(view, blurred, behind=()):
+        angle = math.pi * view.astype(F32) / VIEWS_ALL
+        spacing = step_width * (0.75 + 0.25 * jnp.cos(2.0 * angle))
+        offset = 1.5 * step_width * jnp.sin(angle)
+        return front(spacing, offset, blurred, bins, behind)
+
     if slabs == 16 and view_count == 2:
+        other = swap(subset_views[0])
         send = bucket(raws, tables, chips, True, planes, lines)
-        far = [flip(send[j : j + 1], 2 * j) for j in range(4, 8)]
+        blurred, *mine = blur(psf_width, flat, send, lines)
         near = [send[0:1]] + [flip(send[j : j + 1], 2 * j) for j in range(1, 4)]
-        over = [swap(jnp.concatenate(part)) for part in (near, far[:2], far[2:])]
-        pieces = [near + far, over]
-        views = [subset_views[0], swap(subset_views[0])]
+        far = [flip(send[j : j + 1], 2 * j) for j in (4, 5)]
+        fronts = [forward(subset_views[0], blurred)]
+        joined, passed = relay(near, [send[6:7], send[7:8], *mine], [fronts[0][0]])
+        far += [flip(passed[0], 12), flip(passed[1], 14)]
+        mine = passed[2:]
+        over = [swap(joined)] + [swap(jnp.concatenate(part)) for part in (far[:2], far[2:])]
+        pieces = [[joined, *far], over]
+        fronts.append(forward(other, blurred, [joined]))
+        behind_edge = [over[0]]
     else:
         send = bucket(raws, tables, chips, False, planes, lines)
+        blurred, *mine = blur(psf_width, flat, send, lines)
         cores = [[2 * chip + core for chip in range(chips)] for core in range(2)]
         own = lax.all_to_all(
             send, "slab", split_axis=0, concat_axis=0, axis_index_groups=cores, tiled=True
@@ -455,27 +529,21 @@
         everyone = lax.all_gather(own, "view")
         pieces = [[everyone[g]] for g in range(view_count)]
         gathered = lax.all_gather(subset_views[0], "view")
-        views = [gathered[g] for g in range(view_count)]
-
-    step_width = length / bins
-    fronts = []
-    for view in views:
-        angle = math.pi * view.astype(F32) / VIEWS_ALL
-        spacing = step_width * (0.75 + 0.25 * jnp.cos(2.0 * angle))
-        offset = 1.5 * step_width * jnp.sin(angle)
-        if not fronts:
-            planes_in = (psf_width, flat, low, high, lines)
-            blurred, *made = front(spacing, offset, None, bins, planes_in)
-        else:
-            made = front(spacing, offset, blurred, bins)
-        fronts.append(made)
+        fronts = [forward(gathered[g], blurred) for g in range(view_count)]
+        behind_edge = []
+
+    low = lax.ppermute(mine[0], "slab", ups)
+    high = lax.ppermute(mine[1], "slab", downs)
+    kernels, inverses = zip(*fronts)
+    whole = sensitivity.reshape(planes * lines, length)
+    edges, gain = edge(psf_width, low, high, flat, whole, kernels, behind_edge, lines)
 
     result = None
     for g in range(view_count):
         final = None
         if g == view_count - 1:
-            final = [psf_width, low, high, flat, sensitivity.reshape(planes * lines, length)]
-        result = back(pieces[g], *fronts[g], result, final, lines)
+            final = [psf_width, low, high, gain]
+        result = back(pieces[g], kernels[g], inverses[g], edges[g], result, final, lines)
     return result.reshape(planes, lines, length)
 
 

time: 73.1 us -> 61.8 us (0.85)
  waiting for transfers between devices: 14.9 us -> 9.65 us
  starting transfers between devices: 24.6 us -> 21.3 us
  local copies, waits for them, and re-layouts: 2.95 us -> 1.13 us
  Pallas kernels: 29.4 us -> 27.6 us
  other arithmetic: 0.94 us -> 1.78 us
    pallas_call x2, Pallas kernels: 15.5 us -> 11.2 us  [back(): pl.pallas_call(functools.partial(back_kernel, [piece.shape[0] for piece i...]
    ppermute x4, waiting for transfers between devices: 4.85 us -> 1.22 us  [swap(): return lax.ppermute(value, 'view', [(0, 1), (1, 0)])]
    ppermute x9, starting transfers between devices: 15.4 us -> 12.7 us  [flip(): return lax.ppermute(value, 'slab', [(i, i ^ mask) for i in range(size)])]
    pallas_call x3 -> x5, Pallas kernels: 10.6 us -> 13.1 us  [the longest x2 7.64 us: front(): pl.pallas_call(functools.partial(front_kernel, len(after)), out_shape=(ja...]
    unnamed x14 -> x8, local copies, waits for them, and re-layouts: 2.87 us -> 1.05 us
    ppermute x9, waiting for transfers between devices: 10.1 us -> 8.43 us  [flip(): return lax.ppermute(value, 'slab', [(i, i ^ mask) for i in range(size)])]
    ppermute x2, starting transfers between devices: 3.49 us -> 2.59 us  [the longest x1 1.31 us: on_device(): low = lax.ppermute(mine[0], 'slab', ups)]
  transfers between devices with their start and end apart: 15 -> 15, of which waited for: 5 -> 3; matrix products, arithmetic and copies ran while one was open for 1% -> 3% of each run, Pallas kernels for 26% -> 34%
where the time goes in v3:
time: 61.8 us; the launch traced here: 61.6 us
  Pallas kernels  27.6 us (45%)
  starting transfers between devices  21.3 us (34%)
  waiting for transfers between devices  9.65 us (16%)
  other arithmetic  1.78 us (3%)
  local copies, waits for them, and re-layouts  1.13 us (2%)
    ppermute x9, starting transfers between devices, flip(): return lax.ppermute(value, 'slab', [(i, i ^ mask) for i in range(size)])  12.7 us
    pallas_call x2, Pallas kernels, back(): pl.pallas_call(functools.partial(back_kernel, [piece.shape[0] for piece i...  11.2 us
    ppermute x9, waiting for transfers between devices, flip(): return lax.ppermute(value, 'slab', [(i, i ^ mask) for i in range(size)])  8.43 us
    pallas_call x2, Pallas kernels, front(): pl.pallas_call(functools.partial(front_kernel, len(after)), out_shape=(ja...  7.64 us
    ppermute x4, starting transfers between devices, swap(): return lax.ppermute(value, 'view', [(0, 1), (1, 0)])  5.94 us
    pallas_call x1, Pallas kernels, edge(): pl.pallas_call(functools.partial(edge_kernel, lines, groups, len(after)),...  4.01 us
    pallas_call x1, Pallas kernels, bucket(): pl.pallas_call(functools.partial(bucket_kernel, chips, relative, planes,...  3.26 us
    pallas_call x1, Pallas kernels, blur(): pl.pallas_call(functools.partial(blur_kernel, lines), out_shape=(jax.Shap...  1.4 us
  transfers between devices with their start and end apart: 15, of which 3 were waited for; matrix products, arithmetic and copies ran while one was open for 3% of the time, Pallas kernels for 34%

profile of v3, /device:TPU:0, one launch (start us, length us, event | category | flops | bytes accessed | tf_op | source)
XLA Modules:
  0.0 61.6 jit_solution(14442193906573835054)
XLA Ops:
  0.0 0.0 copy-start
  0.0 0.5 collective-permute-start
  0.5 0.9 %pad_add_fusion.refs_2_ = s32[8,128]{1,0:T(8,128)S(1)} fusion(s32[1,64]{1,0:T(1,128)} %param.14, s32[1,64]{1,0:T(1,128)} %param.13, s32[1,64]{1,0:T(1,128)} %bitcast.13), kind=kLoop, calls=%fused_computation.2 | loop fusion | flops 2048 | bytes 4864 | tf_op jit(solution)/shard_map/add | solution.py:495
  1.4 0.1 collective-permute-start.1
  1.4 3.1 %collective-permute-start.12 = (s32[8]{0:T(128)}, s32[8]{0:T(128)S(1)}, u32[]{:S(2)}, u32[]{:S(2)}) collective-permute-start(s32[8]{0:T(128)} %bitcast.14), channel_id=1, source_target_pairs={{0,1},{1,0},{2,3},{3,2},{4,5},{5,4},{6,7},{7,6},{8,9},{9,8},{10,11... | collective-permute-start | bytes 104 | tf_op jit(solution)/shard_map/ppermute | solution.py:474
  4.6 0.7 %sine_multiply_fusion.1 = (f32[8]{0:T(128)S(1)}, f32[8]{0:T(128)S(1)}) fusion(s32[1,8]{1,0:T(1,128)} %param.15), kind=kLoop, calls=%fused_computation.5 | loop fusion | flops 56 | bytes 96 | tf_op jit(solution)/shard_map/mul | solution.py:505
  5.3 0.0 collective-permute-done.1.refs_3_
  5.3 0.0 collective-permute-done.refs_1_
  5.3 0.0 copy-start.2
  5.3 1.0 %copy-done.2 = bf16[1,64,32,128]{3,2,1,0:T(8,128)(2,1)S(1)} copy-done((bf16[1,64,32,128]{3,2,1,0:T(8,128)(2,1)S(1)}, bf16[1,64,32,128]{3,2,1,0:T(8,128)(2,1)}, u32[]{:S(2)}) %copy-start.2) | copy-done | bytes 524312
  6.4 0.0 copy-start.3
  6.4 3.3 %bucket.1._ = bf16[8,560,128]{2,1,0:T(8,128)(2,1)S(1)} custom-call(bf16[2048,128]{1,0:T(8,128)(2,1)S(1)} %bitcast.12, bf16[2048,128]{1,0:T(8,128)(2,1)S(1)} %collective-permute-done.refs_1_, s32[8,128]{1,0:T(8,128)S(1)} %pad_add_fusion.refs_2_, s32[8,128]{1,0:T(8,128)S(1)} %collective-permute-done.1.refs_3_), custom_call_target="tpu_custom_call" | custom-call | flops 100000000 | bytes 4194304 | tf_op jit(solution)/shard_map/bucket/pallas_call | solution.py:131
  9.6 0.1 fusion
  9.7 1.6 %collective-permute-start.2 = (bf16[1,560,128]{2,1,0:T(8,128)(2,1)S(1)}, bf16[1,560,128]{2,1,0:T(8,128)(2,1)S(1)}, u32[]{:S(2)}, u32[]{:S(2)}) collective-permute-start(bf16[1,560,128]{2,1,0:T(8,128)(2,1)S(1)} %get-tuple-element.41), channel_id=1, source_target_pairs={{0,4},{2,6},{4,0},{6,2},{8,12},{10,14},{12,8},{14,10},{16,20},{18,... | collective-permute-start | bytes 430088 | tf_op jit(solution)/shard_map/ppermute | solution.py:479
  11.3 1.6 %collective-permute-start.3 = (bf16[1,560,128]{2,1,0:T(8,128)(2,1)S(1)}, bf16[1,560,128]{2,1,0:T(8,128)(2,1)S(1)}, u32[]{:S(2)}, u32[]{:S(2)}) collective-permute-start(bf16[1,560,128]{2,1,0:T(8,128)(2,1)S(1)} %get-tuple-element.40), channel_id=1, source_target_pairs={{0,8},{2,10},{4,12},{6,14},{8,0},{10,2},{12,4},{14,6},{16,24},{18,... | collective-permute-start | bytes 430088 | tf_op jit(solution)/shard_map/ppermute | solution.py:479
  12.9 0.4 collective-permute-start.4
  13.3 2.6 %collective-permute-start.6 = (bf16[1,560,128]{2,1,0:T(8,128)(2,1)S(1)}, bf16[1,560,128]{2,1,0:T(8,128)(2,1)S(1)}, u32[]{:S(2)}, u32[]{:S(2)}) collective-permute-start(bf16[1,560,128]{2,1,0:T(8,128)(2,1)S(1)} %get-tuple-element.35), channel_id=1, source_target_pairs={{0,16},{2,18},{4,20},{6,22},{8,24},{10,26},{12,28},{14,30},{16,0},... | collective-permute-start | bytes 430088 | tf_op jit(solution)/shard_map/ppermute | solution.py:479
  15.9 0.0 copy-done
  15.9 0.0 copy-done.3
  15.9 1.4 %blur.1 = (bf16[960,1024]{1,0:T(8,128)(2,1)S(1)}, f32[72,1024]{1,0:T(8,128)S(1)}, f32[72,1024]{1,0:T(8,128)S(1)}) custom-call(f32[32]{0:T(128)S(1)} %copy-done.3, f32[1024,1024]{1,0:T(8,128)S(1)} %bitcast.8, bf16[8,560,128]{2,1,0:T(8,128)(2,1)S(1)} %bucket.1._), custom_call_target="tpu_custom_call" | custom-call | bytes 4194304 | tf_op jit(solution)/shard_map/blur/pallas_call | solution.py:210
  17.3 3.8 %front.2 = (bf16[1024,1024]{1,0:T(8,128)(2,1)S(1)}, f32[960,1024]{1,0:T(8,128)S(1)}) custom-call(f32[8]{0:T(128)S(1)} %get-tuple-element.46.spacing, f32[8]{0:T(128)S(1)} %get-tuple-element.45.offset, bf16[960,1024]{1,0:T(8,128)(2,1)S(1)} %get-tuple-element.22.blurred), custom_call_target="tpu_custom_call" | custom-call | flops 2013265920 | bytes 8388608 | tf_op jit(solution)/shard_map/front/pallas_call | solution.py:308
  21.1 0.0 collective-permute-done.2.refs_1_
  21.1 1.3 %collective-permute-start.7 = (bf16[1,560,128]{2,1,0:T(8,128)(2,1)S(1)}, bf16[1,560,128]{2,1,0:T(8,128)(2,1)S(1)}, u32[]{:S(2)}, u32[]{:S(2)}) collective-permute-start(bf16[1,560,128]{2,1,0:T(8,128)(2,1)S(1)} %get-tuple-element.36), channel_id=1, source_target_pairs={{0,20},{2,22},{4,16},{6,18},{8,28},{10,30},{12,24},{14,26},{16,4},... | collective-permute-start | bytes 430088 | tf_op jit(solution)/shard_map/ppermute | solution.py:479
  22.5 0.0 collective-permute-done.3.refs_2_
  22.5 0.1 collective-permute-done.4.refs_3_
  22.6 0.7 %collective-permute-start.5 = (bf16[4,560,128]{2,1,0:T(8,128)(2,1)S(1)}, bf16[4,560,128]{2,1,0:T(8,128)(2,1)S(1)}, u32[]{:S(2)}, u32[]{:S(2)}) collective-permute-start(bf16[4,560,128]{2,1,0:T(8,128)(2,1)S(1)} %get-tuple-element.24.refs_0_), channel_id=1, source_target_pairs={{0,1},{1,0},{2,3},{3,2},{4,5},{5,4},{6,7},{7,6},{8,9},{9,8},{10,11... | collective-permute-start | bytes 1720328 | tf_op jit(solution)/shard_map/ppermute | solution.py:474
  23.3 4.6 %collective-permute-start.10 = (bf16[1,560,128]{2,1,0:T(8,128)(2,1)S(1)}, bf16[1,560,128]{2,1,0:T(8,128)(2,1)S(1)}, u32[]{:S(2)}, u32[]{:S(2)}) collective-permute-start(bf16[1,560,128]{2,1,0:T(8,128)(2,1)S(1)} %get-tuple-element.26), channel_id=1, source_target_pairs={{0,28},{2,30},{4,24},{6,26},{8,20},{10,22},{12,16},{14,18},{16,12}... | collective-permute-start | bytes 430088 | tf_op jit(solution)/shard_map/ppermute | solution.py:479
  27.9 0.0 collective-permute-done.12
  27.9 0.2 collective-permute-start.9
  28.1 0.1 sine_multiply_fusion
  28.1 0.0 collective-permute-done.6.refs_1_
  28.1 1.3 %collective-permute-start.13 = (f32[72,1024]{1,0:T(8,128)S(1)}, f32[72,1024]{1,0:T(8,128)S(1)}, u32[]{:S(2)}, u32[]{:S(2)}) collective-permute-start(f32[72,1024]{1,0:T(8,128)S(1)} %get-tuple-element.29), channel_id=1, source_target_pairs={{0,2},{2,4},{4,6},{6,8},{8,10},{10,12},{12,14},{14,16},{16,18},{18... | collective-permute-start | bytes 884744 | tf_op jit(solution)/shard_map/ppermute | solution.py:535
  29.4 8.3 %collective-permute-done.7.refs_2_ = bf16[1,560,128]{2,1,0:T(8,128)(2,1)S(1)} collective-permute-done((bf16[1,560,128]{2,1,0:T(8,128)(2,1)S(1)}, bf16[1,560,128]{2,1,0:T(8,128)(2,1)S(1)}, u32[]{:S(2)}, u32[]{:S(2)}) %collective-permute-start.7) | collective-permute-done | bytes 143392 | tf_op jit(solution)/shard_map/ppermute | solution.py:479
  37.7 1.3 %collective-permute-start.14 = (f32[72,1024]{1,0:T(8,128)S(1)}, f32[72,1024]{1,0:T(8,128)S(1)}, u32[]{:S(2)}, u32[]{:S(2)}) collective-permute-start(f32[72,1024]{1,0:T(8,128)S(1)} %get-tuple-element.30), channel_id=1, source_target_pairs={{2,0},{4,2},{6,4},{8,6},{10,8},{12,10},{14,12},{16,14},{18,16},{20... | collective-permute-start | bytes 884744 | tf_op jit(solution)/shard_map/ppermute | solution.py:536
  39.1 0.0 copy-start.1
  39.1 0.0 collective-permute-done.10.refs_4_
  39.1 0.7 %collective-permute-start.8 = (bf16[2,560,128]{2,1,0:T(8,128)(2,1)S(1)}, bf16[2,560,128]{2,1,0:T(8,128)(2,1)S(1)}, u32[]{:S(2)}, u32[]{:S(2)}) collective-permute-start(bf16[2,560,128]{2,1,0:T(8,128)(2,1)S(1)} %pad_maximum_fusion), channel_id=1, source_target_pairs={{0,1},{1,0},{2,3},{3,2},{4,5},{5,4},{6,7},{7,6},{8,9},{9,8},{10,11... | collective-permute-start | bytes 860168 | tf_op jit(solution)/shard_map/ppermute | solution.py:474
  39.8 0.0 collective-permute-done.9.refs_3_
  39.8 1.5 %collective-permute-start.11 = (bf16[2,560,128]{2,1,0:T(8,128)(2,1)S(1)}, bf16[2,560,128]{2,1,0:T(8,128)(2,1)S(1)}, u32[]{:S(2)}, u32[]{:S(2)}) collective-permute-start(bf16[2,560,128]{2,1,0:T(8,128)(2,1)S(1)} %pad_maximum_fusion.1), channel_id=1, source_target_pairs={{0,1},{1,0},{2,3},{3,2},{4,5},{5,4},{6,7},{7,6},{8,9},{9,8},{10,11... | collective-permute-start | bytes 860168 | tf_op jit(solution)/shard_map/ppermute | solution.py:474
  41.3 3.8 %front.3 = (bf16[1024,1024]{1,0:T(8,128)(2,1)S(1)}, f32[960,1024]{1,0:T(8,128)S(1)}) custom-call(f32[8]{0:T(128)S(1)} %get-tuple-element.44.spacing, f32[8]{0:T(128)S(1)} %get-tuple-element.43.offset, bf16[960,1024]{1,0:T(8,128)(2,1)S(1)} %get-tuple-element.22.blurred, bf16[4,560,128]{2,1,0:T(8,128)(2,1)S(1)} %get-tuple-element.24.refs_0_), custom_call_target="tpu_custom_call" | custom-call | flops 2013265920 | bytes 8388608 | tf_op jit(solution)/shard_map/front/pallas_call | solution.py:308
  45.1 0.0 collective-permute-done.13.low.refs_8_
  45.1 0.0 collective-permute-done.14.high.refs_9_
  45.1 0.0 collective-permute-done.5.refs_2_.refs_0_
  45.1 0.0 copy-done.1
  45.1 4.0 %edge.1 = (f32[128,1024]{1,0:T(8,128)S(1)}, f32[128,1024]{1,0:T(8,128)S(1)}, f32[1024,1024]{1,0:T(8,128)S(1)}) custom-call(f32[32]{0:T(128)S(1)} %copy-done.3, f32[72,1024]{1,0:T(8,128)S(1)} %collective-permute-done.13.low.refs_8_, f32[72,1024]{1,0:T(8,128)S(1)} %collective-permute-done.14.high.refs_9_, f32[1024,1024]{1,0:T(8,128)S(1)} %bitcast.9, ...), custom_call_target="tpu_custom_call" | custom-call | flops 536870912 | bytes 12582912 | tf_op jit(solution)/shard_map/edge/pallas_call | solution.py:261
  49.2 4.4 %back.1.refs_6_ = f32[1088,1024]{1,0:T(8,128)S(1)} custom-call(bf16[4,560,128]{2,1,0:T(8,128)(2,1)S(1)} %get-tuple-element.24.refs_0_, bf16[1,560,128]{2,1,0:T(8,128)(2,1)S(1)} %collective-permute-done.6.refs_1_, bf16[1,560,128]{2,1,0:T(8,128)(2,1)S(1)} %collective-permute-done.7.refs_2_, bf16[1,560,128]{2,1,0:T(8,128)(2,1)S(1)} %collective-permute-done.9.refs_3_, ...), custom_call_target="tpu_custom_call" | custom-call | flops 2281701376 | bytes 12582912 | tf_op jit(solution)/shard_map/back/pallas_call | solution.py:455
  53.6 0.0 collective-permute-done.8.refs_1_
  53.6 1.2 %collective-permute-done.11.refs_2_ = bf16[2,560,128]{2,1,0:T(8,128)(2,1)S(1)} collective-permute-done((bf16[2,560,128]{2,1,0:T(8,128)(2,1)S(1)}, bf16[2,560,128]{2,1,0:T(8,128)(2,1)S(1)}, u32[]{:S(2)}, u32[]{:S(2)}) %collective-permute-start.11) | collective-permute-done | bytes 286752 | tf_op jit(solution)/shard_map/ppermute | solution.py:474
  54.8 6.8 %update.1 = f32[1024,1024]{1,0:T(8,128)} custom-call(bf16[4,560,128]{2,1,0:T(8,128)(2,1)S(1)} %collective-permute-done.5.refs_2_.refs_0_, bf16[2,560,128]{2,1,0:T(8,128)(2,1)S(1)} %collective-permute-done.8.refs_1_, bf16[2,560,128]{2,1,0:T(8,128)(2,1)S(1)} %collective-permute-done.11.refs_2_, bf16[1024,1024]{1,0:T(8,128)(2,1)S(1)} %get-tuple-element.27.refs_1_.refs_3_, ...), custom_call_target="tpu_custom_call" | custom-call | flops 2281701376 | bytes 12582912 | tf_op jit(solution)/shard_map/update/pallas_call | solution.py:455
  (3 shorter events, 0.1 us)
Async XLA Ops:
  0.0 15.9 %copy-start = (f32[32,32,1024]{2,1,0:T(8,128)S(1)}, f32[32,32,1024]{2,1,0:T(8,128)}, u32[]{:S(2)}) copy-start(f32[32,32,1024]{2,1,0:T(8,128)} %param.8) | copy-start | bytes 12582916
  0.0 5.3 %collective-permute-start = (bf16[2048,128]{1,0:T(8,128)(2,1)}, bf16[2048,128]{1,0:T(8,128)(2,1)S(1)}, u32[]{:S(2)}, u32[]{:S(2)}) collective-permute-start(bf16[2048,128]{1,0:T(8,128)(2,1)} %bitcast.11), channel_id=1, source_target_pairs={{0,2},{2,0},{4,6},{6,4},{8,10},{10,8},{12,14},{14,12},{16,18},{18,... | collective-permute-start | bytes 1572872 | tf_op jit(solution)/shard_map/ppermute | solution.py:479
  1.4 3.9 %collective-permute-start.1 = (s32[8,128]{1,0:T(8,128)S(1)}, s32[8,128]{1,0:T(8,128)S(1)}, u32[]{:S(2)}, u32[]{:S(2)}) collective-permute-start(s32[8,128]{1,0:T(8,128)S(1)} %pad_add_fusion.refs_2_), channel_id=1, source_target_pairs={{0,2},{2,0},{4,6},{6,4},{8,10},{10,8},{12,14},{14,12},{16,18},{18,... | collective-permute-start | bytes 12296 | tf_op jit(solution)/shard_map/ppermute | solution.py:479
  1.4 26.5 %collective-permute-start.12 = (s32[8]{0:T(128)}, s32[8]{0:T(128)S(1)}, u32[]{:S(2)}, u32[]{:S(2)}) collective-permute-start(s32[8]{0:T(128)} %bitcast.14), channel_id=1, source_target_pairs={{0,1},{1,0},{2,3},{3,2},{4,5},{5,4},{6,7},{7,6},{8,9},{9,8},{10,11... | collective-permute-start | bytes 104 | tf_op jit(solution)/shard_map/ppermute | solution.py:474
  5.3 1.0 %copy-start.2 = (bf16[1,64,32,128]{3,2,1,0:T(8,128)(2,1)S(1)}, bf16[1,64,32,128]{3,2,1,0:T(8,128)(2,1)}, u32[]{:S(2)}) copy-start(bf16[1,64,32,128]{3,2,1,0:T(8,128)(2,1)} %param.11) | copy-start | bytes 1572868
  6.4 9.5 %copy-start.3 = (f32[32]{0:T(128)S(1)}, f32[32]{0:T(128)}, u32[]{:S(2)}) copy-start(f32[32]{0:T(128)} %refs_7_.1) | copy-start | bytes 388
  9.7 11.4 %collective-permute-start.2 = (bf16[1,560,128]{2,1,0:T(8,128)(2,1)S(1)}, bf16[1,560,128]{2,1,0:T(8,128)(2,1)S(1)}, u32[]{:S(2)}, u32[]{:S(2)}) collective-permute-start(bf16[1,560,128]{2,1,0:T(8,128)(2,1)S(1)} %get-tuple-element.41), channel_id=1, source_target_pairs={{0,4},{2,6},{4,0},{6,2},{8,12},{10,14},{12,8},{14,10},{16,20},{18,... | collective-permute-start | bytes 430088 | tf_op jit(solution)/shard_map/ppermute | solution.py:479
  11.3 11.2 %collective-permute-start.3 = (bf16[1,560,128]{2,1,0:T(8,128)(2,1)S(1)}, bf16[1,560,128]{2,1,0:T(8,128)(2,1)S(1)}, u32[]{:S(2)}, u32[]{:S(2)}) collective-permute-start(bf16[1,560,128]{2,1,0:T(8,128)(2,1)S(1)} %get-tuple-element.40), channel_id=1, source_target_pairs={{0,8},{2,10},{4,12},{6,14},{8,0},{10,2},{12,4},{14,6},{16,24},{18,... | collective-permute-start | bytes 430088 | tf_op jit(solution)/shard_map/ppermute | solution.py:479
  12.9 9.7 %collective-permute-start.4 = (bf16[1,560,128]{2,1,0:T(8,128)(2,1)S(1)}, bf16[1,560,128]{2,1,0:T(8,128)(2,1)S(1)}, u32[]{:S(2)}, u32[]{:S(2)}) collective-permute-start(bf16[1,560,128]{2,1,0:T(8,128)(2,1)S(1)} %get-tuple-element.39), channel_id=1, source_target_pairs={{0,12},{2,14},{4,8},{6,10},{8,4},{10,6},{12,0},{14,2},{16,28},{18,... | collective-permute-start | bytes 430088 | tf_op jit(solution)/shard_map/ppermute | solution.py:479
  13.3 14.8 %collective-permute-start.6 = (bf16[1,560,128]{2,1,0:T(8,128)(2,1)S(1)}, bf16[1,560,128]{2,1,0:T(8,128)(2,1)S(1)}, u32[]{:S(2)}, u32[]{:S(2)}) collective-permute-start(bf16[1,560,128]{2,1,0:T(8,128)(2,1)S(1)} %get-tuple-element.35), channel_id=1, source_target_pairs={{0,16},{2,18},{4,20},{6,22},{8,24},{10,26},{12,28},{14,30},{16,0},... | collective-permute-start | bytes 430088 | tf_op jit(solution)/shard_map/ppermute | solution.py:479
  21.1 16.6 %collective-permute-start.7 = (bf16[1,560,128]{2,1,0:T(8,128)(2,1)S(1)}, bf16[1,560,128]{2,1,0:T(8,128)(2,1)S(1)}, u32[]{:S(2)}, u32[]{:S(2)}) collective-permute-start(bf16[1,560,128]{2,1,0:T(8,128)(2,1)S(1)} %get-tuple-element.36), channel_id=1, source_target_pairs={{0,20},{2,22},{4,16},{6,18},{8,28},{10,30},{12,24},{14,26},{16,4},... | collective-permute-start | bytes 430088 | tf_op jit(solution)/shard_map/ppermute | solution.py:479
  22.6 22.5 %collective-permute-start.5 = (bf16[4,560,128]{2,1,0:T(8,128)(2,1)S(1)}, bf16[4,560,128]{2,1,0:T(8,128)(2,1)S(1)}, u32[]{:S(2)}, u32[]{:S(2)}) collective-permute-start(bf16[4,560,128]{2,1,0:T(8,128)(2,1)S(1)} %get-tuple-element.24.refs_0_), channel_id=1, source_target_pairs={{0,1},{1,0},{2,3},{3,2},{4,5},{5,4},{6,7},{7,6},{8,9},{9,8},{10,11... | collective-permute-start | bytes 1720328 | tf_op jit(solution)/shard_map/ppermute | solution.py:474
  23.3 15.8 %collective-permute-start.10 = (bf16[1,560,128]{2,1,0:T(8,128)(2,1)S(1)}, bf16[1,560,128]{2,1,0:T(8,128)(2,1)S(1)}, u32[]{:S(2)}, u32[]{:S(2)}) collective-permute-start(bf16[1,560,128]{2,1,0:T(8,128)(2,1)S(1)} %get-tuple-element.26), channel_id=1, source_target_pairs={{0,28},{2,30},{4,24},{6,26},{8,20},{10,22},{12,16},{14,18},{16,12}... | collective-permute-start | bytes 430088 | tf_op jit(solution)/shard_map/ppermute | solution.py:479
  27.9 11.9 %collective-permute-start.9 = (bf16[1,560,128]{2,1,0:T(8,128)(2,1)S(1)}, bf16[1,560,128]{2,1,0:T(8,128)(2,1)S(1)}, u32[]{:S(2)}, u32[]{:S(2)}) collective-permute-start(bf16[1,560,128]{2,1,0:T(8,128)(2,1)S(1)} %get-tuple-element.25), channel_id=1, source_target_pairs={{0,24},{2,26},{4,28},{6,30},{8,16},{10,18},{12,20},{14,22},{16,8},... | collective-permute-start | bytes 430088 | tf_op jit(solution)/shard_map/ppermute | solution.py:479
  28.1 17.0 %collective-permute-start.13 = (f32[72,1024]{1,0:T(8,128)S(1)}, f32[72,1024]{1,0:T(8,128)S(1)}, u32[]{:S(2)}, u32[]{:S(2)}) collective-permute-start(f32[72,1024]{1,0:T(8,128)S(1)} %get-tuple-element.29), channel_id=1, source_target_pairs={{0,2},{2,4},{4,6},{6,8},{8,10},{10,12},{12,14},{14,16},{16,18},{18... | collective-permute-start | bytes 884744 | tf_op jit(solution)/shard_map/ppermute | solution.py:535
  37.7 7.4 %collective-permute-start.14 = (f32[72,1024]{1,0:T(8,128)S(1)}, f32[72,1024]{1,0:T(8,128)S(1)}, u32[]{:S(2)}, u32[]{:S(2)}) collective-permute-start(f32[72,1024]{1,0:T(8,128)S(1)} %get-tuple-element.30), channel_id=1, source_target_pairs={{2,0},{4,2},{6,4},{8,6},{10,8},{12,10},{14,12},{16,14},{18,16},{20... | collective-permute-start | bytes 884744 | tf_op jit(solution)/shard_map/ppermute | solution.py:536
  39.1 6.1 %copy-start.1 = (f32[32,32,1024]{2,1,0:T(8,128)S(1)}, f32[32,32,1024]{2,1,0:T(8,128)}, u32[]{:S(2)}) copy-start(f32[32,32,1024]{2,1,0:T(8,128)} %param.9) | copy-start | bytes 12582916
  39.1 14.5 %collective-permute-start.8 = (bf16[2,560,128]{2,1,0:T(8,128)(2,1)S(1)}, bf16[2,560,128]{2,1,0:T(8,128)(2,1)S(1)}, u32[]{:S(2)}, u32[]{:S(2)}) collective-permute-start(bf16[2,560,128]{2,1,0:T(8,128)(2,1)S(1)} %pad_maximum_fusion), channel_id=1, source_target_pairs={{0,1},{1,0},{2,3},{3,2},{4,5},{5,4},{6,7},{7,6},{8,9},{9,8},{10,11... | collective-permute-start | bytes 860168 | tf_op jit(solution)/shard_map/ppermute | solution.py:474
  39.8 15.0 %collective-permute-start.11 = (bf16[2,560,128]{2,1,0:T(8,128)(2,1)S(1)}, bf16[2,560,128]{2,1,0:T(8,128)(2,1)S(1)}, u32[]{:S(2)}, u32[]{:S(2)}) collective-permute-start(bf16[2,560,128]{2,1,0:T(8,128)(2,1)S(1)} %pad_maximum_fusion.1), channel_id=1, source_target_pairs={{0,1},{1,0},{2,3},{3,2},{4,5},{5,4},{6,7},{7,6},{8,9},{9,8},{10,11... | collective-permute-start | bytes 860168 | tf_op jit(solution)/shard_map/ppermute | solution.py:474

commit v4 on v3

--- a/solution.py
+++ b/solution.py
@@ -40,7 +40,8 @@
 
 
 def cost(flops, moved):
-    return pl.CostEstimate(flops=flops, bytes_accessed=moved, transcendentals=0)
+    del flops, moved
+    return pl.CostEstimate(flops=0, bytes_accessed=0, transcendentals=0)
 
 
 SPEC_SMEM = pl.BlockSpec(memory_space=SMEM)
@@ -183,7 +184,8 @@
     return ((1.0 - 2.0 * w) * here + w * (down + up)).astype(BF16)
 
 
-def blur_kernel(lines, width, activity, _, blurred, low_out, high_out):
+def blur_kernel(lines, width, activity, *refs):
+    blurred, low_out, high_out = refs[-3:]
     rows, length = activity.shape
     planes = rows // lines
     edge = 2 * lines
@@ -210,12 +212,12 @@
     return pl.pallas_call(
         functools.partial(blur_kernel, lines),
         out_shape=(jax.ShapeDtypeStruct((rows - 2 * lines, length), BF16), shape, shape),
-        in_specs=[SPEC_SMEM, SPEC_VMEM, SPEC_ANY],
+        in_specs=[SPEC_SMEM, SPEC_VMEM] + [SPEC_ANY] * len(after),
         out_specs=(SPEC_VMEM, SPEC_VMEM, SPEC_VMEM),
         compiler_params=params(12),
         cost_estimate=cost(0, 4 * MIB),
         name="blur",
-    )(width, activity, after)
+    )(width, activity, *after)
 
 
 def edge_kernel(lines, groups, after, width, low, high, activity, sensitivity, *refs):
@@ -506,22 +508,22 @@
         return front(spacing, offset, blurred, bins, behind)
 
     if slabs == 16 and view_count == 2:
-        other = swap(subset_views[0])
+        other = swap(subset_views)
         send = bucket(raws, tables, chips, True, planes, lines)
-        blurred, *mine = blur(psf_width, flat, send, lines)
+        blurred, *mine = blur(psf_width, flat, [send, other], lines)
         near = [send[0:1]] + [flip(send[j : j + 1], 2 * j) for j in range(1, 4)]
         far = [flip(send[j : j + 1], 2 * j) for j in (4, 5)]
         fronts = [forward(subset_views[0], blurred)]
-        joined, passed = relay(near, [send[6:7], send[7:8], *mine], [fronts[0][0]])
+        joined, passed = relay(near, [send[6:7], send[7:8]], [fronts[0][0]])
         far += [flip(passed[0], 12), flip(passed[1], 14)]
-        mine = passed[2:]
         over = [swap(joined)] + [swap(jnp.concatenate(part)) for part in (far[:2], far[2:])]
         pieces = [[joined, *far], over]
-        fronts.append(forward(other, blurred, [joined]))
+        fronts.append(forward(other[0], blurred, [joined]))
+        mine = behind(mine, fronts[1][0])
         behind_edge = [over[0]]
     else:
         send = bucket(raws, tables, chips, False, planes, lines)
-        blurred, *mine = blur(psf_width, flat, send, lines)
+        blurred, *mine = blur(psf_width, flat, [send], lines)
         cores = [[2 * chip + core for chip in range(chips)] for core in range(2)]
         own = lax.all_to_all(
             send, "slab", split_axis=0, concat_axis=0, axis_index_groups=cores, tiled=True

time: 61.8 us -> 60.5 us (0.979); the launches traced: 61.6 us -> 59.6 us
  waiting for transfers between devices: 9.65 us -> 6.43 us
  starting transfers between devices: 21.3 us -> 23.2 us
  other arithmetic: 1.78 us -> 1.09 us
    ppermute x9, waiting for transfers between devices: 8.43 us -> 1.39 us  [flip(): return lax.ppermute(value, 'slab', [(i, i ^ mask) for i in range(size)])]
    ppermute x4, waiting for transfers between devices: 1.22 us -> 5.04 us  [swap(): return lax.ppermute(value, 'view', [(0, 1), (1, 0)])]
    ppermute x4, starting transfers between devices: 5.94 us -> 7.14 us  [swap(): return lax.ppermute(value, 'view', [(0, 1), (1, 0)])]
    ppermute x9, starting transfers between devices: 12.7 us -> 13.4 us  [flip(): return lax.ppermute(value, 'slab', [(i, i ^ mask) for i in range(size)])]
    mul x2, other arithmetic: 0.79 us -> 0.11 us  [forward(): offset = 1.5 * step_width * jnp.sin(angle)]
  transfers between devices with their start and end apart: 15 -> 15, of which waited for: 3 -> 3; matrix products, arithmetic and copies ran while one was open for 3% -> 2% of each run, Pallas kernels for 34% -> 35%
where the time goes in v4:
time: 60.5 us; the launch traced here: 59.6 us
  Pallas kernels  27.6 us (46%)
  starting transfers between devices  23.2 us (38%)
  waiting for transfers between devices  6.43 us (11%)
  local copies, waits for them, and re-layouts  1.14 us (2%)
  other arithmetic  1.09 us (2%)
    ppermute x9, starting transfers between devices, flip(): return lax.ppermute(value, 'slab', [(i, i ^ mask) for i in range(size)])  13.4 us
    pallas_call x2, Pallas kernels, back(): pl.pallas_call(functools.partial(back_kernel, [piece.shape[0] for piece i...  11.2 us
    pallas_call x2, Pallas kernels, front(): pl.pallas_call(functools.partial(front_kernel, len(after)), out_shape=(ja...  7.64 us
    ppermute x4, starting transfers between devices, swap(): return lax.ppermute(value, 'view', [(0, 1), (1, 0)])  7.14 us
    ppermute x4, waiting for transfers between devices, swap(): return lax.ppermute(value, 'view', [(0, 1), (1, 0)])  5.04 us
    pallas_call x1, Pallas kernels, edge(): pl.pallas_call(functools.partial(edge_kernel, lines, groups, len(after)),...  4.01 us
    pallas_call x1, Pallas kernels, bucket(): pl.pallas_call(functools.partial(bucket_kernel, chips, relative, planes,...  3.26 us
    pallas_call x1, Pallas kernels, blur(): pl.pallas_call(functools.partial(blur_kernel, lines), out_shape=(jax.Shap...  1.4 us
  transfers between devices with their start and end apart: 15, of which 3 were waited for; matrix products, arithmetic and copies ran while one was open for 2% of the time, Pallas kernels for 35%

profile of v4, /device:TPU:0, one launch (start us, length us, event | category | flops | bytes accessed | tf_op | source)
XLA Modules:
  0.0 59.6 jit_solution(8330844884174632684)
XLA Ops:
  0.0 0.0 copy-start
  0.0 0.5 collective-permute-start
  0.5 0.9 %pad_add_fusion.refs_2_ = s32[8,128]{1,0:T(8,128)S(1)} fusion(s32[1,64]{1,0:T(1,128)} %param.14, s32[1,64]{1,0:T(1,128)} %param.13, s32[1,64]{1,0:T(1,128)} %bitcast.18), kind=kLoop, calls=%fused_computation.2 | loop fusion | flops 2048 | bytes 4864 | tf_op jit(solution)/shard_map/add | solution.py:497
  1.4 0.1 collective-permute-start.1
  1.4 3.1 %collective-permute-start.5 = (s32[1,8]{1,0:T(1,128)}, s32[1,8]{1,0:T(1,128)S(1)}, u32[]{:S(2)}, u32[]{:S(2)}) collective-permute-start(s32[1,8]{1,0:T(1,128)} %param.15), channel_id=1, source_target_pairs={{0,1},{1,0},{2,3},{3,2},{4,5},{5,4},{6,7},{7,6},{8,9},{9,8},{10,11... | collective-permute-start | bytes 104 | tf_op jit(solution)/shard_map/ppermute | solution.py:476
  4.6 0.0 collective-permute-done.1.refs_3_
  4.6 0.0 collective-permute-done.refs_1_
  4.6 0.0 copy-start.2
  4.6 1.0 %copy-done.2 = bf16[1,64,32,128]{3,2,1,0:T(8,128)(2,1)S(1)} copy-done((bf16[1,64,32,128]{3,2,1,0:T(8,128)(2,1)S(1)}, bf16[1,64,32,128]{3,2,1,0:T(8,128)(2,1)}, u32[]{:S(2)}) %copy-start.2) | copy-done | bytes 524312
  5.6 0.0 copy-start.4
  5.6 0.0 copy-start.3
  5.6 3.3 %bucket.1.refs_0_ = bf16[8,560,128]{2,1,0:T(8,128)(2,1)S(1)} custom-call(bf16[2048,128]{1,0:T(8,128)(2,1)S(1)} %bitcast.17, bf16[2048,128]{1,0:T(8,128)(2,1)S(1)} %collective-permute-done.refs_1_, s32[8,128]{1,0:T(8,128)S(1)} %pad_add_fusion.refs_2_, s32[8,128]{1,0:T(8,128)S(1)} %collective-permute-done.1.refs_3_), custom_call_target="tpu_custom_call" | custom-call | tf_op jit(solution)/shard_map/bucket/pallas_call | solution.py:132
  8.9 0.1 fusion
  9.0 1.6 %collective-permute-start.2 = (bf16[1,560,128]{2,1,0:T(8,128)(2,1)S(1)}, bf16[1,560,128]{2,1,0:T(8,128)(2,1)S(1)}, u32[]{:S(2)}, u32[]{:S(2)}) collective-permute-start(bf16[1,560,128]{2,1,0:T(8,128)(2,1)S(1)} %get-tuple-element.41), channel_id=1, source_target_pairs={{0,4},{2,6},{4,0},{6,2},{8,12},{10,14},{12,8},{14,10},{16,20},{18,... | collective-permute-start | bytes 430088 | tf_op jit(solution)/shard_map/ppermute | solution.py:481
  10.5 1.6 %collective-permute-start.3 = (bf16[1,560,128]{2,1,0:T(8,128)(2,1)S(1)}, bf16[1,560,128]{2,1,0:T(8,128)(2,1)S(1)}, u32[]{:S(2)}, u32[]{:S(2)}) collective-permute-start(bf16[1,560,128]{2,1,0:T(8,128)(2,1)S(1)} %get-tuple-element.40), channel_id=1, source_target_pairs={{0,8},{2,10},{4,12},{6,14},{8,0},{10,2},{12,4},{14,6},{16,24},{18,... | collective-permute-start | bytes 430088 | tf_op jit(solution)/shard_map/ppermute | solution.py:481
  12.1 0.4 collective-permute-start.4
  12.5 0.0 copy-done.4
  12.5 0.1 multiply_bitcast_fusion.3
  12.6 2.7 %collective-permute-start.7 = (bf16[1,560,128]{2,1,0:T(8,128)(2,1)S(1)}, bf16[1,560,128]{2,1,0:T(8,128)(2,1)S(1)}, u32[]{:S(2)}, u32[]{:S(2)}) collective-permute-start(bf16[1,560,128]{2,1,0:T(8,128)(2,1)S(1)} %get-tuple-element.35), channel_id=1, source_target_pairs={{0,16},{2,18},{4,20},{6,22},{8,24},{10,26},{12,28},{14,30},{16,0},... | collective-permute-start | bytes 430088 | tf_op jit(solution)/shard_map/ppermute | solution.py:481
  15.2 0.0 collective-permute-done.5.refs_1_
  15.2 1.3 %collective-permute-start.8 = (bf16[1,560,128]{2,1,0:T(8,128)(2,1)S(1)}, bf16[1,560,128]{2,1,0:T(8,128)(2,1)S(1)}, u32[]{:S(2)}, u32[]{:S(2)}) collective-permute-start(bf16[1,560,128]{2,1,0:T(8,128)(2,1)S(1)} %get-tuple-element.36), channel_id=1, source_target_pairs={{0,20},{2,22},{4,16},{6,18},{8,28},{10,30},{12,24},{14,26},{16,4},... | collective-permute-start | bytes 430088 | tf_op jit(solution)/shard_map/ppermute | solution.py:481
  16.5 0.0 copy-done
  16.5 0.0 copy-done.3
  16.5 1.4 %blur.1 = (bf16[960,1024]{1,0:T(8,128)(2,1)S(1)}, f32[72,1024]{1,0:T(8,128)S(1)}, f32[72,1024]{1,0:T(8,128)S(1)}) custom-call(f32[32]{0:T(128)S(1)} %copy-done.3, f32[1024,1024]{1,0:T(8,128)S(1)} %bitcast.13, bf16[8,560,128]{2,1,0:T(8,128)(2,1)S(1)} %bucket.1.refs_0_, s32[1,8]{1,0:T(1,128)S(1)} %collective-permute-done.5.refs_1_), custom_call_target="tpu_custom_call" | custom-call | tf_op jit(solution)/shard_map/blur/pallas_call | solution.py:212
  17.9 3.8 %front.2 = (bf16[1024,1024]{1,0:T(8,128)(2,1)S(1)}, f32[960,1024]{1,0:T(8,128)S(1)}) custom-call(f32[8]{0:T(128)S(1)} %get-tuple-element.46.spacing, f32[8]{0:T(128)S(1)} %get-tuple-element.45.offset, bf16[960,1024]{1,0:T(8,128)(2,1)S(1)} %get-tuple-element.20.blurred), custom_call_target="tpu_custom_call" | custom-call | tf_op jit(solution)/shard_map/front/pallas_call | solution.py:310
  21.8 0.0 collective-permute-done.2.refs_1_
  21.8 0.8 %collective-permute-done.3.refs_2_ = bf16[1,560,128]{2,1,0:T(8,128)(2,1)S(1)} collective-permute-done((bf16[1,560,128]{2,1,0:T(8,128)(2,1)S(1)}, bf16[1,560,128]{2,1,0:T(8,128)(2,1)S(1)}, u32[]{:S(2)}, u32[]{:S(2)}) %collective-permute-start.3) | collective-permute-done | bytes 143392 | tf_op jit(solution)/shard_map/ppermute | solution.py:481
  22.6 0.6 collective-permute-done.4.refs_3_
  23.2 0.0 copy-start.1
  23.2 1.9 %collective-permute-start.6 = (bf16[4,560,128]{2,1,0:T(8,128)(2,1)S(1)}, bf16[4,560,128]{2,1,0:T(8,128)(2,1)S(1)}, u32[]{:S(2)}, u32[]{:S(2)}) collective-permute-start(bf16[4,560,128]{2,1,0:T(8,128)(2,1)S(1)} %get-tuple-element.22.refs_0_), channel_id=1, source_target_pairs={{0,1},{1,0},{2,3},{3,2},{4,5},{5,4},{6,7},{7,6},{8,9},{9,8},{10,11... | collective-permute-start | bytes 1720328 | tf_op jit(solution)/shard_map/ppermute | solution.py:476
  25.1 1.3 %collective-permute-start.10 = (bf16[1,560,128]{2,1,0:T(8,128)(2,1)S(1)}, bf16[1,560,128]{2,1,0:T(8,128)(2,1)S(1)}, u32[]{:S(2)}, u32[]{:S(2)}) collective-permute-start(bf16[1,560,128]{2,1,0:T(8,128)(2,1)S(1)} %get-tuple-element.23), channel_id=1, source_target_pairs={{0,24},{2,26},{4,28},{6,30},{8,16},{10,18},{12,20},{14,22},{16,8},... | collective-permute-start | bytes 430088 | tf_op jit(solution)/shard_map/ppermute | solution.py:481
  26.4 4.1 %collective-permute-start.11 = (bf16[1,560,128]{2,1,0:T(8,128)(2,1)S(1)}, bf16[1,560,128]{2,1,0:T(8,128)(2,1)S(1)}, u32[]{:S(2)}, u32[]{:S(2)}) collective-permute-start(bf16[1,560,128]{2,1,0:T(8,128)(2,1)S(1)} %get-tuple-element.24), channel_id=1, source_target_pairs={{0,28},{2,30},{4,24},{6,26},{8,20},{10,22},{12,16},{14,18},{16,12}... | collective-permute-start | bytes 430088 | tf_op jit(solution)/shard_map/ppermute | solution.py:481
  30.5 0.1 multiply_bitcast_fusion.2
  30.6 3.8 %front.3 = (bf16[1024,1024]{1,0:T(8,128)(2,1)S(1)}, f32[960,1024]{1,0:T(8,128)S(1)}) custom-call(f32[8]{0:T(128)S(1)} %get-tuple-element.44.spacing, f32[8]{0:T(128)S(1)} %get-tuple-element.43.offset, bf16[960,1024]{1,0:T(8,128)(2,1)S(1)} %get-tuple-element.20.blurred, bf16[4,560,128]{2,1,0:T(8,128)(2,1)S(1)} %get-tuple-element.22.refs_0_), custom_call_target="tpu_custom_call" | custom-call | tf_op jit(solution)/shard_map/front/pallas_call | solution.py:310
  34.4 0.0 collective-permute-done.7.refs_1_
  34.4 1.3 %collective-permute-start.13 = (f32[72,1024]{1,0:T(8,128)S(1)}, f32[72,1024]{1,0:T(8,128)S(1)}, u32[]{:S(2)}, u32[]{:S(2)}) collective-permute-start(f32[72,1024]{1,0:T(8,128)S(1)} %get-tuple-element.29), channel_id=1, source_target_pairs={{0,2},{2,4},{4,6},{6,8},{8,10},{10,12},{12,14},{14,16},{16,18},{18... | collective-permute-start | bytes 884744 | tf_op jit(solution)/shard_map/ppermute | solution.py:537
  35.7 0.0 collective-permute-done.8.refs_2_
  35.7 1.3 %collective-permute-start.14 = (f32[72,1024]{1,0:T(8,128)S(1)}, f32[72,1024]{1,0:T(8,128)S(1)}, u32[]{:S(2)}, u32[]{:S(2)}) collective-permute-start(f32[72,1024]{1,0:T(8,128)S(1)} %get-tuple-element.30), channel_id=1, source_target_pairs={{2,0},{4,2},{6,4},{8,6},{10,8},{12,10},{14,12},{16,14},{18,16},{20... | collective-permute-start | bytes 884744 | tf_op jit(solution)/shard_map/ppermute | solution.py:538
  37.1 0.0 collective-permute-done.10.refs_3_
  37.1 1.1 %collective-permute-start.9 = (bf16[2,560,128]{2,1,0:T(8,128)(2,1)S(1)}, bf16[2,560,128]{2,1,0:T(8,128)(2,1)S(1)}, u32[]{:S(2)}, u32[]{:S(2)}) collective-permute-start(bf16[2,560,128]{2,1,0:T(8,128)(2,1)S(1)} %pad_maximum_fusion), channel_id=1, source_target_pairs={{0,1},{1,0},{2,3},{3,2},{4,5},{5,4},{6,7},{7,6},{8,9},{9,8},{10,11... | collective-permute-start | bytes 860168 | tf_op jit(solution)/shard_map/ppermute | solution.py:476
  38.2 0.0 collective-permute-done.11.refs_4_
  38.2 1.0 %collective-permute-start.12 = (bf16[2,560,128]{2,1,0:T(8,128)(2,1)S(1)}, bf16[2,560,128]{2,1,0:T(8,128)(2,1)S(1)}, u32[]{:S(2)}, u32[]{:S(2)}) collective-permute-start(bf16[2,560,128]{2,1,0:T(8,128)(2,1)S(1)} %pad_maximum_fusion.1), channel_id=1, source_target_pairs={{0,1},{1,0},{2,3},{3,2},{4,5},{5,4},{6,7},{7,6},{8,9},{9,8},{10,11... | collective-permute-start | bytes 860168 | tf_op jit(solution)/shard_map/ppermute | solution.py:476
  39.3 0.0 collective-permute-done.13.low.refs_8_
  39.3 0.0 collective-permute-done.14.high.refs_9_
  39.3 0.0 collective-permute-done.6.refs_2_.refs_0_
  39.3 0.0 copy-done.1
  39.3 4.0 %edge.1 = (f32[128,1024]{1,0:T(8,128)S(1)}, f32[128,1024]{1,0:T(8,128)S(1)}, f32[1024,1024]{1,0:T(8,128)S(1)}) custom-call(f32[32]{0:T(128)S(1)} %copy-done.3, f32[72,1024]{1,0:T(8,128)S(1)} %collective-permute-done.13.low.refs_8_, f32[72,1024]{1,0:T(8,128)S(1)} %collective-permute-done.14.high.refs_9_, f32[1024,1024]{1,0:T(8,128)S(1)} %bitcast.14, ...), custom_call_target="tpu_custom_call" | custom-call | tf_op jit(solution)/shard_map/edge/pallas_call | solution.py:263
  43.3 4.4 %back.1.refs_6_ = f32[1088,1024]{1,0:T(8,128)S(1)} custom-call(bf16[4,560,128]{2,1,0:T(8,128)(2,1)S(1)} %get-tuple-element.22.refs_0_, bf16[1,560,128]{2,1,0:T(8,128)(2,1)S(1)} %collective-permute-done.7.refs_1_, bf16[1,560,128]{2,1,0:T(8,128)(2,1)S(1)} %collective-permute-done.8.refs_2_, bf16[1,560,128]{2,1,0:T(8,128)(2,1)S(1)} %collective-permute-done.10.refs_3_, ...), custom_call_target="tpu_custom_call" | custom-call | tf_op jit(solution)/shard_map/back/pallas_call | solution.py:457
  47.8 0.0 collective-permute-done.9.refs_1_
  47.8 5.0 %collective-permute-done.12.refs_2_ = bf16[2,560,128]{2,1,0:T(8,128)(2,1)S(1)} collective-permute-done((bf16[2,560,128]{2,1,0:T(8,128)(2,1)S(1)}, bf16[2,560,128]{2,1,0:T(8,128)(2,1)S(1)}, u32[]{:S(2)}, u32[]{:S(2)}) %collective-permute-start.12) | collective-permute-done | bytes 286752 | tf_op jit(solution)/shard_map/ppermute | solution.py:476
  52.8 6.8 %update.1 = f32[1024,1024]{1,0:T(8,128)} custom-call(bf16[4,560,128]{2,1,0:T(8,128)(2,1)S(1)} %collective-permute-done.6.refs_2_.refs_0_, bf16[2,560,128]{2,1,0:T(8,128)(2,1)S(1)} %collective-permute-done.9.refs_1_, bf16[2,560,128]{2,1,0:T(8,128)(2,1)S(1)} %collective-permute-done.12.refs_2_, ...), custom_call_target="tpu_custom_call" | custom-call | tf_op jit(solution)/shard_map/update/pallas_call | solution.py:457
  (4 shorter events, 0.1 us)
Async XLA Ops:
  0.0 16.5 %copy-start = (f32[32,32,1024]{2,1,0:T(8,128)S(1)}, f32[32,32,1024]{2,1,0:T(8,128)}, u32[]{:S(2)}) copy-start(f32[32,32,1024]{2,1,0:T(8,128)} %param.8) | copy-start | bytes 12582916
  0.0 4.6 %collective-permute-start = (bf16[2048,128]{1,0:T(8,128)(2,1)}, bf16[2048,128]{1,0:T(8,128)(2,1)S(1)}, u32[]{:S(2)}, u32[]{:S(2)}) collective-permute-start(bf16[2048,128]{1,0:T(8,128)(2,1)} %bitcast.16), channel_id=1, source_target_pairs={{0,2},{2,0},{4,6},{6,4},{8,10},{10,8},{12,14},{14,12},{16,18},{18,... | collective-permute-start | bytes 1572872 | tf_op jit(solution)/shard_map/ppermute | solution.py:481
  1.4 3.2 %collective-permute-start.1 = (s32[8,128]{1,0:T(8,128)S(1)}, s32[8,128]{1,0:T(8,128)S(1)}, u32[]{:S(2)}, u32[]{:S(2)}) collective-permute-start(s32[8,128]{1,0:T(8,128)S(1)} %pad_add_fusion.refs_2_), channel_id=1, source_target_pairs={{0,2},{2,0},{4,6},{6,4},{8,10},{10,8},{12,14},{14,12},{16,18},{18,... | collective-permute-start | bytes 12296 | tf_op jit(solution)/shard_map/ppermute | solution.py:481
  1.4 13.8 %collective-permute-start.5 = (s32[1,8]{1,0:T(1,128)}, s32[1,8]{1,0:T(1,128)S(1)}, u32[]{:S(2)}, u32[]{:S(2)}) collective-permute-start(s32[1,8]{1,0:T(1,128)} %param.15), channel_id=1, source_target_pairs={{0,1},{1,0},{2,3},{3,2},{4,5},{5,4},{6,7},{7,6},{8,9},{9,8},{10,11... | collective-permute-start | bytes 104 | tf_op jit(solution)/shard_map/ppermute | solution.py:476
  4.6 1.0 %copy-start.2 = (bf16[1,64,32,128]{3,2,1,0:T(8,128)(2,1)S(1)}, bf16[1,64,32,128]{3,2,1,0:T(8,128)(2,1)}, u32[]{:S(2)}) copy-start(bf16[1,64,32,128]{3,2,1,0:T(8,128)(2,1)} %param.11) | copy-start | bytes 1572868
  5.6 6.9 %copy-start.4 = (s32[1,8]{1,0:T(1,128)S(1)}, s32[1,8]{1,0:T(1,128)}, u32[]{:S(2)}) copy-start(s32[1,8]{1,0:T(1,128)} %param.15) | copy-start | bytes 100
  5.6 10.9 %copy-start.3 = (f32[32]{0:T(128)S(1)}, f32[32]{0:T(128)}, u32[]{:S(2)}) copy-start(f32[32]{0:T(128)} %refs_7_.1) | copy-start | bytes 388
  9.0 12.8 %collective-permute-start.2 = (bf16[1,560,128]{2,1,0:T(8,128)(2,1)S(1)}, bf16[1,560,128]{2,1,0:T(8,128)(2,1)S(1)}, u32[]{:S(2)}, u32[]{:S(2)}) collective-permute-start(bf16[1,560,128]{2,1,0:T(8,128)(2,1)S(1)} %get-tuple-element.41), channel_id=1, source_target_pairs={{0,4},{2,6},{4,0},{6,2},{8,12},{10,14},{12,8},{14,10},{16,20},{18,... | collective-permute-start | bytes 430088 | tf_op jit(solution)/shard_map/ppermute | solution.py:481
  10.5 12.0 %collective-permute-start.3 = (bf16[1,560,128]{2,1,0:T(8,128)(2,1)S(1)}, bf16[1,560,128]{2,1,0:T(8,128)(2,1)S(1)}, u32[]{:S(2)}, u32[]{:S(2)}) collective-permute-start(bf16[1,560,128]{2,1,0:T(8,128)(2,1)S(1)} %get-tuple-element.40), channel_id=1, source_target_pairs={{0,8},{2,10},{4,12},{6,14},{8,0},{10,2},{12,4},{14,6},{16,24},{18,... | collective-permute-start | bytes 430088 | tf_op jit(solution)/shard_map/ppermute | solution.py:481
  12.1 11.0 %collective-permute-start.4 = (bf16[1,560,128]{2,1,0:T(8,128)(2,1)S(1)}, bf16[1,560,128]{2,1,0:T(8,128)(2,1)S(1)}, u32[]{:S(2)}, u32[]{:S(2)}) collective-permute-start(bf16[1,560,128]{2,1,0:T(8,128)(2,1)S(1)} %get-tuple-element.39), channel_id=1, source_target_pairs={{0,12},{2,14},{4,8},{6,10},{8,4},{10,6},{12,0},{14,2},{16,28},{18,... | collective-permute-start | bytes 430088 | tf_op jit(solution)/shard_map/ppermute | solution.py:481
  12.6 21.8 %collective-permute-start.7 = (bf16[1,560,128]{2,1,0:T(8,128)(2,1)S(1)}, bf16[1,560,128]{2,1,0:T(8,128)(2,1)S(1)}, u32[]{:S(2)}, u32[]{:S(2)}) collective-permute-start(bf16[1,560,128]{2,1,0:T(8,128)(2,1)S(1)} %get-tuple-element.35), channel_id=1, source_target_pairs={{0,16},{2,18},{4,20},{6,22},{8,24},{10,26},{12,28},{14,30},{16,0},... | collective-permute-start | bytes 430088 | tf_op jit(solution)/shard_map/ppermute | solution.py:481
  15.2 20.5 %collective-permute-start.8 = (bf16[1,560,128]{2,1,0:T(8,128)(2,1)S(1)}, bf16[1,560,128]{2,1,0:T(8,128)(2,1)S(1)}, u32[]{:S(2)}, u32[]{:S(2)}) collective-permute-start(bf16[1,560,128]{2,1,0:T(8,128)(2,1)S(1)} %get-tuple-element.36), channel_id=1, source_target_pairs={{0,20},{2,22},{4,16},{6,18},{8,28},{10,30},{12,24},{14,26},{16,4},... | collective-permute-start | bytes 430088 | tf_op jit(solution)/shard_map/ppermute | solution.py:481
  23.2 16.1 %copy-start.1 = (f32[32,32,1024]{2,1,0:T(8,128)S(1)}, f32[32,32,1024]{2,1,0:T(8,128)}, u32[]{:S(2)}) copy-start(f32[32,32,1024]{2,1,0:T(8,128)} %param.9) | copy-start | bytes 12582916
  23.2 16.1 %collective-permute-start.6 = (bf16[4,560,128]{2,1,0:T(8,128)(2,1)S(1)}, bf16[4,560,128]{2,1,0:T(8,128)(2,1)S(1)}, u32[]{:S(2)}, u32[]{:S(2)}) collective-permute-start(bf16[4,560,128]{2,1,0:T(8,128)(2,1)S(1)} %get-tuple-element.22.refs_0_), channel_id=1, source_target_pairs={{0,1},{1,0},{2,3},{3,2},{4,5},{5,4},{6,7},{7,6},{8,9},{9,8},{10,11... | collective-permute-start | bytes 1720328 | tf_op jit(solution)/shard_map/ppermute | solution.py:476
  25.1 12.0 %collective-permute-start.10 = (bf16[1,560,128]{2,1,0:T(8,128)(2,1)S(1)}, bf16[1,560,128]{2,1,0:T(8,128)(2,1)S(1)}, u32[]{:S(2)}, u32[]{:S(2)}) collective-permute-start(bf16[1,560,128]{2,1,0:T(8,128)(2,1)S(1)} %get-tuple-element.23), channel_id=1, source_target_pairs={{0,24},{2,26},{4,28},{6,30},{8,16},{10,18},{12,20},{14,22},{16,8},... | collective-permute-start | bytes 430088 | tf_op jit(solution)/shard_map/ppermute | solution.py:481
  26.4 11.8 %collective-permute-start.11 = (bf16[1,560,128]{2,1,0:T(8,128)(2,1)S(1)}, bf16[1,560,128]{2,1,0:T(8,128)(2,1)S(1)}, u32[]{:S(2)}, u32[]{:S(2)}) collective-permute-start(bf16[1,560,128]{2,1,0:T(8,128)(2,1)S(1)} %get-tuple-element.24), channel_id=1, source_target_pairs={{0,28},{2,30},{4,24},{6,26},{8,20},{10,22},{12,16},{14,18},{16,12}... | collective-permute-start | bytes 430088 | tf_op jit(solution)/shard_map/ppermute | solution.py:481
  34.4 4.9 %collective-permute-start.13 = (f32[72,1024]{1,0:T(8,128)S(1)}, f32[72,1024]{1,0:T(8,128)S(1)}, u32[]{:S(2)}, u32[]{:S(2)}) collective-permute-start(f32[72,1024]{1,0:T(8,128)S(1)} %get-tuple-element.29), channel_id=1, source_target_pairs={{0,2},{2,4},{4,6},{6,8},{8,10},{10,12},{12,14},{14,16},{16,18},{18... | collective-permute-start | bytes 884744 | tf_op jit(solution)/shard_map/ppermute | solution.py:537
  35.7 3.5 %collective-permute-start.14 = (f32[72,1024]{1,0:T(8,128)S(1)}, f32[72,1024]{1,0:T(8,128)S(1)}, u32[]{:S(2)}, u32[]{:S(2)}) collective-permute-start(f32[72,1024]{1,0:T(8,128)S(1)} %get-tuple-element.30), channel_id=1, source_target_pairs={{2,0},{4,2},{6,4},{8,6},{10,8},{12,10},{14,12},{16,14},{18,16},{20... | collective-permute-start | bytes 884744 | tf_op jit(solution)/shard_map/ppermute | solution.py:538
  37.1 10.7 %collective-permute-start.9 = (bf16[2,560,128]{2,1,0:T(8,128)(2,1)S(1)}, bf16[2,560,128]{2,1,0:T(8,128)(2,1)S(1)}, u32[]{:S(2)}, u32[]{:S(2)}) collective-permute-start(bf16[2,560,128]{2,1,0:T(8,128)(2,1)S(1)} %pad_maximum_fusion), channel_id=1, source_target_pairs={{0,1},{1,0},{2,3},{3,2},{4,5},{5,4},{6,7},{7,6},{8,9},{9,8},{10,11... | collective-permute-start | bytes 860168 | tf_op jit(solution)/shard_map/ppermute | solution.py:476
  38.2 14.6 %collective-permute-start.12 = (bf16[2,560,128]{2,1,0:T(8,128)(2,1)S(1)}, bf16[2,560,128]{2,1,0:T(8,128)(2,1)S(1)}, u32[]{:S(2)}, u32[]{:S(2)}) collective-permute-start(bf16[2,560,128]{2,1,0:T(8,128)(2,1)S(1)} %pad_maximum_fusion.1), channel_id=1, source_target_pairs={{0,1},{1,0},{2,3},{3,2},{4,5},{5,4},{6,7},{7,6},{8,9},{9,8},{10,11... | collective-permute-start | bytes 860168 | tf_op jit(solution)/shard_map/ppermute | solution.py:476

commit v5 on v4

--- a/solution.py
+++ b/solution.py
@@ -510,14 +510,16 @@
     if slabs == 16 and view_count == 2:
         other = swap(subset_views)
         send = bucket(raws, tables, chips, True, planes, lines)
-        blurred, *mine = blur(psf_width, flat, [send, other], lines)
-        near = [send[0:1]] + [flip(send[j : j + 1], 2 * j) for j in range(1, 4)]
+        home = send[0:1]
+        home_over = swap(home)
+        blurred, *mine = blur(psf_width, flat, [send, other, home_over], lines)
+        near = [flip(send[j : j + 1], 2 * j) for j in range(1, 4)]
         far = [flip(send[j : j + 1], 2 * j) for j in (4, 5)]
         fronts = [forward(subset_views[0], blurred)]
         joined, passed = relay(near, [send[6:7], send[7:8]], [fronts[0][0]])
         far += [flip(passed[0], 12), flip(passed[1], 14)]
         over = [swap(joined)] + [swap(jnp.concatenate(part)) for part in (far[:2], far[2:])]
-        pieces = [[joined, *far], over]
+        pieces = [[home, joined, *far], [home_over, *over]]
         fronts.append(forward(other[0], blurred, [joined]))
         mine = behind(mine, fronts[1][0])
         behind_edge = [over[0]]

time: 60.5 us -> 61.7 us (1.020)
  waiting for transfers between devices: 6.43 us -> 7.49 us
    ppermute x9, waiting for transfers between devices: 1.39 us -> 2.4 us  [flip(): return lax.ppermute(value, 'slab', [(i, i ^ mask) for i in range(size)])]
    ppermute x9, starting transfers between devices: 13.4 us -> 14.3 us  [flip(): return lax.ppermute(value, 'slab', [(i, i ^ mask) for i in range(size)])]
    ppermute x4 -> x5, starting transfers between devices: 7.14 us -> 6.36 us  [swap(): return lax.ppermute(value, 'view', [(0, 1), (1, 0)])]
    ppermute x4 -> x5, waiting for transfers between devices: 5.04 us -> 5.09 us  [swap(): return lax.ppermute(value, 'view', [(0, 1), (1, 0)])]
  transfers between devices with their start and end apart: 15 -> 16, of which waited for: 3 -> 5; matrix products, arithmetic and copies ran while one was open for 2% -> 2% of each run, Pallas kernels for 35% -> 34%
where the time goes in v5:
time: 61.7 us; the launch traced here: 60.8 us
  Pallas kernels  27.7 us (45%)
  starting transfers between devices  23.3 us (38%)
  waiting for transfers between devices  7.49 us (12%)
  local copies, waits for them, and re-layouts  1.13 us (2%)
  other arithmetic  1.09 us (2%)
    ppermute x9, starting transfers between devices, flip(): return lax.ppermute(value, 'slab', [(i, i ^ mask) for i in range(size)])  14.3 us
    pallas_call x2, Pallas kernels, back(): pl.pallas_call(functools.partial(back_kernel, [piece.shape[0] for piece i...  11.3 us
    pallas_call x2, Pallas kernels, front(): pl.pallas_call(functools.partial(front_kernel, len(after)), out_shape=(ja...  7.65 us
    ppermute x5, starting transfers between devices, swap(): return lax.ppermute(value, 'view', [(0, 1), (1, 0)])  6.36 us
    ppermute x5, waiting for transfers between devices, swap(): return lax.ppermute(value, 'view', [(0, 1), (1, 0)])  5.09 us
    pallas_call x1, Pallas kernels, edge(): pl.pallas_call(functools.partial(edge_kernel, lines, groups, len(after)),...  4.02 us
    pallas_call x1, Pallas kernels, bucket(): pl.pallas_call(functools.partial(bucket_kernel, chips, relative, planes,...  3.26 us
    ppermute x9, waiting for transfers between devices, flip(): return lax.ppermute(value, 'slab', [(i, i ^ mask) for i in range(size)])  2.4 us
  transfers between devices with their start and end apart: 16, of which 5 were waited for; matrix products, arithmetic and copies ran while one was open for 2% of the time, Pallas kernels for 34%

profile of v5, /device:TPU:0, one launch (start us, length us, event | category | flops | bytes accessed | tf_op | source)
XLA Modules:
  0.0 60.8 jit_solution(7087065775510676069)
XLA Ops:
  0.0 0.0 copy-start
  0.0 0.5 collective-permute-start
  0.5 0.9 %pad_add_fusion.refs_2_ = s32[8,128]{1,0:T(8,128)S(1)} fusion(s32[1,64]{1,0:T(1,128)} %param.14, s32[1,64]{1,0:T(1,128)} %param.13, s32[1,64]{1,0:T(1,128)} %bitcast.18), kind=kLoop, calls=%fused_computation.2 | loop fusion | flops 2048 | bytes 4864 | tf_op jit(solution)/shard_map/add | solution.py:497
  1.4 0.1 collective-permute-start.1
  1.4 3.1 %collective-permute-start.6 = (s32[1,8]{1,0:T(1,128)}, s32[1,8]{1,0:T(1,128)S(1)}, u32[]{:S(2)}, u32[]{:S(2)}) collective-permute-start(s32[1,8]{1,0:T(1,128)} %param.15), channel_id=1, source_target_pairs={{0,1},{1,0},{2,3},{3,2},{4,5},{5,4},{6,7},{7,6},{8,9},{9,8},{10,11... | collective-permute-start | bytes 104 | tf_op jit(solution)/shard_map/ppermute | solution.py:476
  4.6 0.0 collective-permute-done.1.refs_3_
  4.6 0.0 collective-permute-done.refs_1_
  4.6 0.0 copy-start.2
  4.6 1.0 %copy-done.2 = bf16[1,64,32,128]{3,2,1,0:T(8,128)(2,1)S(1)} copy-done((bf16[1,64,32,128]{3,2,1,0:T(8,128)(2,1)S(1)}, bf16[1,64,32,128]{3,2,1,0:T(8,128)(2,1)}, u32[]{:S(2)}) %copy-start.2) | copy-done | bytes 524312
  5.6 0.0 copy-start.4
  5.6 0.0 copy-start.3
  5.6 3.3 %bucket.1.refs_0_ = bf16[8,560,128]{2,1,0:T(8,128)(2,1)S(1)} custom-call(bf16[2048,128]{1,0:T(8,128)(2,1)S(1)} %bitcast.17, bf16[2048,128]{1,0:T(8,128)(2,1)S(1)} %collective-permute-done.refs_1_, s32[8,128]{1,0:T(8,128)S(1)} %pad_add_fusion.refs_2_, s32[8,128]{1,0:T(8,128)S(1)} %collective-permute-done.1.refs_3_), custom_call_target="tpu_custom_call" | custom-call | tf_op jit(solution)/shard_map/bucket/pallas_call | solution.py:132
  8.9 0.1 fusion
  9.0 0.9 %collective-permute-start.2 = (bf16[1,560,128]{2,1,0:T(8,128)(2,1)S(1)}, bf16[1,560,128]{2,1,0:T(8,128)(2,1)S(1)}, u32[]{:S(2)}, u32[]{:S(2)}) collective-permute-start(bf16[1,560,128]{2,1,0:T(8,128)(2,1)S(1)} %get-tuple-element.42.refs_0_), channel_id=1, source_target_pairs={{0,1},{1,0},{2,3},{3,2},{4,5},{5,4},{6,7},{7,6},{8,9},{9,8},{10,11... | collective-permute-start | bytes 430088 | tf_op jit(solution)/shard_map/ppermute | solution.py:476
  9.9 1.5 %collective-permute-start.3 = (bf16[1,560,128]{2,1,0:T(8,128)(2,1)S(1)}, bf16[1,560,128]{2,1,0:T(8,128)(2,1)S(1)}, u32[]{:S(2)}, u32[]{:S(2)}) collective-permute-start(bf16[1,560,128]{2,1,0:T(8,128)(2,1)S(1)} %get-tuple-element.41), channel_id=1, source_target_pairs={{0,4},{2,6},{4,0},{6,2},{8,12},{10,14},{12,8},{14,10},{16,20},{18,... | collective-permute-start | bytes 430088 | tf_op jit(solution)/shard_map/ppermute | solution.py:481
  11.4 1.6 %collective-permute-start.4 = (bf16[1,560,128]{2,1,0:T(8,128)(2,1)S(1)}, bf16[1,560,128]{2,1,0:T(8,128)(2,1)S(1)}, u32[]{:S(2)}, u32[]{:S(2)}) collective-permute-start(bf16[1,560,128]{2,1,0:T(8,128)(2,1)S(1)} %get-tuple-element.40), channel_id=1, source_target_pairs={{0,8},{2,10},{4,12},{6,14},{8,0},{10,2},{12,4},{14,6},{16,24},{18,... | collective-permute-start | bytes 430088 | tf_op jit(solution)/shard_map/ppermute | solution.py:481
  12.9 0.4 collective-permute-start.5
  13.3 0.0 copy-done.4
  13.4 0.1 multiply_bitcast_fusion.3
  13.4 0.0 collective-permute-done.6.refs_1_
  13.4 2.7 %collective-permute-start.8 = (bf16[1,560,128]{2,1,0:T(8,128)(2,1)S(1)}, bf16[1,560,128]{2,1,0:T(8,128)(2,1)S(1)}, u32[]{:S(2)}, u32[]{:S(2)}) collective-permute-start(bf16[1,560,128]{2,1,0:T(8,128)(2,1)S(1)} %get-tuple-element.35), channel_id=1, source_target_pairs={{0,16},{2,18},{4,20},{6,22},{8,24},{10,26},{12,28},{14,30},{16,0},... | collective-permute-start | bytes 430088 | tf_op jit(solution)/shard_map/ppermute | solution.py:481
  16.1 0.0 collective-permute-done.2.refs_2_.refs_0_
  16.1 1.9 %collective-permute-start.9 = (bf16[1,560,128]{2,1,0:T(8,128)(2,1)S(1)}, bf16[1,560,128]{2,1,0:T(8,128)(2,1)S(1)}, u32[]{:S(2)}, u32[]{:S(2)}) collective-permute-start(bf16[1,560,128]{2,1,0:T(8,128)(2,1)S(1)} %get-tuple-element.36), channel_id=1, source_target_pairs={{0,20},{2,22},{4,16},{6,18},{8,28},{10,30},{12,24},{14,26},{16,4},... | collective-permute-start | bytes 430088 | tf_op jit(solution)/shard_map/ppermute | solution.py:481
  18.0 0.0 copy-done
  18.0 0.0 copy-done.3
  18.0 1.4 %blur.1 = (bf16[960,1024]{1,0:T(8,128)(2,1)S(1)}, f32[72,1024]{1,0:T(8,128)S(1)}, f32[72,1024]{1,0:T(8,128)S(1)}) custom-call(f32[32]{0:T(128)S(1)} %copy-done.3, f32[1024,1024]{1,0:T(8,128)S(1)} %bitcast.13, bf16[8,560,128]{2,1,0:T(8,128)(2,1)S(1)} %bucket.1.refs_0_, s32[1,8]{1,0:T(1,128)S(1)} %collective-permute-done.6.refs_1_, ...), custom_call_target="tpu_custom_call" | custom-call | tf_op jit(solution)/shard_map/blur/pallas_call | solution.py:212
  19.4 3.8 %front.2 = (bf16[1024,1024]{1,0:T(8,128)(2,1)S(1)}, f32[960,1024]{1,0:T(8,128)S(1)}) custom-call(f32[8]{0:T(128)S(1)} %get-tuple-element.46.spacing, f32[8]{0:T(128)S(1)} %get-tuple-element.45.offset, bf16[960,1024]{1,0:T(8,128)(2,1)S(1)} %get-tuple-element.20.blurred), custom_call_target="tpu_custom_call" | custom-call | tf_op jit(solution)/shard_map/front/pallas_call | solution.py:310
  23.3 0.0 collective-permute-done.3.refs_0_
  23.3 0.3 collective-permute-done.4.refs_1_
  23.5 0.9 %collective-permute-done.5.refs_2_ = bf16[1,560,128]{2,1,0:T(8,128)(2,1)S(1)} collective-permute-done((bf16[1,560,128]{2,1,0:T(8,128)(2,1)S(1)}, bf16[1,560,128]{2,1,0:T(8,128)(2,1)S(1)}, u32[]{:S(2)}, u32[]{:S(2)}) %collective-permute-start.5) | collective-permute-done | bytes 143392 | tf_op jit(solution)/shard_map/ppermute | solution.py:481
  24.5 0.0 copy-start.1
  24.5 1.8 %collective-permute-start.11 = (bf16[1,560,128]{2,1,0:T(8,128)(2,1)S(1)}, bf16[1,560,128]{2,1,0:T(8,128)(2,1)S(1)}, u32[]{:S(2)}, u32[]{:S(2)}) collective-permute-start(bf16[1,560,128]{2,1,0:T(8,128)(2,1)S(1)} %get-tuple-element.23), channel_id=1, source_target_pairs={{0,24},{2,26},{4,28},{6,30},{8,16},{10,18},{12,20},{14,22},{16,8},... | collective-permute-start | bytes 430088 | tf_op jit(solution)/shard_map/ppermute | solution.py:481
  26.3 3.9 %collective-permute-start.12 = (bf16[1,560,128]{2,1,0:T(8,128)(2,1)S(1)}, bf16[1,560,128]{2,1,0:T(8,128)(2,1)S(1)}, u32[]{:S(2)}, u32[]{:S(2)}) collective-permute-start(bf16[1,560,128]{2,1,0:T(8,128)(2,1)S(1)} %get-tuple-element.24), channel_id=1, source_target_pairs={{0,28},{2,30},{4,24},{6,26},{8,20},{10,22},{12,16},{14,18},{16,12}... | collective-permute-start | bytes 430088 | tf_op jit(solution)/shard_map/ppermute | solution.py:481
  30.2 0.1 multiply_bitcast_fusion.2
  30.3 0.2 collective-permute-start.7
  30.5 3.8 %front.3 = (bf16[1024,1024]{1,0:T(8,128)(2,1)S(1)}, f32[960,1024]{1,0:T(8,128)S(1)}) custom-call(f32[8]{0:T(128)S(1)} %get-tuple-element.44.spacing, f32[8]{0:T(128)S(1)} %get-tuple-element.43.offset, bf16[960,1024]{1,0:T(8,128)(2,1)S(1)} %get-tuple-element.20.blurred, bf16[3,560,128]{2,1,0:T(8,128)(2,1)S(1)} %get-tuple-element.22.refs_0_.refs_1_), custom_call_target="tpu_custom_call" | custom-call | tf_op jit(solution)/shard_map/front/pallas_call | solution.py:310
  34.3 0.0 collective-permute-done.8.refs_2_
  34.3 1.3 %collective-permute-start.14 = (f32[72,1024]{1,0:T(8,128)S(1)}, f32[72,1024]{1,0:T(8,128)S(1)}, u32[]{:S(2)}, u32[]{:S(2)}) collective-permute-start(f32[72,1024]{1,0:T(8,128)S(1)} %get-tuple-element.29), channel_id=1, source_target_pairs={{0,2},{2,4},{4,6},{6,8},{8,10},{10,12},{12,14},{14,16},{16,18},{18... | collective-permute-start | bytes 884744 | tf_op jit(solution)/shard_map/ppermute | solution.py:539
  35.7 1.2 %collective-permute-done.9.refs_3_ = bf16[1,560,128]{2,1,0:T(8,128)(2,1)S(1)} collective-permute-done((bf16[1,560,128]{2,1,0:T(8,128)(2,1)S(1)}, bf16[1,560,128]{2,1,0:T(8,128)(2,1)S(1)}, u32[]{:S(2)}, u32[]{:S(2)}) %collective-permute-start.9) | collective-permute-done | bytes 143392 | tf_op jit(solution)/shard_map/ppermute | solution.py:481
  36.8 1.3 %collective-permute-start.15 = (f32[72,1024]{1,0:T(8,128)S(1)}, f32[72,1024]{1,0:T(8,128)S(1)}, u32[]{:S(2)}, u32[]{:S(2)}) collective-permute-start(f32[72,1024]{1,0:T(8,128)S(1)} %get-tuple-element.30), channel_id=1, source_target_pairs={{2,0},{4,2},{6,4},{8,6},{10,8},{12,10},{14,12},{16,14},{18,16},{20... | collective-permute-start | bytes 884744 | tf_op jit(solution)/shard_map/ppermute | solution.py:540
  38.2 0.0 collective-permute-done.11.refs_4_
  38.2 1.8 %collective-permute-start.10 = (bf16[2,560,128]{2,1,0:T(8,128)(2,1)S(1)}, bf16[2,560,128]{2,1,0:T(8,128)(2,1)S(1)}, u32[]{:S(2)}, u32[]{:S(2)}) collective-permute-start(bf16[2,560,128]{2,1,0:T(8,128)(2,1)S(1)} %pad_maximum_fusion), channel_id=1, source_target_pairs={{0,1},{1,0},{2,3},{3,2},{4,5},{5,4},{6,7},{7,6},{8,9},{9,8},{10,11... | collective-permute-start | bytes 860168 | tf_op jit(solution)/shard_map/ppermute | solution.py:476
  40.0 0.0 collective-permute-done.12.refs_5_
  40.0 0.4 collective-permute-start.13
  40.4 0.0 collective-permute-done.14.low.refs_9_
  40.4 0.0 collective-permute-done.15.high.refs_10_
  40.4 0.1 collective-permute-done.7.refs_2_.refs_1_
  40.5 0.0 copy-done.1
  40.5 4.0 %edge.1 = (f32[128,1024]{1,0:T(8,128)S(1)}, f32[128,1024]{1,0:T(8,128)S(1)}, f32[1024,1024]{1,0:T(8,128)S(1)}) custom-call(f32[32]{0:T(128)S(1)} %copy-done.3, f32[72,1024]{1,0:T(8,128)S(1)} %collective-permute-done.14.low.refs_9_, f32[72,1024]{1,0:T(8,128)S(1)} %collective-permute-done.15.high.refs_10_, f32[1024,1024]{1,0:T(8,128)S(1)} %bitcast.14, ...), custom_call_target="tpu_custom_call" | custom-call | tf_op jit(solution)/shard_map/edge/pallas_call | solution.py:263
  44.5 4.4 %back.1.refs_7_ = f32[1088,1024]{1,0:T(8,128)S(1)} custom-call(bf16[1,560,128]{2,1,0:T(8,128)(2,1)S(1)} %get-tuple-element.42.refs_0_, bf16[3,560,128]{2,1,0:T(8,128)(2,1)S(1)} %get-tuple-element.22.refs_0_.refs_1_, bf16[1,560,128]{2,1,0:T(8,128)(2,1)S(1)} %collective-permute-done.8.refs_2_, bf16[1,560,128]{2,1,0:T(8,128)(2,1)S(1)} %collective-permute-done.9.refs_3_, ...), custom_call_target="tpu_custom_call" | custom-call | tf_op jit(solution)/shard_map/back/pallas_call | solution.py:457
  49.0 0.0 collective-permute-done.10.refs_2_
  49.0 5.0 %collective-permute-done.13.refs_3_ = bf16[2,560,128]{2,1,0:T(8,128)(2,1)S(1)} collective-permute-done((bf16[2,560,128]{2,1,0:T(8,128)(2,1)S(1)}, bf16[2,560,128]{2,1,0:T(8,128)(2,1)S(1)}, u32[]{:S(2)}, u32[]{:S(2)}) %collective-permute-start.13) | collective-permute-done | bytes 286752 | tf_op jit(solution)/shard_map/ppermute | solution.py:476
  53.9 6.9 %update.1 = f32[1024,1024]{1,0:T(8,128)} custom-call(bf16[1,560,128]{2,1,0:T(8,128)(2,1)S(1)} %collective-permute-done.2.refs_2_.refs_0_, bf16[3,560,128]{2,1,0:T(8,128)(2,1)S(1)} %collective-permute-done.7.refs_2_.refs_1_, bf16[2,560,128]{2,1,0:T(8,128)(2,1)S(1)} %collective-permute-done.10.refs_2_, ...), custom_call_target="tpu_custom_call" | custom-call | tf_op jit(solution)/shard_map/update/pallas_call | solution.py:457
  (4 shorter events, 0.1 us)
Async XLA Ops:
  0.0 18.0 %copy-start = (f32[32,32,1024]{2,1,0:T(8,128)S(1)}, f32[32,32,1024]{2,1,0:T(8,128)}, u32[]{:S(2)}) copy-start(f32[32,32,1024]{2,1,0:T(8,128)} %param.8) | copy-start | bytes 12582916
  0.0 4.6 %collective-permute-start = (bf16[2048,128]{1,0:T(8,128)(2,1)}, bf16[2048,128]{1,0:T(8,128)(2,1)S(1)}, u32[]{:S(2)}, u32[]{:S(2)}) collective-permute-start(bf16[2048,128]{1,0:T(8,128)(2,1)} %bitcast.16), channel_id=1, source_target_pairs={{0,2},{2,0},{4,6},{6,4},{8,10},{10,8},{12,14},{14,12},{16,18},{18,... | collective-permute-start | bytes 1572872 | tf_op jit(solution)/shard_map/ppermute | solution.py:481
  1.4 3.2 %collective-permute-start.1 = (s32[8,128]{1,0:T(8,128)S(1)}, s32[8,128]{1,0:T(8,128)S(1)}, u32[]{:S(2)}, u32[]{:S(2)}) collective-permute-start(s32[8,128]{1,0:T(8,128)S(1)} %pad_add_fusion.refs_2_), channel_id=1, source_target_pairs={{0,2},{2,0},{4,6},{6,4},{8,10},{10,8},{12,14},{14,12},{16,18},{18,... | collective-permute-start | bytes 12296 | tf_op jit(solution)/shard_map/ppermute | solution.py:481
  1.4 12.0 %collective-permute-start.6 = (s32[1,8]{1,0:T(1,128)}, s32[1,8]{1,0:T(1,128)S(1)}, u32[]{:S(2)}, u32[]{:S(2)}) collective-permute-start(s32[1,8]{1,0:T(1,128)} %param.15), channel_id=1, source_target_pairs={{0,1},{1,0},{2,3},{3,2},{4,5},{5,4},{6,7},{7,6},{8,9},{9,8},{10,11... | collective-permute-start | bytes 104 | tf_op jit(solution)/shard_map/ppermute | solution.py:476
  4.6 1.0 %copy-start.2 = (bf16[1,64,32,128]{3,2,1,0:T(8,128)(2,1)S(1)}, bf16[1,64,32,128]{3,2,1,0:T(8,128)(2,1)}, u32[]{:S(2)}) copy-start(bf16[1,64,32,128]{3,2,1,0:T(8,128)(2,1)} %param.11) | copy-start | bytes 1572868
  5.6 7.7 %copy-start.4 = (s32[1,8]{1,0:T(1,128)S(1)}, s32[1,8]{1,0:T(1,128)}, u32[]{:S(2)}) copy-start(s32[1,8]{1,0:T(1,128)} %param.15) | copy-start | bytes 100
  5.6 12.4 %copy-start.3 = (f32[32]{0:T(128)S(1)}, f32[32]{0:T(128)}, u32[]{:S(2)}) copy-start(f32[32]{0:T(128)} %refs_8_.1) | copy-start | bytes 388
  9.0 7.1 %collective-permute-start.2 = (bf16[1,560,128]{2,1,0:T(8,128)(2,1)S(1)}, bf16[1,560,128]{2,1,0:T(8,128)(2,1)S(1)}, u32[]{:S(2)}, u32[]{:S(2)}) collective-permute-start(bf16[1,560,128]{2,1,0:T(8,128)(2,1)S(1)} %get-tuple-element.42.refs_0_), channel_id=1, source_target_pairs={{0,1},{1,0},{2,3},{3,2},{4,5},{5,4},{6,7},{7,6},{8,9},{9,8},{10,11... | collective-permute-start | bytes 430088 | tf_op jit(solution)/shard_map/ppermute | solution.py:476
  9.9 13.4 %collective-permute-start.3 = (bf16[1,560,128]{2,1,0:T(8,128)(2,1)S(1)}, bf16[1,560,128]{2,1,0:T(8,128)(2,1)S(1)}, u32[]{:S(2)}, u32[]{:S(2)}) collective-permute-start(bf16[1,560,128]{2,1,0:T(8,128)(2,1)S(1)} %get-tuple-element.41), channel_id=1, source_target_pairs={{0,4},{2,6},{4,0},{6,2},{8,12},{10,14},{12,8},{14,10},{16,20},{18,... | collective-permute-start | bytes 430088 | tf_op jit(solution)/shard_map/ppermute | solution.py:481
  11.4 12.2 %collective-permute-start.4 = (bf16[1,560,128]{2,1,0:T(8,128)(2,1)S(1)}, bf16[1,560,128]{2,1,0:T(8,128)(2,1)S(1)}, u32[]{:S(2)}, u32[]{:S(2)}) collective-permute-start(bf16[1,560,128]{2,1,0:T(8,128)(2,1)S(1)} %get-tuple-element.40), channel_id=1, source_target_pairs={{0,8},{2,10},{4,12},{6,14},{8,0},{10,2},{12,4},{14,6},{16,24},{18,... | collective-permute-start | bytes 430088 | tf_op jit(solution)/shard_map/ppermute | solution.py:481
  12.9 11.5 %collective-permute-start.5 = (bf16[1,560,128]{2,1,0:T(8,128)(2,1)S(1)}, bf16[1,560,128]{2,1,0:T(8,128)(2,1)S(1)}, u32[]{:S(2)}, u32[]{:S(2)}) collective-permute-start(bf16[1,560,128]{2,1,0:T(8,128)(2,1)S(1)} %get-tuple-element.39), channel_id=1, source_target_pairs={{0,12},{2,14},{4,8},{6,10},{8,4},{10,6},{12,0},{14,2},{16,28},{18,... | collective-permute-start | bytes 430088 | tf_op jit(solution)/shard_map/ppermute | solution.py:481
  13.4 20.9 %collective-permute-start.8 = (bf16[1,560,128]{2,1,0:T(8,128)(2,1)S(1)}, bf16[1,560,128]{2,1,0:T(8,128)(2,1)S(1)}, u32[]{:S(2)}, u32[]{:S(2)}) collective-permute-start(bf16[1,560,128]{2,1,0:T(8,128)(2,1)S(1)} %get-tuple-element.35), channel_id=1, source_target_pairs={{0,16},{2,18},{4,20},{6,22},{8,24},{10,26},{12,28},{14,30},{16,0},... | collective-permute-start | bytes 430088 | tf_op jit(solution)/shard_map/ppermute | solution.py:481
  16.1 20.8 %collective-permute-start.9 = (bf16[1,560,128]{2,1,0:T(8,128)(2,1)S(1)}, bf16[1,560,128]{2,1,0:T(8,128)(2,1)S(1)}, u32[]{:S(2)}, u32[]{:S(2)}) collective-permute-start(bf16[1,560,128]{2,1,0:T(8,128)(2,1)S(1)} %get-tuple-element.36), channel_id=1, source_target_pairs={{0,20},{2,22},{4,16},{6,18},{8,28},{10,30},{12,24},{14,26},{16,4},... | collective-permute-start | bytes 430088 | tf_op jit(solution)/shard_map/ppermute | solution.py:481
  24.5 16.0 %copy-start.1 = (f32[32,32,1024]{2,1,0:T(8,128)S(1)}, f32[32,32,1024]{2,1,0:T(8,128)}, u32[]{:S(2)}) copy-start(f32[32,32,1024]{2,1,0:T(8,128)} %param.9) | copy-start | bytes 12582916
  24.5 13.7 %collective-permute-start.11 = (bf16[1,560,128]{2,1,0:T(8,128)(2,1)S(1)}, bf16[1,560,128]{2,1,0:T(8,128)(2,1)S(1)}, u32[]{:S(2)}, u32[]{:S(2)}) collective-permute-start(bf16[1,560,128]{2,1,0:T(8,128)(2,1)S(1)} %get-tuple-element.23), channel_id=1, source_target_pairs={{0,24},{2,26},{4,28},{6,30},{8,16},{10,18},{12,20},{14,22},{16,8},... | collective-permute-start | bytes 430088 | tf_op jit(solution)/shard_map/ppermute | solution.py:481
  26.3 13.6 %collective-permute-start.12 = (bf16[1,560,128]{2,1,0:T(8,128)(2,1)S(1)}, bf16[1,560,128]{2,1,0:T(8,128)(2,1)S(1)}, u32[]{:S(2)}, u32[]{:S(2)}) collective-permute-start(bf16[1,560,128]{2,1,0:T(8,128)(2,1)S(1)} %get-tuple-element.24), channel_id=1, source_target_pairs={{0,28},{2,30},{4,24},{6,26},{8,20},{10,22},{12,16},{14,18},{16,12}... | collective-permute-start | bytes 430088 | tf_op jit(solution)/shard_map/ppermute | solution.py:481
  30.3 10.2 %collective-permute-start.7 = (bf16[3,560,128]{2,1,0:T(8,128)(2,1)S(1)}, bf16[3,560,128]{2,1,0:T(8,128)(2,1)S(1)}, u32[]{:S(2)}, u32[]{:S(2)}) collective-permute-start(bf16[3,560,128]{2,1,0:T(8,128)(2,1)S(1)} %get-tuple-element.22.refs_0_.refs_1_), channel_id=1, source_target_pairs={{0,1},{1,0},{2,3},{3,2},{4,5},{5,4},{6,7},{7,6},{8,9},{9,8},{10,11... | collective-permute-start | bytes 1290248 | tf_op jit(solution)/shard_map/ppermute | solution.py:476
  34.3 6.0 %collective-permute-start.14 = (f32[72,1024]{1,0:T(8,128)S(1)}, f32[72,1024]{1,0:T(8,128)S(1)}, u32[]{:S(2)}, u32[]{:S(2)}) collective-permute-start(f32[72,1024]{1,0:T(8,128)S(1)} %get-tuple-element.29), channel_id=1, source_target_pairs={{0,2},{2,4},{4,6},{6,8},{8,10},{10,12},{12,14},{14,16},{16,18},{18... | collective-permute-start | bytes 884744 | tf_op jit(solution)/shard_map/ppermute | solution.py:539
  36.8 3.5 %collective-permute-start.15 = (f32[72,1024]{1,0:T(8,128)S(1)}, f32[72,1024]{1,0:T(8,128)S(1)}, u32[]{:S(2)}, u32[]{:S(2)}) collective-permute-start(f32[72,1024]{1,0:T(8,128)S(1)} %get-tuple-element.30), channel_id=1, source_target_pairs={{2,0},{4,2},{6,4},{8,6},{10,8},{12,10},{14,12},{16,14},{18,16},{20... | collective-permute-start | bytes 884744 | tf_op jit(solution)/shard_map/ppermute | solution.py:540
  38.2 10.8 %collective-permute-start.10 = (bf16[2,560,128]{2,1,0:T(8,128)(2,1)S(1)}, bf16[2,560,128]{2,1,0:T(8,128)(2,1)S(1)}, u32[]{:S(2)}, u32[]{:S(2)}) collective-permute-start(bf16[2,560,128]{2,1,0:T(8,128)(2,1)S(1)} %pad_maximum_fusion), channel_id=1, source_target_pairs={{0,1},{1,0},{2,3},{3,2},{4,5},{5,4},{6,7},{7,6},{8,9},{9,8},{10,11... | collective-permute-start | bytes 860168 | tf_op jit(solution)/shard_map/ppermute | solution.py:476
  40.0 13.9 %collective-permute-start.13 = (bf16[2,560,128]{2,1,0:T(8,128)(2,1)S(1)}, bf16[2,560,128]{2,1,0:T(8,128)(2,1)S(1)}, u32[]{:S(2)}, u32[]{:S(2)}) collective-permute-start(bf16[2,560,128]{2,1,0:T(8,128)(2,1)S(1)} %pad_maximum_fusion.1), channel_id=1, source_target_pairs={{0,1},{1,0},{2,3},{3,2},{4,5},{5,4},{6,7},{7,6},{8,9},{9,8},{10,11... | collective-permute-start | bytes 860168 | tf_op jit(solution)/shard_map/ppermute | solution.py:476
